TPU v7x, 512 devices: a whole 4x8x8 slice. The times are simulated.
512 devices in a mesh: dp: 32 (over y, x), tensor: 16 (over z, core).
Axes of the slice: x: 4, y: 8, z: 8, core: 2. Of those that a mesh axis runs over, the one named last changes fastest.
Arguments:
- hidden_in: bfloat16 [2048, 12288], P('dp'), may hold values from -6 to 6
- norm_gain: bfloat16 [12288], replicated, may hold values from 0.099609375 to 1.8984375
- norm_shift: bfloat16 [12288], replicated, may hold values from -3 to 3
- up_weight: bfloat16 [12288, 24576], P('dp', 'tensor'), may hold values from -0.0546875 to 0.0546875
- up_bias: bfloat16 [24576], P('tensor'), may hold values from -3 to 3
- down_weight: bfloat16 [24576, 12288], P('tensor', 'dp'), may hold values from -0.09375 to 0.09375
- down_bias: bfloat16 [12288], P('tensor'), may hold values from -3 to 3
- active: int32 [64, 16, 4], P(None, 'tensor'), may hold values from 0 to 11, as said below
- counts: int32 [64, 16], P(None, 'tensor'), may hold values from 1 to 4, as said below
Outputs:
- hidden_out: bfloat16 [2048, 12288], P('dp', 'tensor')
Inputs may be any that keep to these rules, and one draw needn't show every extreme that they name: The 4 entries of each list are distinct; only the first counts entries are active. `counts`: every row group has a list with all 4 slots valid.
All inputs are finite; a program needn't handle non-finite values.
Results may differ from a plain program's by a relative error of at most 0.022.
Values may be sent and summed in bfloat16 or wider, within the bound.
No kernel may reach another device: no remote copies, remote signals or barrier semaphores. Data moves between devices by JAX's collectives and lax.ppermute only.
A program may use at most 64 MiB of HBM per device.

v0:
```python
import math

import jax
import jax.numpy as jnp
from jax import lax
from jax.sharding import PartitionSpec as P

BLOCK = 128
GROUP = 32


def in_blocks(step_fn, arrays):
    total = arrays[0].shape[0]
    per = math.gcd(total, 8)
    stacked = tuple((item.reshape((total // per, per) + item.shape[1:]) for item in arrays))
    result = lax.map(step_fn, stacked)
    return result.reshape((total,) + result.shape[2:])


def select_up(rows, ids, up_table):
    ngroups, slots = ids.shape
    grouped = rows.reshape(ngroups, -1, rows.shape[1])

    def step(pair):
        block_rows, block_ids = pair
        chosen = jnp.take(up_table, block_ids, axis=1)
        return jnp.einsum("grd,dgcb->grcb", block_rows, chosen, preferred_element_type=jnp.float32)

    result = in_blocks(step, (grouped, ids))
    return result.reshape(rows.shape[0], slots * up_table.shape[2])


def select_down(act, ids, down_table):
    ngroups, slots = ids.shape
    grouped = act.reshape(ngroups, -1, slots, down_table.shape[1])

    def step(pair):
        block_act, block_ids = pair
        chosen = jnp.take(down_table, block_ids, axis=0)
        return jnp.einsum("grcb,gcbd->grd", block_act, chosen, preferred_element_type=jnp.float32)

    result = in_blocks(step, (grouped, ids))
    return result.reshape(act.shape[0], down_table.shape[2])


def activate(pre, ids, valid, bias_table):
    ngroups, slots = ids.shape
    own = bias_table.shape[0]
    onehot = (ids[:, :, None] == jnp.arange(own, dtype=jnp.int32)[None, None, :]).astype(
        jnp.float32
    )
    bias_sel = jnp.einsum("gco,ob->gcb", onehot, bias_table, precision=lax.Precision.HIGHEST)
    mask = (jnp.arange(slots, dtype=jnp.int32)[None, :] < valid[:, None]).astype(jnp.float32)
    shaped = pre.reshape(ngroups, -1, slots, bias_table.shape[1])
    result = jnp.maximum(shaped + bias_sel[:, None], 0.0) * mask[:, None, :, None]
    return result.astype(jnp.bfloat16).reshape(pre.shape)


def body(
    hidden_in, norm_gain, norm_shift, up_weight, up_bias, down_weight, down_bias, active, counts
):
    row_dev = hidden_in.shape[0]
    values = hidden_in.astype(jnp.float32)
    center = values - jnp.mean(values, axis=-1, keepdims=True)
    spread = jnp.mean(center * center, axis=-1, keepdims=True)
    normed = (
        center * lax.rsqrt(spread + 1e-05) * norm_gain.astype(jnp.float32)
        + norm_shift.astype(jnp.float32)
    ).astype(jnp.bfloat16)
    columns = lax.all_to_all(normed, "dp", split_axis=1, concat_axis=0, tiled=True)
    d_part = up_weight.shape[0]
    own = up_weight.shape[1] // BLOCK
    up_table = up_weight.reshape(d_part, own, BLOCK)
    down_table = down_weight.reshape(own, BLOCK, d_part)
    bias_table = up_bias.astype(jnp.float32).reshape(own, BLOCK)
    ids = active[:, 0, :]
    valid = counts[:, 0]
    pre_own = lax.psum_scatter(
        select_up(columns, ids, up_table).astype(jnp.bfloat16),
        "dp",
        scatter_dimension=0,
        tiled=True,
    ).astype(jnp.float32)
    per_dev = row_dev // GROUP
    first = lax.axis_index("dp") * per_dev
    own_ids = lax.dynamic_slice_in_dim(ids, first, per_dev, 0)
    own_valid = lax.dynamic_slice_in_dim(valid, first, per_dev, 0)
    act_own = activate(pre_own, own_ids, own_valid, bias_table)
    act = lax.all_gather(act_own, "dp", axis=0, tiled=True)
    branch = select_down(act, ids, down_table)
    branch = branch.astype(jnp.bfloat16)
    returned = lax.all_to_all(branch, "dp", split_axis=0, concat_axis=1, tiled=True)
    summed = lax.psum_scatter(
        returned.astype(jnp.float32).astype(jnp.bfloat16), "tensor", scatter_dimension=1, tiled=True
    ).astype(jnp.float32)
    width = summed.shape[1]
    resid = lax.dynamic_slice_in_dim(hidden_in, lax.axis_index("tensor") * width, width, 1).astype(
        jnp.float32
    )
    return (resid + summed + down_bias.astype(jnp.float32)).astype(jnp.bfloat16)


def solution(mesh):
    placed = (
        P("dp", None),
        P(),
        P(),
        P("dp", "tensor"),
        P("tensor"),
        P("tensor", "dp"),
        P("tensor"),
        P(None, "tensor", None),
        P(None, "tensor"),
    )
    return jax.shard_map(
        body, mesh=mesh, in_specs=placed, out_specs=P("dp", "tensor"), check_vma=False
    )
```

profile of v0, /device:TPU:6, one launch (start us, length us, event | category | flops | bytes accessed | tf_op | source)
XLA Modules:
  0.0 595.1 jit_solution(5143126974400507887)
XLA Ops:
  11.2 10.4 %all-to-all-start = ((bf16[64,32,384]{2,0,1:T(8,128)(2,1)}), bf16[64,32,384]{2,0,1:T(8,128)(2,1)}, u32[]{:S(2)}, u32[]{:S(2)}) async-start(bf16[64,32,384]{2,0,1:T(8,128)(2,1)} %bitcast.85), calls=%async_computation | async-start | bytes 3145728 | tf_op jit(solution)/shard_map/all_to_all | solution.py:70
  24.9 36.1 %all-to-all-done = bf16[64,32,384]{2,0,1:T(8,128)(2,1)} async-done(((bf16[64,32,384]{2,0,1:T(8,128)(2,1)}), bf16[64,32,384]{2,0,1:T(8,128)(2,1)}, u32[]{:S(2)}, u32[]{:S(2)}) %all-to-all-start) | async-done | bytes 1572896 | tf_op jit(solution)/shard_map/all_to_all | solution.py:70
  60.9 51.3 %while.20 = (s32[]{:T(128)}, bf16[8,8,32,4,128]{4,2,3,1,0:T(8,128)(2,1)}, bf16[8,8,32,384]{3,2,1,0:T(8,128)(2,1)}, s32[8,8,4]{1,2,0:T(4,128)S(1)}, bf16[384,12,128]{2,0,1:T(8,128)(2,1)S(1)}, /*index=5*/s32[]{:T(128)}) while((s32[]{:T(128)}, bf16[8,8,32,4,128]{4,2,3,1,0:T(8,128)(2,1)}, bf16[8,8,32,384]{3,2,1,0:T(8,128)(2,1)}, ...), condition=%wide.region_3.4_spmd, body=%wide.region_2.3_spmd.sunk | while | flops 102237472 | bytes 10164557 | solution.py:16
  63.8 3.5 fusion.45
  70.2 3.5 fusion.45
  76.6 3.6 fusion.45
  83.0 3.5 fusion.45
  89.4 3.5 fusion.45
  95.8 3.6 fusion.45
  102.3 3.5 fusion.45
  108.7 3.5 fusion.45
  117.6 219.8 %reduce-scatter.3.cloned.1.call-done = bf16[64,512]{1,0:T(8,128)(2,1)} async-done(((bf16[2048,512]{1,0:T(8,128)(2,1)}), bf16[64,512]{1,0:T(8,128)(2,1)}) %reduce-scatter.3.cloned.1.call-update) | async-done | bytes 65552 | tf_op jit(solution)/shard_map/reduce_scatter | solution.py:78
  339.1 83.5 %all-gather.2.cloned.1.call-done = bf16[2048,512]{1,0:T(8,128)(2,1)} async-done(((bf16[64,512]{1,0:T(8,128)(2,1)}), bf16[2048,512]{1,0:T(8,128)(2,1)}) %all-gather.2.cloned.1.call-update) | async-done | bytes 2097168 | tf_op jit(solution)/shard_map/all_gather | solution.py:89
  422.6 4.0 reshape_reshape.9
  426.6 57.6 %while.21 = (s32[]{:T(128)}, bf16[8,8,32,384]{3,2,1,0:T(8,128)(2,1)}, bf16[8,8,32,4,128]{4,3,2,1,0:T(4,128)(2,1)}, s32[8,8,4]{1,2,0:T(4,128)S(1)}, bf16[12,128,384]{2,1,0:T(8,128)(2,1)S(1)}, /*index=5*/s32[]{:T(128)}) while((s32[]{:T(128)}, bf16[8,8,32,384]{3,2,1,0:T(8,128)(2,1)}, bf16[8,8,32,4,128]{4,3,2,1,0:T(4,128)(2,1)}, ...), condition=%wide.region_6.7_spmd, body=%wide.region_5.6_spmd.sunk | while | flops 102237472 | bytes 10622801 | solution.py:16
  430.5 3.3 fusion.47
  437.7 3.3 fusion.47
  444.9 3.3 fusion.47
  452.1 3.3 fusion.47
  466.5 3.3 fusion.47
  473.7 3.2 fusion.47
  480.9 3.3 fusion.47
  484.2 42.5 %all_to_all.32 = bf16[32,64,384]{2,1,0:T(8,128)(2,1)S(1)} all-to-all(bf16[32,64,384]{2,1,0:T(8,128)(2,1)} %bitcast.117), channel_id=1, replica_groups=mesh['dp'=32,'tensor'=16] {'dp'}, dimensions={0} | all-to-all | bytes 3145728 | tf_op jit(solution)/shard_map/all_to_all | solution.py:92
  528.0 59.0 %reduce-scatter.5.cloned.1.call-done = bf16[64,768]{1,0:T(8,128)(2,1)} async-done(((bf16[64,12288]{1,0:T(8,128)(2,1)}), bf16[64,768]{1,0:T(8,128)(2,1)}) %reduce-scatter.5.cloned.1.call-update) | async-done | bytes 98320 | tf_op jit(solution)/shard_map/reduce_scatter | solution.py:93
  (172 shorter events, 75.5 us)
Async XLA Ops:
  6.5 110.9 %copy-start = (bf16[1536]{0:T(1024)(128)(2,1)S(1)}, bf16[1536]{0:T(1024)(128)(2,1)}, u32[]{:S(2)}) copy-start(bf16[1536]{0:T(1024)(128)(2,1)} %param.17) | copy-start | bytes 9220
  6.5 1.9 copy-start.2
  6.5 2.5 copy-start.4
  6.5 2.5 copy-start.5
  11.2 10.4 %copy-start.6 = (s32[64,1,4]{0,2,1:T(4,128)S(1)}, s32[64,1,4]{0,2,1:T(4,128)}, u32[]{:S(2)}) copy-start(s32[64,1,4]{0,2,1:T(4,128)} %param.20) | copy-start | bytes 3076
  11.2 10.5 %copy-start.3 = (bf16[384,1536]{1,0:T(8,128)(2,1)S(1)}, bf16[384,1536]{1,0:T(8,128)(2,1)}, u32[]{:S(2)}) copy-start(bf16[384,1536]{1,0:T(8,128)(2,1)} %param.16) | copy-start | bytes 3538948
  11.2 49.7 %all-to-all-start = ((bf16[64,32,384]{2,0,1:T(8,128)(2,1)}), bf16[64,32,384]{2,0,1:T(8,128)(2,1)}, u32[]{:S(2)}, u32[]{:S(2)}) async-start(bf16[64,32,384]{2,0,1:T(8,128)(2,1)} %bitcast.85), calls=%async_computation | async-start | bytes 3145728 | tf_op jit(solution)/shard_map/all_to_all | solution.py:70
  21.6 315.8 %reduce-scatter.3.cloned.1.call-start = ((), (), s32[]{:S(2)}) async-start(), calls=%async_computation.4 | async-start | bytes 2162688 | tf_op jit(solution)/shard_map/reduce_scatter | solution.py:78
  116.6 0.7 copy-start.8
  116.6 306.0 %all-gather.2.cloned.1.call-start = ((), (), s32[]{:S(2)}) async-start(), calls=%async_computation.5 | async-start | bytes 2162688 | tf_op jit(solution)/shard_map/all_gather | solution.py:89
  339.0 248.0 %reduce-scatter.5.cloned.1.call-start = ((), (), s32[]{:S(2)}) async-start(), calls=%async_computation.6 | async-start | bytes 1671168 | tf_op jit(solution)/shard_map/reduce_scatter | solution.py:93
  339.1 87.5 %copy-start.1 = (bf16[1536,384]{1,0:T(8,128)(2,1)S(1)}, bf16[1536,384]{1,0:T(8,128)(2,1)}, u32[]{:S(2)}) copy-start(bf16[1536,384]{1,0:T(8,128)(2,1)} %param.18) | copy-start | bytes 3538948
  526.7 1.4 copy-start.7
Sparse Core Ops, SparseCore 0:
  116.7 220.6 reduce-scatter.2
  341.0 81.5 all-gather.1
  528.1 58.8 reduce-scatter.4
where the time goes:
time: 596 us; the launch traced here: 595 us
  waiting for transfers between devices  398 us (67%)
  local copies, waits for them, and re-layouts  69.3 us (12%)
  matrix products  54.5 us (9%)
  blocking collectives  42.5 us (7%)
  between operations  13.3 us (2%)
  starting transfers between devices  10.5 us (2%)
  other arithmetic  6.56 us (1%)
    reduce_scatter x1, waiting for transfers between devices, body(): lax.psum_scatter(select_up(columns, ids, up_table).astype(jnp.bfloat16),...  220 us
    all_gather x1, waiting for transfers between devices, body(): act = lax.all_gather(act_own, 'dp', axis=0, tiled=True)  83.5 us
    reduce_scatter x1, waiting for transfers between devices, body(): lax.psum_scatter(returned.astype(jnp.float32).astype(jnp.bfloat16), 'tens...  59 us
    all_to_all x1, blocking collectives, body(): lax.all_to_all(branch, 'dp', split_axis=0, concat_axis=1, tiled=True)  42.5 us
    all_to_all x1, waiting for transfers between devices, body(): lax.all_to_all(normed, 'dp', split_axis=1, concat_axis=0, tiled=True)  36.1 us
    dot_general x8, matrix products, step(): jnp.einsum('grd,dgcb->grcb', block_rows, chosen, preferred_element_type=j...  28.3 us
    dot_general x8, matrix products, step(): jnp.einsum('grcb,gcbd->grd', block_act, chosen, preferred_element_type=jn...  26 us
    gather x8, local copies, waits for them, and re-layouts, step(): chosen = jnp.take(down_table, block_ids, axis=0)  20.9 us
  transfers between devices with their start and end apart: 4, of which 4 were waited for; matrix products, arithmetic and copies ran while one was open for 1% of the time, Pallas kernels for 0%

commit v1 on v0

v1 whole, which is shorter than its diff:
```python
import functools

import jax
import jax.numpy as jnp
from jax import lax
from jax.experimental import pallas as pl
from jax.experimental.pallas import tpu as pltpu
from jax.sharding import Mesh, PartitionSpec as P

BLOCK = 128
GROUP = 32
CAP = 4
NY, NX, NZ, NC = 8, 4, 8, 2
ROW = 64
PIECE = 384
F32 = jnp.float32
BF16 = jnp.bfloat16
ALL = ("y", "x", "z", "c")


def around(size, k):
    return [(i, (i + k) % size) for i in range(size)]


def up_kernel(where, ids, own, other, weight, out, rows, total):
    step = pl.program_id(0)
    c = where[1]
    half = own.shape[1]
    rows[pl.ds(pl.multiple_of(c * half, half), half), :] = own[0]
    rows[pl.ds(pl.multiple_of((1 - c) * half, half), half), :] = other[0]
    total[...] = jnp.dot(rows[...], weight[...], preferred_element_type=F32)
    groups = 2 * half // GROUP
    for g in range(groups):
        for s in range(CAP):
            block = ids[step * groups + g, s]
            picked = total[
                g * GROUP : (g + 1) * GROUP, pl.ds(pl.multiple_of(block * BLOCK, BLOCK), BLOCK)
            ]
            out[g // 2, 0, (g % 2) * GROUP : (g % 2 + 1) * GROUP, s * BLOCK : (s + 1) * BLOCK] = (
                picked.astype(BF16)
            )


def up(where, ids, own, other, weight):
    half = own.shape[1]
    return pl.pallas_call(
        up_kernel,
        out_shape=jax.ShapeDtypeStruct((NX, NY, ROW, CAP * BLOCK), BF16),
        grid_spec=pltpu.PrefetchScalarGridSpec(
            num_scalar_prefetch=2,
            grid=(NY,),
            in_specs=[
                pl.BlockSpec((1, half, PIECE), lambda i, *_: (i, 0, 0)),
                pl.BlockSpec((1, half, PIECE), lambda i, *_: (i, 0, 0)),
                pl.BlockSpec(weight.shape, lambda i, *_: (0, 0)),
            ],
            out_specs=pl.BlockSpec((NX, 1, ROW, CAP * BLOCK), lambda i, *_: (0, i, 0, 0)),
            scratch_shapes=[
                pltpu.VMEM((2 * half, PIECE), BF16),
                pltpu.VMEM((2 * half, weight.shape[1]), F32),
            ],
        ),
        compiler_params=pltpu.CompilerParams(vmem_limit_bytes=32 * 2**20),
        name="up",
    )(where, ids, own, other, weight)


def act_kernel(where, ids, valid, parts, bias, out):
    pre = jnp.sum(parts[...].astype(F32), axis=0)
    for g in range(ROW // GROUP):
        group = where[0] * (ROW // GROUP) + g
        for s in range(CAP):
            block = ids[group, s]
            keep = (s < valid[group]).astype(F32)
            mine = pre[g * GROUP : (g + 1) * GROUP, s * BLOCK : (s + 1) * BLOCK]
            value = jnp.maximum(mine + bias[pl.ds(block, 1), :], 0.0) * keep
            out[g * GROUP : (g + 1) * GROUP, s * BLOCK : (s + 1) * BLOCK] = value.astype(BF16)


def activate(where, ids, valid, parts, bias):
    smem = pl.BlockSpec(memory_space=pltpu.SMEM)
    vmem = pl.BlockSpec(memory_space=pltpu.VMEM)
    return pl.pallas_call(
        act_kernel,
        out_shape=jax.ShapeDtypeStruct((ROW, CAP * BLOCK), BF16),
        in_specs=[smem, smem, smem, vmem, vmem],
        out_specs=vmem,
        compiler_params=pltpu.CompilerParams(vmem_limit_bytes=32 * 2**20),
        name="act",
    )(where, ids, valid, parts, bias)


def down_kernel(where, ids, a0, a1, a2, a3, weight, keep, send, wide):
    step = pl.program_id(0)
    x, c = where[2], where[1]
    wide[...] = jnp.zeros_like(wide)
    for k, ref in enumerate((a0, a1, a2, a3)):
        source = lax.rem(x + NX - k, NX)
        for g in range(ROW // GROUP):
            group = (step * NX + source) * (ROW // GROUP) + g
            at = pl.multiple_of(source * ROW + g * GROUP, GROUP)
            for s in range(CAP):
                block = ids[group, s]
                wide[pl.ds(at, GROUP), pl.ds(pl.multiple_of(block * BLOCK, BLOCK), BLOCK)] = ref[
                    0, g * GROUP : (g + 1) * GROUP, s * BLOCK : (s + 1) * BLOCK
                ]
    half = keep.shape[1]
    for ref, part in ((keep, c), (send, 1 - c)):
        rows = wide[pl.ds(pl.multiple_of(part * half, half), half), :]
        ref[0] = jnp.dot(rows, weight[...], preferred_element_type=F32).astype(BF16)


def down(where, ids, acts, weight):
    half = NX * ROW // 2
    spec = pl.BlockSpec((1, ROW, CAP * BLOCK), lambda i, *_: (i, 0, 0))
    out_spec = pl.BlockSpec((1, half, PIECE), lambda i, *_: (i, 0, 0))
    return pl.pallas_call(
        down_kernel,
        out_shape=[jax.ShapeDtypeStruct((NY, half, PIECE), BF16)] * 2,
        grid_spec=pltpu.PrefetchScalarGridSpec(
            num_scalar_prefetch=2,
            grid=(NY,),
            in_specs=[spec] * 4 + [pl.BlockSpec(weight.shape, lambda i, *_: (0, 0))],
            out_specs=[out_spec, out_spec],
            scratch_shapes=[pltpu.VMEM((2 * half, weight.shape[0]), BF16)],
        ),
        compiler_params=pltpu.CompilerParams(vmem_limit_bytes=32 * 2**20),
        name="down",
    )(where, ids, *acts, weight)


def body(
    hidden_in, norm_gain, norm_shift, up_weight, up_bias, down_weight, down_bias, active, counts
):
    y, x = lax.axis_index("y"), lax.axis_index("x")
    z, c = lax.axis_index("z"), lax.axis_index("c")
    r, t = y * NX + x, z * NC + c
    odd = lax.rem(r, 2) == 1
    ids, valid = active[:, 0, :], counts[:, 0]
    where = jnp.stack([r, c, x]).astype(jnp.int32)
    width = down_bias.shape[0]

    values = hidden_in.astype(F32)
    mean = jnp.mean(values, axis=-1, keepdims=True)
    center = values - mean
    spread = jnp.mean(center * center, axis=-1, keepdims=True)
    mine = lax.dynamic_slice_in_dim(hidden_in, t * width, width, 1).astype(F32)
    gain = lax.dynamic_slice_in_dim(norm_gain, t * width, width, 0).astype(F32)
    shift = lax.dynamic_slice_in_dim(norm_shift, t * width, width, 0).astype(F32)
    normed = ((mine - mean) * lax.rsqrt(spread + 1e-05) * gain + shift).astype(BF16)

    there = [
        [
            (p * 16 + q, (2 * q + (j ^ (p & 1))) * 16 + p // 2)
            for p in range(32)
            for q in range(16)
        ]
        for j in range(2)
    ]
    back = [
        [
            (p * 16 + q, (2 * q + (j ^ (p & 1))) * 16 + p // 2)
            for p in range(32)
            for q in range(16)
        ]
        for j in range(2)
    ]
    low, high = normed[:, :PIECE], normed[:, PIECE:]
    first = lax.ppermute(jnp.where(odd, high, low), ALL, there[0])
    second = lax.ppermute(jnp.where(odd, low, high), ALL, there[1])
    rows = jnp.concatenate(
        [jnp.where(odd, second, first), jnp.where(odd, first, second)], axis=0
    )
    own = lax.all_gather(rows, "z", axis=0, tiled=False)
    other = lax.ppermute(own, "c", around(NC, 1))

    part = up(where, ids, own, other, up_weight)
    part = lax.all_to_all(part, "x", split_axis=0, concat_axis=0, tiled=True)
    part = jnp.sum(part.astype(F32), axis=0).astype(BF16)
    part = lax.all_to_all(part, "y", split_axis=0, concat_axis=0, tiled=True)
    bias = up_bias.astype(F32).reshape(-1, BLOCK)
    act = activate(where, ids, valid, part, bias)

    act = lax.all_gather(act, "y", axis=0, tiled=False)
    acts = [act] + [lax.ppermute(act, "x", around(NX, k)) for k in range(1, NX)]
    keep, send = down(where, ids, acts, down_weight)
    got = lax.ppermute(send, "c", around(NC, 1))
    pair = (keep.astype(F32) + got.astype(F32)).astype(BF16)
    pair = lax.all_to_all(pair, "z", split_axis=0, concat_axis=0, tiled=True)
    branch = jnp.sum(pair.astype(F32), axis=0).astype(BF16)

    low, high = branch[:ROW], branch[ROW:]
    first = lax.ppermute(jnp.where(odd, high, low), ALL, back[0])
    second = lax.ppermute(jnp.where(odd, low, high), ALL, back[1])
    summed = jnp.concatenate(
        [jnp.where(odd, second, first), jnp.where(odd, first, second)], axis=1
    ).astype(F32)
    resid = lax.dynamic_slice_in_dim(hidden_in, t * width, width, 1).astype(F32)
    return (resid + summed + down_bias.astype(F32)).astype(BF16)


def solution(mesh):
    fine = Mesh(mesh.devices.reshape(NY, NX, NZ, NC), ALL)
    dp, tensor = ("y", "x"), ("z", "c")
    placed = (
        P(dp, None),
        P(),
        P(),
        P(dp, tensor),
        P(tensor),
        P(tensor, dp),
        P(tensor),
        P(None, tensor, None),
        P(None, tensor),
    )
    return jax.shard_map(
        body, mesh=fine, in_specs=placed, out_specs=P(dp, tensor), check_vma=False
    )
```

time: 596 us -> 235 us (0.39)
  the two profiles are of different devices: /device:TPU:6 before, /device:TPU:33 now
where the time goes in v1:
time: 235 us; the launch traced here: 234 us
  blocking collectives  98.3 us (42%)
  starting transfers between devices  59.2 us (25%)
  waiting for transfers between devices  55.4 us (24%)
  Pallas kernels  14.4 us (6%)
  other arithmetic  6.67 us (3%)
    all_to_all x1, blocking collectives, body(): part = lax.all_to_all(part, 'x', split_axis=0, concat_axis=0, tiled=True)  29.5 us
    all_to_all x1, blocking collectives, body(): pair = lax.all_to_all(pair, 'z', split_axis=0, concat_axis=0, tiled=True)  26.8 us
    all_gather x1, blocking collectives, body(): own = lax.all_gather(rows, 'z', axis=0, tiled=False)  21.1 us
    all_gather x1, blocking collectives, body(): act = lax.all_gather(act, 'y', axis=0, tiled=False)  20.8 us
    ppermute x3, waiting for transfers between devices, body(): acts = [act] + [lax.ppermute(act, 'x', around(NX, k)) for k in range(1, NX)]  17.3 us
    ppermute x1, starting transfers between devices, body(): second = lax.ppermute(jnp.where(odd, low, high), ALL, there[1])  12.9 us
    ppermute x1, waiting for transfers between devices, body(): first = lax.ppermute(jnp.where(odd, high, low), ALL, there[0])  12.3 us
    all_to_all x1, waiting for transfers between devices, body(): part = lax.all_to_all(part, 'y', split_axis=0, concat_axis=0, tiled=True)  10.8 us
  transfers between devices with their start and end apart: 10, of which 10 were waited for; matrix products, arithmetic and copies ran while one was open for 0% of the time, Pallas kernels for 0%

profile of v1, /device:TPU:33, one launch (start us, length us, event | category | flops | bytes accessed | tf_op | source)
XLA Modules:
  0.0 234.2 jit_solution(15103661217317777702)
XLA Ops:
  0.0 1.8 convert_reduce_fusion
  3.4 12.9 %collective-permute-start = (bf16[64,384]{1,0:T(8,128)(2,1)S(1)}, bf16[64,384]{1,0:T(8,128)(2,1)S(1)}, u32[]{:S(2)}, u32[]{:S(2)}) collective-permute-start(bf16[64,384]{1,0:T(8,128)(2,1)S(1)} %get-tuple-element.15), channel_id=1, source_target_pairs={{0,16},{1,48},{2,80},{3,112},{4,144},{5,176},{6,208},{7,240},{8,27... | collective-permute-start | bytes 147464 | tf_op jit(solution)/shard_map/ppermute | solution.py:170
  16.4 3.8 %collective-permute-start.1 = (bf16[64,384]{1,0:T(8,128)(2,1)S(1)}, bf16[64,384]{1,0:T(8,128)(2,1)S(1)}, u32[]{:S(2)}, u32[]{:S(2)}) collective-permute-start(bf16[64,384]{1,0:T(8,128)(2,1)S(1)} %get-tuple-element.16), channel_id=1, source_target_pairs={{0,0},{1,32},{2,64},{3,96},{4,128},{5,160},{6,192},{7,224},{8,256}... | collective-permute-start | bytes 147464 | tf_op jit(solution)/shard_map/ppermute | solution.py:169
  20.7 12.3 %collective-permute-done.1 = bf16[64,384]{1,0:T(8,128)(2,1)S(1)} collective-permute-done((bf16[64,384]{1,0:T(8,128)(2,1)S(1)}, bf16[64,384]{1,0:T(8,128)(2,1)S(1)}, u32[]{:S(2)}, u32[]{:S(2)}) %collective-permute-start.1) | collective-permute-done | bytes 49184 | tf_op jit(solution)/shard_map/ppermute | solution.py:169
  33.1 21.1 %all-gather = bf16[1024,384]{1,0:T(8,128)(2,1)S(1)} all-gather(bf16[128,384]{1,0:T(8,128)(2,1)S(1)} %pad_maximum_fusion), channel_id=2, replica_groups=mesh['y'=8,'x'=4,'z'=8,'c'=2] {'z'}, dimensions={0}, use_global_device_ids=true | all-gather | bytes 884736 | tf_op jit(solution)/shard_map/all_gather | solution.py:174
  54.2 4.5 %collective-permute-start.2 = (bf16[8,128,384]{2,1,0:T(8,128)(2,1)S(1)}, bf16[8,128,384]{2,1,0:T(8,128)(2,1)S(1)}, u32[]{:S(2)}, u32[]{:S(2)}) collective-permute-start(bf16[8,128,384]{2,1,0:T(8,128)(2,1)S(1)} %bitcast.10), channel_id=1, source_target_pairs={{0,1},{1,0},{2,3},{3,2},{4,5},{5,4},{6,7},{7,6},{8,9},{9,8},{10,11... | collective-permute-start | bytes 2359304 | tf_op jit(solution)/shard_map/ppermute | solution.py:175
  60.5 6.4 %up.1 = bf16[4,8,64,512]{3,2,1,0:T(8,128)(2,1)S(1)} custom-call(s32[3]{0:T(128)S(1)} %pad_add_fusion.where, s32[64,4]{1,0:T(8,128)S(1)} %bitcast.16, bf16[8,128,384]{2,1,0:T(8,128)(2,1)S(1)} %bitcast.11, bf16[8,128,384]{2,1,0:T(8,128)(2,1)S(1)} %collective-permute-done.2.other, bf16[384,1536]{1,0:T(8,128)(2,1)S(1)} %copy-done), custom_call_target="tpu_custom_call" | custom-call | tf_op jit(solution)/shard_map/up/pallas_call | solution.py:46
  67.0 29.5 %all_to_all.15 = bf16[4,8,64,512]{3,2,1,0:T(8,128)(2,1)S(1)} all-to-all(bf16[4,8,64,512]{3,2,1,0:T(8,128)(2,1)S(1)} %up.1), channel_id=1, replica_groups=mesh['y'=8,'x'=4,'z'=8,'c'=2] {'x'}, dimensions={0} | all-to-all | bytes 4194304 | tf_op jit(solution)/shard_map/all_to_all | solution.py:178
  97.8 6.8 %all-to-all-start.1 = ((bf16[8,64,512]{2,1,0:T(8,128)(2,1)}), bf16[8,64,512]{2,1,0:T(8,128)(2,1)S(1)}, u32[]{:S(2)}, u32[]{:S(2)}) async-start(bf16[8,64,512]{2,1,0:T(8,128)(2,1)} %reduce_sum.44), calls=%async_computation.1 | async-start | bytes 1048576 | tf_op jit(solution)/shard_map/all_to_all | solution.py:180
  104.6 10.8 %all-to-all-done.1.parts = bf16[8,64,512]{2,1,0:T(8,128)(2,1)S(1)} async-done(((bf16[8,64,512]{2,1,0:T(8,128)(2,1)}), bf16[8,64,512]{2,1,0:T(8,128)(2,1)S(1)}, u32[]{:S(2)}, u32[]{:S(2)}) %all-to-all-start.1) | async-done | bytes 524320 | tf_op jit(solution)/shard_map/all_to_all | solution.py:180
  116.5 20.8 %all-gather.1 = bf16[512,512]{1,0:T(8,128)(2,1)S(1)} all-gather(bf16[64,512]{1,0:T(8,128)(2,1)S(1)} %act.1), channel_id=3, replica_groups=mesh['y'=8,'x'=4,'z'=8,'c'=2] {'y'}, dimensions={0}, use_global_device_ids=true | all-gather | bytes 589824 | tf_op jit(solution)/shard_map/all_gather | solution.py:184
  137.3 2.2 collective-permute-start.3
  139.5 3.7 %collective-permute-start.4 = (bf16[8,64,512]{2,1,0:T(8,128)(2,1)S(1)}, bf16[8,64,512]{2,1,0:T(8,128)(2,1)S(1)}, u32[]{:S(2)}, u32[]{:S(2)}) collective-permute-start(bf16[8,64,512]{2,1,0:T(8,128)(2,1)S(1)} %bitcast.13), channel_id=1, source_target_pairs={{0,32},{16,48},{32,0},{48,16},{1,33},{17,49},{33,1},{49,17},{2,34}... | collective-permute-start | bytes 1572872 | tf_op jit(solution)/shard_map/ppermute | solution.py:185
  143.2 2.5 %collective-permute-start.5 = (bf16[8,64,512]{2,1,0:T(8,128)(2,1)S(1)}, bf16[8,64,512]{2,1,0:T(8,128)(2,1)S(1)}, u32[]{:S(2)}, u32[]{:S(2)}) collective-permute-start(bf16[8,64,512]{2,1,0:T(8,128)(2,1)S(1)} %bitcast.14), channel_id=1, source_target_pairs={{0,48},{16,0},{32,16},{48,32},{1,49},{17,1},{33,17},{49,33},{2,50}... | collective-permute-start | bytes 1572872 | tf_op jit(solution)/shard_map/ppermute | solution.py:185
  145.8 6.7 %collective-permute-done.3.a1 = bf16[8,64,512]{2,1,0:T(8,128)(2,1)S(1)} collective-permute-done((bf16[8,64,512]{2,1,0:T(8,128)(2,1)S(1)}, bf16[8,64,512]{2,1,0:T(8,128)(2,1)S(1)}, u32[]{:S(2)}, u32[]{:S(2)}) %collective-permute-start.3) | collective-permute-done | bytes 524320 | tf_op jit(solution)/shard_map/ppermute | solution.py:185
  152.4 4.0 %collective-permute-done.4.a2 = bf16[8,64,512]{2,1,0:T(8,128)(2,1)S(1)} collective-permute-done((bf16[8,64,512]{2,1,0:T(8,128)(2,1)S(1)}, bf16[8,64,512]{2,1,0:T(8,128)(2,1)S(1)}, u32[]{:S(2)}, u32[]{:S(2)}) %collective-permute-start.4) | collective-permute-done | bytes 524320 | tf_op jit(solution)/shard_map/ppermute | solution.py:185
  156.4 6.6 %collective-permute-done.5.a3 = bf16[8,64,512]{2,1,0:T(8,128)(2,1)S(1)} collective-permute-done((bf16[8,64,512]{2,1,0:T(8,128)(2,1)S(1)}, bf16[8,64,512]{2,1,0:T(8,128)(2,1)S(1)}, u32[]{:S(2)}, u32[]{:S(2)}) %collective-permute-start.5) | collective-permute-done | bytes 524320 | tf_op jit(solution)/shard_map/ppermute | solution.py:185
  163.0 6.8 %down.1 = (bf16[8,128,384]{2,1,0:T(8,128)(2,1)S(1)}, bf16[8,128,384]{2,1,0:T(8,128)(2,1)S(1)}) custom-call(s32[3]{0:T(128)S(1)} %pad_add_fusion.where, s32[64,4]{1,0:T(8,128)S(1)} %bitcast.18, bf16[8,64,512]{2,1,0:T(8,128)(2,1)S(1)} %bitcast.15, bf16[8,64,512]{2,1,0:T(8,128)(2,1)S(1)} %collective-permute-done.3.a1, ...), custom_call_target="tpu_custom_call" | custom-call | tf_op jit(solution)/shard_map/down/pallas_call | solution.py:117
  169.8 7.4 %collective-permute-start.6 = (bf16[8,128,384]{2,1,0:T(8,128)(2,1)S(1)}, bf16[8,128,384]{2,1,0:T(8,128)(2,1)S(1)}, u32[]{:S(2)}, u32[]{:S(2)}) collective-permute-start(bf16[8,128,384]{2,1,0:T(8,128)(2,1)S(1)} %get-tuple-element.8), channel_id=1, source_target_pairs={{0,1},{1,0},{2,3},{3,2},{4,5},{5,4},{6,7},{7,6},{8,9},{9,8},{10,11... | collective-permute-start | bytes 2359304 | tf_op jit(solution)/shard_map/ppermute | solution.py:187
  177.3 1.9 collective-permute-done.6
  179.4 26.8 %all_to_all.16 = bf16[8,128,384]{2,1,0:T(8,128)(2,1)S(1)} all-to-all(bf16[8,128,384]{2,1,0:T(8,128)(2,1)S(1)} %add_convert_fusion), channel_id=1, replica_groups=mesh['y'=8,'x'=4,'z'=8,'c'=2] {'z'}, dimensions={0} | all-to-all | bytes 1572864 | tf_op jit(solution)/shard_map/all_to_all | solution.py:189
  206.3 9.8 %collective-permute-start.7 = (bf16[64,384]{1,0:T(8,128)(2,1)S(1)}, bf16[64,384]{1,0:T(8,128)(2,1)S(1)}, u32[]{:S(2)}, u32[]{:S(2)}) collective-permute-start(bf16[64,384]{1,0:T(8,128)(2,1)S(1)} %get-tuple-element.11), channel_id=1, source_target_pairs={{0,16},{1,48},{2,80},{3,112},{4,144},{5,176},{6,208},{7,240},{8,27... | collective-permute-start | bytes 147464 | tf_op jit(solution)/shard_map/ppermute | solution.py:194
  216.1 5.6 %collective-permute-start.8 = (bf16[64,384]{1,0:T(8,128)(2,1)S(1)}, bf16[64,384]{1,0:T(8,128)(2,1)S(1)}, u32[]{:S(2)}, u32[]{:S(2)}) collective-permute-start(bf16[64,384]{1,0:T(8,128)(2,1)S(1)} %get-tuple-element.12), channel_id=1, source_target_pairs={{0,0},{1,32},{2,64},{3,96},{4,128},{5,160},{6,192},{7,224},{8,256}... | collective-permute-start | bytes 147464 | tf_op jit(solution)/shard_map/ppermute | solution.py:193
  222.7 10.0 %collective-permute-done.8 = bf16[64,384]{1,0:T(8,128)(2,1)S(1)} collective-permute-done((bf16[64,384]{1,0:T(8,128)(2,1)S(1)}, bf16[64,384]{1,0:T(8,128)(2,1)S(1)}, u32[]{:S(2)}, u32[]{:S(2)}) %collective-permute-start.8) | collective-permute-done | bytes 49184 | tf_op jit(solution)/shard_map/ppermute | solution.py:193
  (36 shorter events, 9.3 us)
Async XLA Ops:
  0.0 1.9 copy-start.3
  1.9 56.8 %copy-start.5 = (s32[64,1,4]{0,2,1:T(4,128)S(1)}, s32[64,1,4]{0,2,1:T(4,128)}, u32[]{:S(2)}) copy-start(s32[64,1,4]{0,2,1:T(4,128)} %param.16) | copy-start | bytes 3076
  1.9 58.7 %copy-start = (bf16[384,1536]{1,0:T(8,128)(2,1)S(1)}, bf16[384,1536]{1,0:T(8,128)(2,1)}, u32[]{:S(2)}) copy-start(bf16[384,1536]{1,0:T(8,128)(2,1)} %weight.2) | copy-start | bytes 3538948
  3.4 17.3 %collective-permute-start = (bf16[64,384]{1,0:T(8,128)(2,1)S(1)}, bf16[64,384]{1,0:T(8,128)(2,1)S(1)}, u32[]{:S(2)}, u32[]{:S(2)}) collective-permute-start(bf16[64,384]{1,0:T(8,128)(2,1)S(1)} %get-tuple-element.15), channel_id=1, source_target_pairs={{0,16},{1,48},{2,80},{3,112},{4,144},{5,176},{6,208},{7,240},{8,27... | collective-permute-start | bytes 147464 | tf_op jit(solution)/shard_map/ppermute | solution.py:170
  16.4 16.6 %collective-permute-start.1 = (bf16[64,384]{1,0:T(8,128)(2,1)S(1)}, bf16[64,384]{1,0:T(8,128)(2,1)S(1)}, u32[]{:S(2)}, u32[]{:S(2)}) collective-permute-start(bf16[64,384]{1,0:T(8,128)(2,1)S(1)} %get-tuple-element.16), channel_id=1, source_target_pairs={{0,0},{1,32},{2,64},{3,96},{4,128},{5,160},{6,192},{7,224},{8,256}... | collective-permute-start | bytes 147464 | tf_op jit(solution)/shard_map/ppermute | solution.py:169
  54.2 6.4 %collective-permute-start.2 = (bf16[8,128,384]{2,1,0:T(8,128)(2,1)S(1)}, bf16[8,128,384]{2,1,0:T(8,128)(2,1)S(1)}, u32[]{:S(2)}, u32[]{:S(2)}) collective-permute-start(bf16[8,128,384]{2,1,0:T(8,128)(2,1)S(1)} %bitcast.10), channel_id=1, source_target_pairs={{0,1},{1,0},{2,3},{3,2},{4,5},{5,4},{6,7},{7,6},{8,9},{9,8},{10,11... | collective-permute-start | bytes 2359304 | tf_op jit(solution)/shard_map/ppermute | solution.py:175
  96.5 8.1 %copy-start.4 = (bf16[1536]{0:T(1024)(128)(2,1)S(1)}, bf16[1536]{0:T(1024)(128)(2,1)}, u32[]{:S(2)}) copy-start(bf16[1536]{0:T(1024)(128)(2,1)} %param.13) | copy-start | bytes 9220
  96.5 18.9 %copy-start.2 = (s32[64,1]{0,1:T(1,128)S(1)}, s32[64,1]{0,1:T(1,128)}, u32[]{:S(2)}) copy-start(s32[64,1]{0,1:T(1,128)} %param.17) | copy-start | bytes 772
  97.8 65.3 %copy-start.1 = (bf16[1536,384]{1,0:T(8,128)(2,1)S(1)}, bf16[1536,384]{1,0:T(8,128)(2,1)}, u32[]{:S(2)}) copy-start(bf16[1536,384]{1,0:T(8,128)(2,1)} %weight.3) | copy-start | bytes 3538948
  97.8 17.6 %all-to-all-start.1 = ((bf16[8,64,512]{2,1,0:T(8,128)(2,1)}), bf16[8,64,512]{2,1,0:T(8,128)(2,1)S(1)}, u32[]{:S(2)}, u32[]{:S(2)}) async-start(bf16[8,64,512]{2,1,0:T(8,128)(2,1)} %reduce_sum.44), calls=%async_computation.1 | async-start | bytes 1048576 | tf_op jit(solution)/shard_map/all_to_all | solution.py:180
  137.3 15.1 %collective-permute-start.3 = (bf16[8,64,512]{2,1,0:T(8,128)(2,1)S(1)}, bf16[8,64,512]{2,1,0:T(8,128)(2,1)S(1)}, u32[]{:S(2)}, u32[]{:S(2)}) collective-permute-start(bf16[8,64,512]{2,1,0:T(8,128)(2,1)S(1)} %bitcast.12), channel_id=1, source_target_pairs={{0,16},{16,32},{32,48},{48,0},{1,17},{17,33},{33,49},{49,1},{2,18}... | collective-permute-start | bytes 1572872 | tf_op jit(solution)/shard_map/ppermute | solution.py:185
  139.5 16.9 %collective-permute-start.4 = (bf16[8,64,512]{2,1,0:T(8,128)(2,1)S(1)}, bf16[8,64,512]{2,1,0:T(8,128)(2,1)S(1)}, u32[]{:S(2)}, u32[]{:S(2)}) collective-permute-start(bf16[8,64,512]{2,1,0:T(8,128)(2,1)S(1)} %bitcast.13), channel_id=1, source_target_pairs={{0,32},{16,48},{32,0},{48,16},{1,33},{17,49},{33,1},{49,17},{2,34}... | collective-permute-start | bytes 1572872 | tf_op jit(solution)/shard_map/ppermute | solution.py:185
  143.2 19.8 %collective-permute-start.5 = (bf16[8,64,512]{2,1,0:T(8,128)(2,1)S(1)}, bf16[8,64,512]{2,1,0:T(8,128)(2,1)S(1)}, u32[]{:S(2)}, u32[]{:S(2)}) collective-permute-start(bf16[8,64,512]{2,1,0:T(8,128)(2,1)S(1)} %bitcast.14), channel_id=1, source_target_pairs={{0,48},{16,0},{32,16},{48,32},{1,49},{17,1},{33,17},{49,33},{2,50}... | collective-permute-start | bytes 1572872 | tf_op jit(solution)/shard_map/ppermute | solution.py:185
  169.8 9.3 %collective-permute-start.6 = (bf16[8,128,384]{2,1,0:T(8,128)(2,1)S(1)}, bf16[8,128,384]{2,1,0:T(8,128)(2,1)S(1)}, u32[]{:S(2)}, u32[]{:S(2)}) collective-permute-start(bf16[8,128,384]{2,1,0:T(8,128)(2,1)S(1)} %get-tuple-element.8), channel_id=1, source_target_pairs={{0,1},{1,0},{2,3},{3,2},{4,5},{5,4},{6,7},{7,6},{8,9},{9,8},{10,11... | collective-permute-start | bytes 2359304 | tf_op jit(solution)/shard_map/ppermute | solution.py:187
  179.4 42.4 %copy-start.6 = (bf16[768]{0:T(1024)(128)(2,1)S(1)}, bf16[768]{0:T(1024)(128)(2,1)}, u32[]{:S(2)}) copy-start(bf16[768]{0:T(1024)(128)(2,1)} %param.15) | copy-start | bytes 4612
  206.3 16.3 %collective-permute-start.7 = (bf16[64,384]{1,0:T(8,128)(2,1)S(1)}, bf16[64,384]{1,0:T(8,128)(2,1)S(1)}, u32[]{:S(2)}, u32[]{:S(2)}) collective-permute-start(bf16[64,384]{1,0:T(8,128)(2,1)S(1)} %get-tuple-element.11), channel_id=1, source_target_pairs={{0,16},{1,48},{2,80},{3,112},{4,144},{5,176},{6,208},{7,240},{8,27... | collective-permute-start | bytes 147464 | tf_op jit(solution)/shard_map/ppermute | solution.py:194
  216.1 16.5 %collective-permute-start.8 = (bf16[64,384]{1,0:T(8,128)(2,1)S(1)}, bf16[64,384]{1,0:T(8,128)(2,1)S(1)}, u32[]{:S(2)}, u32[]{:S(2)}) collective-permute-start(bf16[64,384]{1,0:T(8,128)(2,1)S(1)} %get-tuple-element.12), channel_id=1, source_target_pairs={{0,0},{1,32},{2,64},{3,96},{4,128},{5,160},{6,192},{7,224},{8,256}... | collective-permute-start | bytes 147464 | tf_op jit(solution)/shard_map/ppermute | solution.py:193

commit v2 on v1

v2 whole, which is shorter than its diff:
```python
import jax
import jax.numpy as jnp
from jax import lax
from jax.experimental import pallas as pl
from jax.experimental.pallas import tpu as pltpu
from jax.sharding import Mesh, PartitionSpec as P

BLOCK = 128
GROUP = 32
CAP = 4
NY, NX, NZ, NC = 8, 4, 8, 2
ROW = 64
PIECE = 384
F32 = jnp.float32
BF16 = jnp.bfloat16
ALL = ("y", "x", "z", "c")


def around(size, k):
    return [(i, (i + k) % size) for i in range(size)]


def norm_kernel(half, hidden, gain, shift, out):
    rows, features = hidden.shape
    pieces = features // PIECE

    def piece(p):
        return hidden[:, p * PIECE : (p + 1) * PIECE].astype(F32)

    total = jnp.zeros((rows, PIECE), F32)
    for p in range(pieces):
        total += piece(p)
    mean = jnp.sum(total, axis=1, keepdims=True) / features
    total = jnp.zeros((rows, PIECE), F32)
    for p in range(pieces):
        center = piece(p) - mean
        total += center * center
    spread = jnp.sum(total, axis=1, keepdims=True) / features
    scale = lax.rsqrt(spread + 1e-05)
    for p in range(pieces):
        value = (piece(p) - mean) * scale * gain[p : p + 1, :] + shift[p : p + 1, :]
        out[p] = value.astype(BF16)


def norm(half, hidden, gain, shift):
    features = hidden.shape[1]
    pieces = features // PIECE
    return pl.pallas_call(
        norm_kernel,
        out_shape=jax.ShapeDtypeStruct((pieces, GROUP, PIECE), BF16),
        grid_spec=pltpu.PrefetchScalarGridSpec(
            num_scalar_prefetch=1,
            grid=(1,),
            in_specs=[
                pl.BlockSpec((GROUP, features), lambda i, half: (half[0], 0)),
                pl.BlockSpec((pieces, PIECE), lambda i, half: (0, 0)),
                pl.BlockSpec((pieces, PIECE), lambda i, half: (0, 0)),
            ],
            out_specs=pl.BlockSpec((pieces, GROUP, PIECE), lambda i, half: (0, 0, 0)),
        ),
        compiler_params=pltpu.CompilerParams(vmem_limit_bytes=32 * 2**20),
        name="norm",
    )(half, hidden, gain, shift)


SMEM = pl.BlockSpec(memory_space=pltpu.SMEM)
VMEM = pl.BlockSpec(memory_space=pltpu.VMEM)
TOGETHER = 8


def up_kernel(half, ids, rows, weight, *rest):
    out, total = rest[-2:]
    h = half[0]
    for first in range(0, NY * NX, TOGETHER):
        block_rows = rows[first : first + TOGETHER].reshape(TOGETHER * GROUP, PIECE)
        total[...] = jnp.dot(block_rows, weight[...], preferred_element_type=F32)
        for i in range(TOGETHER):
            r = first + i
            for s in range(CAP):
                at = pl.multiple_of(ids[2 * r + h, s] * BLOCK, BLOCK)
                picked = total[i * GROUP : (i + 1) * GROUP, pl.ds(at, BLOCK)]
                out[r % NX, r // NX, h, :, s * BLOCK : (s + 1) * BLOCK] = picked.astype(BF16)


def up(half, ids, rows, weight, before=None):
    shape = (NX, NY, ROW // GROUP, GROUP, CAP * BLOCK)
    more = () if before is None else (before,)
    return pl.pallas_call(
        up_kernel,
        out_shape=jax.ShapeDtypeStruct(shape, BF16),
        in_specs=[SMEM, SMEM, VMEM, VMEM] + [VMEM] * len(more),
        out_specs=VMEM,
        scratch_shapes=[pltpu.VMEM((TOGETHER * GROUP, weight.shape[1]), F32)],
        input_output_aliases={4: 0} if more else {},
        compiler_params=pltpu.CompilerParams(vmem_limit_bytes=24 * 2**20),
        name="up_second" if more else "up_first",
    )(half, ids, rows, weight, *more)


def act_kernel(where, ids, valid, parts, bias, out):
    pre = jnp.sum(parts[...].astype(F32), axis=0)
    for g in range(ROW // GROUP):
        group = where[0] * (ROW // GROUP) + g
        for s in range(CAP):
            block = ids[group, s]
            keep = (s < valid[group]).astype(F32)
            mine = pre[g * GROUP : (g + 1) * GROUP, s * BLOCK : (s + 1) * BLOCK]
            value = (jnp.maximum(mine + bias[pl.ds(block, 1), :], 0.0) * keep).astype(BF16)
            for copy in range(out.shape[0]):
                out[copy, g * GROUP : (g + 1) * GROUP, s * BLOCK : (s + 1) * BLOCK] = value


def activate(where, ids, valid, parts, bias):
    return pl.pallas_call(
        act_kernel,
        out_shape=jax.ShapeDtypeStruct((NY, ROW, CAP * BLOCK), BF16),
        in_specs=[SMEM, SMEM, SMEM, VMEM, VMEM],
        out_specs=VMEM,
        compiler_params=pltpu.CompilerParams(vmem_limit_bytes=24 * 2**20),
        name="act",
    )(where, ids, valid, parts, bias)


def down_kernel(where, ids, a0, a1, a2, a3, weight, keep, send, wide):
    x, c = where[2], where[1]
    for k, ref in enumerate((a0, a1, a2, a3)):
        source = lax.rem(x + NX - k, NX)
        wide[...] = jnp.zeros_like(wide)
        for y in range(NY):
            for g in range(ROW // GROUP):
                group = (y * NX + source) * (ROW // GROUP) + g
                low = y * ROW + g * GROUP
                for s in range(CAP):
                    at = pl.multiple_of(ids[group, s] * BLOCK, BLOCK)
                    wide[low : low + GROUP, pl.ds(at, BLOCK)] = ref[
                        y, g * GROUP : (g + 1) * GROUP, s * BLOCK : (s + 1) * BLOCK
                    ]
        value = jnp.dot(wide[...], weight[...], preferred_element_type=F32).astype(BF16)
        value = value.reshape(NY, ROW, PIECE)
        own, part = source // 2 == c, lax.rem(source, 2)

        @pl.when(own)
        def _():
            keep[:, part] = value

        @pl.when(jnp.logical_not(own))
        def _():
            send[:, part] = value


def down(where, ids, acts, weight):
    return pl.pallas_call(
        down_kernel,
        out_shape=[jax.ShapeDtypeStruct((NY, 2, ROW, PIECE), BF16)] * 2,
        in_specs=[SMEM, SMEM] + [VMEM] * 5,
        out_specs=[VMEM, VMEM],
        scratch_shapes=[pltpu.VMEM((NY * ROW, weight.shape[0]), BF16)],
        compiler_params=pltpu.CompilerParams(vmem_limit_bytes=24 * 2**20),
        name="down",
    )(where, ids, *acts, weight)


def body(
    hidden_in, norm_gain, norm_shift, up_weight, up_bias, down_weight, down_bias, active, counts
):
    y, x = lax.axis_index("y"), lax.axis_index("x")
    z, c = lax.axis_index("z"), lax.axis_index("c")
    r, t = y * NX + x, z * NC + c
    odd = lax.rem(r, 2) == 1
    ids, valid = active[:, 0, :], counts[:, 0]
    where = jnp.stack([r, c, x]).astype(jnp.int32)
    width = down_bias.shape[0]

    mine, others = c.reshape(1), (1 - c).reshape(1)
    gain = norm_gain.astype(F32).reshape(-1, PIECE)
    shift = norm_shift.astype(F32).reshape(-1, PIECE)
    normed = norm(mine, hidden_in, gain, shift)
    own = lax.all_to_all(normed, ("y", "x"), split_axis=0, concat_axis=0, tiled=True)
    other = lax.ppermute(own, "c", around(NC, 1))
    part = up(mine, ids, own, up_weight)
    part = up(others, ids, other, up_weight, part).reshape(NX, NY, ROW, CAP * BLOCK)
    part = lax.all_to_all(part, "x", split_axis=0, concat_axis=0, tiled=True)
    part = jnp.sum(part.astype(F32), axis=0).astype(BF16)
    part = lax.all_to_all(part, "y", split_axis=0, concat_axis=0, tiled=True)
    bias = up_bias.astype(F32).reshape(-1, BLOCK)
    act = activate(where, ids, valid, part, bias)

    act = lax.all_to_all(act, "y", split_axis=0, concat_axis=0, tiled=True)
    acts = [act] + [lax.ppermute(act, "x", around(NX, k)) for k in range(1, NX)]
    keep, send = down(where, ids, acts, down_weight)
    got = lax.ppermute(send, "c", around(NC, 1))
    pair = (keep.astype(F32) + got.astype(F32)).astype(BF16).reshape(NZ, 2 * ROW, PIECE)
    pair = lax.all_to_all(pair, "z", split_axis=0, concat_axis=0, tiled=True)
    branch = jnp.sum(pair.astype(F32), axis=0).astype(BF16)

    back = [
        [
            (p * 16 + q, (2 * q + (j ^ (p & 1))) * 16 + p // 2)
            for p in range(32)
            for q in range(16)
        ]
        for j in range(2)
    ]
    low, high = branch[:ROW], branch[ROW:]
    first = lax.ppermute(jnp.where(odd, high, low), ALL, back[0])
    second = lax.ppermute(jnp.where(odd, low, high), ALL, back[1])
    summed = jnp.concatenate(
        [jnp.where(odd, second, first), jnp.where(odd, first, second)], axis=1
    ).astype(F32)
    resid = lax.dynamic_slice_in_dim(hidden_in, t * width, width, 1).astype(F32)
    return (resid + summed + down_bias.astype(F32)).astype(BF16)


def solution(mesh):
    fine = Mesh(mesh.devices.reshape(NY, NX, NZ, NC), ALL)
    dp, tensor = ("y", "x"), ("z", "c")
    placed = (
        P(dp, None),
        P(),
        P(),
        P(dp, tensor),
        P(tensor),
        P(tensor, dp),
        P(tensor),
        P(None, tensor, None),
        P(None, tensor),
    )
    return jax.shard_map(
        body, mesh=fine, in_specs=placed, out_specs=P(dp, tensor), check_vma=False
    )
```

time: 235 us -> 218 us (0.928)
  blocking collectives: 98.3 us -> 77 us
  waiting for transfers between devices: 55.4 us -> 68.2 us
  starting transfers between devices: 59.2 us -> 50.4 us
  local copies, waits for them, and re-layouts: 0.16 us -> 3.03 us
  other arithmetic: 6.67 us -> 4.2 us
    all_gather x2 -> x0, blocking collectives: 41.9 us -> none  [the longest x1 21.1 us: body(): own = lax.all_gather(rows, 'z', axis=0, tiled=False)]
    all_to_all x0 -> x1, waiting for transfers between devices: none -> 23.6 us  [body(): pair = lax.all_to_all(pair, 'z', split_axis=0, concat_axis=0, tiled=True)]
    all_to_all x1 -> x2, blocking collectives: 26.8 us -> 48.4 us  [the longest x1 26.9 us: body(): lax.all_to_all(normed, ('y', 'x'), split_axis=0, concat_axis=0, tiled=True)]
    ppermute x2 -> x0, starting transfers between devices: 16.7 us -> none  [the longest x1 12.9 us: body(): second = lax.ppermute(jnp.where(odd, low, high), ALL, there[1])]
    ppermute x2 -> x0, waiting for transfers between devices: 12.9 us -> none  [the longest x1 12.3 us: body(): first = lax.ppermute(jnp.where(odd, high, low), ALL, there[0])]
    all_to_all x0 -> x1, starting transfers between devices: none -> 10.2 us  [body(): pair = lax.all_to_all(pair, 'z', split_axis=0, concat_axis=0, tiled=True)]
    ppermute x1, starting transfers between devices: 7.45 us -> 3.47 us  [body(): got = lax.ppermute(send, 'c', around(NC, 1))]
    ppermute x3, waiting for transfers between devices: 17.3 us -> 21.2 us  [body(): acts = [act] + [lax.ppermute(act, 'x', around(NX, k)) for k in range(1, NX)]]
  transfers between devices with their start and end apart: 10 -> 9, of which waited for: 10 -> 8; matrix products, arithmetic and copies ran while one was open for 0% -> 0% of each run, Pallas kernels for 0% -> 1%
where the time goes in v2:
time: 218 us; the launch traced here: 217 us
  blocking collectives  77 us (35%)
  waiting for transfers between devices  68.2 us (31%)
  starting transfers between devices  50.4 us (23%)
  Pallas kernels  14 us (6%)
  other arithmetic  4.2 us (2%)
  local copies, waits for them, and re-layouts  3.03 us (1%)
    all_to_all x1, blocking collectives, body(): part = lax.all_to_all(part, 'x', split_axis=0, concat_axis=0, tiled=True)  28.6 us
    all_to_all x1, blocking collectives, body(): lax.all_to_all(normed, ('y', 'x'), split_axis=0, concat_axis=0, tiled=True)  26.9 us
    all_to_all x1, waiting for transfers between devices, body(): pair = lax.all_to_all(pair, 'z', split_axis=0, concat_axis=0, tiled=True)  23.6 us
    all_to_all x1, blocking collectives, body(): act = lax.all_to_all(act, 'y', split_axis=0, concat_axis=0, tiled=True)  21.5 us
    ppermute x3, waiting for transfers between devices, body(): acts = [act] + [lax.ppermute(act, 'x', around(NX, k)) for k in range(1, NX)]  21.2 us
    all_to_all x1, waiting for transfers between devices, body(): part = lax.all_to_all(part, 'y', split_axis=0, concat_axis=0, tiled=True)  10.7 us
    all_to_all x1, starting transfers between devices, body(): pair = lax.all_to_all(pair, 'z', split_axis=0, concat_axis=0, tiled=True)  10.2 us
    ppermute x1, waiting for transfers between devices, body(): first = lax.ppermute(jnp.where(odd, high, low), ALL, back[0])  10.1 us
  transfers between devices with their start and end apart: 9, of which 8 were waited for; matrix products, arithmetic and copies ran while one was open for 0% of the time, Pallas kernels for 1%

profile of v2, /device:TPU:33, one launch (start us, length us, event | category | flops | bytes accessed | tf_op | source)
XLA Modules:
  0.0 217.0 jit_solution(847901087418963116)
XLA Ops:
  1.5 1.4 copy-done.1
  3.6 26.9 %all_to_all.25.rows = bf16[32,32,384]{2,1,0:T(8,128)(2,1)S(1)} all-to-all(bf16[32,32,384]{2,1,0:T(8,128)(2,1)S(1)} %norm.1), channel_id=1, replica_groups=mesh['y'=8,'x'=4,'z'=8,'c'=2] {'y','x'}, dimensions={0} | all-to-all | bytes 1572864 | tf_op jit(solution)/shard_map/all_to_all | solution.py:178
  30.5 4.8 %collective-permute-start = (bf16[32,32,384]{2,1,0:T(8,128)(2,1)S(1)}, bf16[32,32,384]{2,1,0:T(8,128)(2,1)S(1)}, u32[]{:S(2)}, u32[]{:S(2)}) collective-permute-start(bf16[32,32,384]{2,1,0:T(8,128)(2,1)S(1)} %all_to_all.25.rows), channel_id=1, source_target_pairs={{0,1},{1,0},{2,3},{3,2},{4,5},{5,4},{6,7},{7,6},{8,9},{9,8},{10,11... | collective-permute-start | bytes 2359304 | tf_op jit(solution)/shard_map/ppermute | solution.py:179
  35.5 3.1 %up_first.1.rest_0_ = bf16[4,8,2,32,512]{4,3,2,1,0:T(8,128)(2,1)S(1)} custom-call(s32[1]{0:T(128)} %bitcast.1.half, s32[64,4]{1,0:T(8,128)S(1)} %bitcast.12, bf16[32,32,384]{2,1,0:T(8,128)(2,1)S(1)} %all_to_all.25.rows, bf16[384,1536]{1,0:T(8,128)(2,1)S(1)} %copy-done), custom_call_target="tpu_custom_call" | custom-call | tf_op jit(solution)/shard_map/up_first/pallas_call | solution.py:88
  38.6 3.1 %up_second.1 = bf16[4,8,2,32,512]{4,3,2,1,0:T(8,128)(2,1)S(1)} custom-call(s32[1]{0:T(128)} %bitcast.5.half, s32[64,4]{1,0:T(8,128)S(1)} %bitcast.13, bf16[32,32,384]{2,1,0:T(8,128)(2,1)S(1)} %collective-permute-done.rows, bf16[384,1536]{1,0:T(8,128)(2,1)S(1)} %copy-done, bf16[4,8,2,32,512]{4,3,2,1,0:T(8,128)(2,1)S(1)} %up_first.1.rest_0_), custom_call_target="tpu_custom_call", output_to_operand_aliasing={{}: (4, {})} | custom-call | tf_op jit(solution)/shard_map/up_second/pallas_call | solution.py:88
  41.8 28.6 %all_to_all.26 = bf16[4,8,64,512]{3,2,1,0:T(8,128)(2,1)S(1)} all-to-all(bf16[4,8,64,512]{3,2,1,0:T(8,128)(2,1)S(1)} %bitcast.11), channel_id=1, replica_groups=mesh['y'=8,'x'=4,'z'=8,'c'=2] {'x'}, dimensions={0} | all-to-all | bytes 4194304 | tf_op jit(solution)/shard_map/all_to_all | solution.py:182
  71.7 8.0 %all-to-all-start.2 = ((bf16[8,64,512]{2,1,0:T(8,128)(2,1)}), bf16[8,64,512]{2,1,0:T(8,128)(2,1)S(1)}, u32[]{:S(2)}, u32[]{:S(2)}) async-start(bf16[8,64,512]{2,1,0:T(8,128)(2,1)} %reduce_sum.24), calls=%async_computation.2 | async-start | bytes 1048576 | tf_op jit(solution)/shard_map/all_to_all | solution.py:184
  79.8 10.7 %all-to-all-done.2.parts = bf16[8,64,512]{2,1,0:T(8,128)(2,1)S(1)} async-done(((bf16[8,64,512]{2,1,0:T(8,128)(2,1)}), bf16[8,64,512]{2,1,0:T(8,128)(2,1)S(1)}, u32[]{:S(2)}, u32[]{:S(2)}) %all-to-all-start.2) | async-done | bytes 524320 | tf_op jit(solution)/shard_map/all_to_all | solution.py:184
  91.7 21.5 %all_to_all.27.a0 = bf16[8,64,512]{2,1,0:T(8,128)(2,1)S(1)} all-to-all(bf16[8,64,512]{2,1,0:T(8,128)(2,1)S(1)} %act.1), channel_id=1, replica_groups=mesh['y'=8,'x'=4,'z'=8,'c'=2] {'y'}, dimensions={0} | all-to-all | bytes 1048576 | tf_op jit(solution)/shard_map/all_to_all | solution.py:188
  113.1 2.2 %collective-permute-start.1 = (bf16[8,64,512]{2,1,0:T(8,128)(2,1)S(1)}, bf16[8,64,512]{2,1,0:T(8,128)(2,1)S(1)}, u32[]{:S(2)}, u32[]{:S(2)}) collective-permute-start(bf16[8,64,512]{2,1,0:T(8,128)(2,1)S(1)} %all_to_all.27.a0), channel_id=1, source_target_pairs={{0,16},{16,32},{32,48},{48,0},{1,17},{17,33},{33,49},{49,1},{2,18}... | collective-permute-start | bytes 1572872 | tf_op jit(solution)/shard_map/ppermute | solution.py:189
  115.3 3.7 %collective-permute-start.2 = (bf16[8,64,512]{2,1,0:T(8,128)(2,1)S(1)}, bf16[8,64,512]{2,1,0:T(8,128)(2,1)S(1)}, u32[]{:S(2)}, u32[]{:S(2)}) collective-permute-start(bf16[8,64,512]{2,1,0:T(8,128)(2,1)S(1)} %all_to_all.27.a0), channel_id=1, source_target_pairs={{0,32},{16,48},{32,0},{48,16},{1,33},{17,49},{33,1},{49,17},{2,34}... | collective-permute-start | bytes 1572872 | tf_op jit(solution)/shard_map/ppermute | solution.py:189
  119.0 2.5 %collective-permute-start.3 = (bf16[8,64,512]{2,1,0:T(8,128)(2,1)S(1)}, bf16[8,64,512]{2,1,0:T(8,128)(2,1)S(1)}, u32[]{:S(2)}, u32[]{:S(2)}) collective-permute-start(bf16[8,64,512]{2,1,0:T(8,128)(2,1)S(1)} %all_to_all.27.a0), channel_id=1, source_target_pairs={{0,48},{16,0},{32,16},{48,32},{1,49},{17,1},{33,17},{49,33},{2,50}... | collective-permute-start | bytes 1572872 | tf_op jit(solution)/shard_map/ppermute | solution.py:189
  121.6 7.2 %collective-permute-done.1.a1 = bf16[8,64,512]{2,1,0:T(8,128)(2,1)S(1)} collective-permute-done((bf16[8,64,512]{2,1,0:T(8,128)(2,1)S(1)}, bf16[8,64,512]{2,1,0:T(8,128)(2,1)S(1)}, u32[]{:S(2)}, u32[]{:S(2)}) %collective-permute-start.1) | collective-permute-done | bytes 524320 | tf_op jit(solution)/shard_map/ppermute | solution.py:189
  128.8 10.1 %collective-permute-done.2.a2 = bf16[8,64,512]{2,1,0:T(8,128)(2,1)S(1)} collective-permute-done((bf16[8,64,512]{2,1,0:T(8,128)(2,1)S(1)}, bf16[8,64,512]{2,1,0:T(8,128)(2,1)S(1)}, u32[]{:S(2)}, u32[]{:S(2)}) %collective-permute-start.2) | collective-permute-done | bytes 524320 | tf_op jit(solution)/shard_map/ppermute | solution.py:189
  138.9 3.9 %collective-permute-done.3.a3 = bf16[8,64,512]{2,1,0:T(8,128)(2,1)S(1)} collective-permute-done((bf16[8,64,512]{2,1,0:T(8,128)(2,1)S(1)}, bf16[8,64,512]{2,1,0:T(8,128)(2,1)S(1)}, u32[]{:S(2)}, u32[]{:S(2)}) %collective-permute-start.3) | collective-permute-done | bytes 524320 | tf_op jit(solution)/shard_map/ppermute | solution.py:189
  142.8 5.9 %down.1 = (bf16[8,2,64,384]{3,2,1,0:T(8,128)(2,1)S(1)}, bf16[8,2,64,384]{3,2,1,0:T(8,128)(2,1)S(1)}) custom-call(s32[3]{0:T(128)S(1)} %pad_add_fusion.where, s32[64,4]{1,0:T(8,128)S(1)} %bitcast.15, bf16[8,64,512]{2,1,0:T(8,128)(2,1)S(1)} %all_to_all.27.a0, bf16[8,64,512]{2,1,0:T(8,128)(2,1)S(1)} %collective-permute-done.1.a1, ...), custom_call_target="tpu_custom_call" | custom-call | tf_op jit(solution)/shard_map/down/pallas_call | solution.py:152
  148.6 3.5 %collective-permute-start.4 = (bf16[8,2,64,384]{3,2,1,0:T(8,128)(2,1)S(1)}, bf16[8,2,64,384]{3,2,1,0:T(8,128)(2,1)S(1)}, u32[]{:S(2)}, u32[]{:S(2)}) collective-permute-start(bf16[8,2,64,384]{3,2,1,0:T(8,128)(2,1)S(1)} %get-tuple-element.8), channel_id=1, source_target_pairs={{0,1},{1,0},{2,3},{3,2},{4,5},{5,4},{6,7},{7,6},{8,9},{9,8},{10,11... | collective-permute-start | bytes 2359304 | tf_op jit(solution)/shard_map/ppermute | solution.py:191
  152.1 1.9 collective-permute-done.4
  155.1 10.2 %all-to-all-start.4 = ((bf16[8,128,384]{2,1,0:T(8,128)(2,1)}), bf16[8,128,384]{2,1,0:T(8,128)(2,1)S(1)}, u32[]{:S(2)}, u32[]{:S(2)}) async-start(bf16[8,128,384]{2,1,0:T(8,128)(2,1)} %bitcast.8), calls=%async_computation.4 | async-start | bytes 1572864 | tf_op jit(solution)/shard_map/all_to_all | solution.py:193
  165.3 23.6 %all-to-all-done.4 = bf16[8,128,384]{2,1,0:T(8,128)(2,1)S(1)} async-done(((bf16[8,128,384]{2,1,0:T(8,128)(2,1)}), bf16[8,128,384]{2,1,0:T(8,128)(2,1)S(1)}, u32[]{:S(2)}, u32[]{:S(2)}) %all-to-all-start.4) | async-done | bytes 786464 | tf_op jit(solution)/shard_map/all_to_all | solution.py:193
  189.0 9.8 %collective-permute-start.5 = (bf16[64,384]{1,0:T(8,128)(2,1)S(1)}, bf16[64,384]{1,0:T(8,128)(2,1)S(1)}, u32[]{:S(2)}, u32[]{:S(2)}) collective-permute-start(bf16[64,384]{1,0:T(8,128)(2,1)S(1)} %get-tuple-element.11), channel_id=1, source_target_pairs={{0,16},{1,48},{2,80},{3,112},{4,144},{5,176},{6,208},{7,240},{8,27... | collective-permute-start | bytes 147464 | tf_op jit(solution)/shard_map/ppermute | solution.py:206
  198.9 5.6 %collective-permute-start.6 = (bf16[64,384]{1,0:T(8,128)(2,1)S(1)}, bf16[64,384]{1,0:T(8,128)(2,1)S(1)}, u32[]{:S(2)}, u32[]{:S(2)}) collective-permute-start(bf16[64,384]{1,0:T(8,128)(2,1)S(1)} %get-tuple-element.12), channel_id=1, source_target_pairs={{0,0},{1,32},{2,64},{3,96},{4,128},{5,160},{6,192},{7,224},{8,256}... | collective-permute-start | bytes 147464 | tf_op jit(solution)/shard_map/ppermute | solution.py:205
  205.3 10.1 %collective-permute-done.6 = bf16[64,384]{1,0:T(8,128)(2,1)S(1)} collective-permute-done((bf16[64,384]{1,0:T(8,128)(2,1)S(1)}, bf16[64,384]{1,0:T(8,128)(2,1)S(1)}, u32[]{:S(2)}, u32[]{:S(2)}) %collective-permute-start.6) | collective-permute-done | bytes 49184 | tf_op jit(solution)/shard_map/ppermute | solution.py:205
  215.4 1.6 add_convert_fusion.1
  (28 shorter events, 6.9 us)
Async XLA Ops:
  1.5 1.4 copy-start.1
  2.9 32.4 %copy-start.5 = (s32[64,1,4]{0,2,1:T(4,128)S(1)}, s32[64,1,4]{0,2,1:T(4,128)}, u32[]{:S(2)}) copy-start(s32[64,1,4]{0,2,1:T(4,128)} %param.16) | copy-start | bytes 3076
  2.9 32.5 %copy-start = (bf16[384,1536]{1,0:T(8,128)(2,1)S(1)}, bf16[384,1536]{1,0:T(8,128)(2,1)}, u32[]{:S(2)}) copy-start(bf16[384,1536]{1,0:T(8,128)(2,1)} %weight.4) | copy-start | bytes 3538948
  30.5 8.1 %collective-permute-start = (bf16[32,32,384]{2,1,0:T(8,128)(2,1)S(1)}, bf16[32,32,384]{2,1,0:T(8,128)(2,1)S(1)}, u32[]{:S(2)}, u32[]{:S(2)}) collective-permute-start(bf16[32,32,384]{2,1,0:T(8,128)(2,1)S(1)} %all_to_all.25.rows), channel_id=1, source_target_pairs={{0,1},{1,0},{2,3},{3,2},{4,5},{5,4},{6,7},{7,6},{8,9},{9,8},{10,11... | collective-permute-start | bytes 2359304 | tf_op jit(solution)/shard_map/ppermute | solution.py:179
  70.4 9.4 %copy-start.4 = (bf16[1536]{0:T(1024)(128)(2,1)S(1)}, bf16[1536]{0:T(1024)(128)(2,1)}, u32[]{:S(2)}) copy-start(bf16[1536]{0:T(1024)(128)(2,1)} %param.13) | copy-start | bytes 9220
  70.4 20.1 %copy-start.3 = (s32[64,1]{0,1:T(1,128)S(1)}, s32[64,1]{0,1:T(1,128)}, u32[]{:S(2)}) copy-start(s32[64,1]{0,1:T(1,128)} %param.17) | copy-start | bytes 772
  71.7 71.1 %copy-start.2 = (bf16[1536,384]{1,0:T(8,128)(2,1)S(1)}, bf16[1536,384]{1,0:T(8,128)(2,1)}, u32[]{:S(2)}) copy-start(bf16[1536,384]{1,0:T(8,128)(2,1)} %weight.5) | copy-start | bytes 3538948
  71.7 18.8 %all-to-all-start.2 = ((bf16[8,64,512]{2,1,0:T(8,128)(2,1)}), bf16[8,64,512]{2,1,0:T(8,128)(2,1)S(1)}, u32[]{:S(2)}, u32[]{:S(2)}) async-start(bf16[8,64,512]{2,1,0:T(8,128)(2,1)} %reduce_sum.24), calls=%async_computation.2 | async-start | bytes 1048576 | tf_op jit(solution)/shard_map/all_to_all | solution.py:184
  113.1 15.7 %collective-permute-start.1 = (bf16[8,64,512]{2,1,0:T(8,128)(2,1)S(1)}, bf16[8,64,512]{2,1,0:T(8,128)(2,1)S(1)}, u32[]{:S(2)}, u32[]{:S(2)}) collective-permute-start(bf16[8,64,512]{2,1,0:T(8,128)(2,1)S(1)} %all_to_all.27.a0), channel_id=1, source_target_pairs={{0,16},{16,32},{32,48},{48,0},{1,17},{17,33},{33,49},{49,1},{2,18}... | collective-permute-start | bytes 1572872 | tf_op jit(solution)/shard_map/ppermute | solution.py:189
  115.3 23.6 %collective-permute-start.2 = (bf16[8,64,512]{2,1,0:T(8,128)(2,1)S(1)}, bf16[8,64,512]{2,1,0:T(8,128)(2,1)S(1)}, u32[]{:S(2)}, u32[]{:S(2)}) collective-permute-start(bf16[8,64,512]{2,1,0:T(8,128)(2,1)S(1)} %all_to_all.27.a0), channel_id=1, source_target_pairs={{0,32},{16,48},{32,0},{48,16},{1,33},{17,49},{33,1},{49,17},{2,34}... | collective-permute-start | bytes 1572872 | tf_op jit(solution)/shard_map/ppermute | solution.py:189
  119.0 23.8 %collective-permute-start.3 = (bf16[8,64,512]{2,1,0:T(8,128)(2,1)S(1)}, bf16[8,64,512]{2,1,0:T(8,128)(2,1)S(1)}, u32[]{:S(2)}, u32[]{:S(2)}) collective-permute-start(bf16[8,64,512]{2,1,0:T(8,128)(2,1)S(1)} %all_to_all.27.a0), channel_id=1, source_target_pairs={{0,48},{16,0},{32,16},{48,32},{1,49},{17,1},{33,17},{49,33},{2,50}... | collective-permute-start | bytes 1572872 | tf_op jit(solution)/shard_map/ppermute | solution.py:189
  148.6 5.4 %collective-permute-start.4 = (bf16[8,2,64,384]{3,2,1,0:T(8,128)(2,1)S(1)}, bf16[8,2,64,384]{3,2,1,0:T(8,128)(2,1)S(1)}, u32[]{:S(2)}, u32[]{:S(2)}) collective-permute-start(bf16[8,2,64,384]{3,2,1,0:T(8,128)(2,1)S(1)} %get-tuple-element.8), channel_id=1, source_target_pairs={{0,1},{1,0},{2,3},{3,2},{4,5},{5,4},{6,7},{7,6},{8,9},{9,8},{10,11... | collective-permute-start | bytes 2359304 | tf_op jit(solution)/shard_map/ppermute | solution.py:191
  155.1 49.4 %copy-start.6 = (bf16[768]{0:T(1024)(128)(2,1)S(1)}, bf16[768]{0:T(1024)(128)(2,1)}, u32[]{:S(2)}) copy-start(bf16[768]{0:T(1024)(128)(2,1)} %param.15) | copy-start | bytes 4612
  155.1 33.7 %all-to-all-start.4 = ((bf16[8,128,384]{2,1,0:T(8,128)(2,1)}), bf16[8,128,384]{2,1,0:T(8,128)(2,1)S(1)}, u32[]{:S(2)}, u32[]{:S(2)}) async-start(bf16[8,128,384]{2,1,0:T(8,128)(2,1)} %bitcast.8), calls=%async_computation.4 | async-start | bytes 1572864 | tf_op jit(solution)/shard_map/all_to_all | solution.py:193
  189.0 16.3 %collective-permute-start.5 = (bf16[64,384]{1,0:T(8,128)(2,1)S(1)}, bf16[64,384]{1,0:T(8,128)(2,1)S(1)}, u32[]{:S(2)}, u32[]{:S(2)}) collective-permute-start(bf16[64,384]{1,0:T(8,128)(2,1)S(1)} %get-tuple-element.11), channel_id=1, source_target_pairs={{0,16},{1,48},{2,80},{3,112},{4,144},{5,176},{6,208},{7,240},{8,27... | collective-permute-start | bytes 147464 | tf_op jit(solution)/shard_map/ppermute | solution.py:206
  198.9 16.5 %collective-permute-start.6 = (bf16[64,384]{1,0:T(8,128)(2,1)S(1)}, bf16[64,384]{1,0:T(8,128)(2,1)S(1)}, u32[]{:S(2)}, u32[]{:S(2)}) collective-permute-start(bf16[64,384]{1,0:T(8,128)(2,1)S(1)} %get-tuple-element.12), channel_id=1, source_target_pairs={{0,0},{1,32},{2,64},{3,96},{4,128},{5,160},{6,192},{7,224},{8,256}... | collective-permute-start | bytes 147464 | tf_op jit(solution)/shard_map/ppermute | solution.py:205

commit v3 on v2

--- a/solution.py
+++ b/solution.py
@@ -1,3 +1,5 @@
+import functools
+
 import jax
 import jax.numpy as jnp
 from jax import lax
@@ -38,7 +40,8 @@
     spread = jnp.sum(total, axis=1, keepdims=True) / features
     scale = lax.rsqrt(spread + 1e-05)
     for p in range(pieces):
-        value = (piece(p) - mean) * scale * gain[p : p + 1, :] + shift[p : p + 1, :]
+        at = slice(p * PIECE, (p + 1) * PIECE)
+        value = (piece(p) - mean) * scale * gain[:, at].astype(F32) + shift[:, at].astype(F32)
         out[p] = value.astype(BF16)
 
 
@@ -53,8 +56,8 @@
             grid=(1,),
             in_specs=[
                 pl.BlockSpec((GROUP, features), lambda i, half: (half[0], 0)),
-                pl.BlockSpec((pieces, PIECE), lambda i, half: (0, 0)),
-                pl.BlockSpec((pieces, PIECE), lambda i, half: (0, 0)),
+                pl.BlockSpec((1, features), lambda i, half: (0, 0)),
+                pl.BlockSpec((1, features), lambda i, half: (0, 0)),
             ],
             out_specs=pl.BlockSpec((pieces, GROUP, PIECE), lambda i, half: (0, 0, 0)),
         ),
@@ -65,36 +68,40 @@
 
 SMEM = pl.BlockSpec(memory_space=pltpu.SMEM)
 VMEM = pl.BlockSpec(memory_space=pltpu.VMEM)
-TOGETHER = 8
-
-
-def up_kernel(half, ids, rows, weight, *rest):
-    out, total = rest[-2:]
-    h = half[0]
-    for first in range(0, NY * NX, TOGETHER):
-        block_rows = rows[first : first + TOGETHER].reshape(TOGETHER * GROUP, PIECE)
+ORDER = (1, 3, 2)
+
+
+def up_kernel(steps, at, ids, rows, weight, *rest):
+    total = rest[-1]
+    outs = rest[-1 - len(steps) : -1]
+    h, x = at[0], at[1]
+    for k, out in zip(steps, outs):
+        target = lax.rem(x + k, NX)
+        block_rows = rows[:, target].reshape(NY * GROUP, PIECE)
         total[...] = jnp.dot(block_rows, weight[...], preferred_element_type=F32)
-        for i in range(TOGETHER):
-            r = first + i
+        for y in range(NY):
+            group = (y * NX + target) * (ROW // GROUP) + h
             for s in range(CAP):
-                at = pl.multiple_of(ids[2 * r + h, s] * BLOCK, BLOCK)
-                picked = total[i * GROUP : (i + 1) * GROUP, pl.ds(at, BLOCK)]
-                out[r % NX, r // NX, h, :, s * BLOCK : (s + 1) * BLOCK] = picked.astype(BF16)
-
-
-def up(half, ids, rows, weight, before=None):
-    shape = (NX, NY, ROW // GROUP, GROUP, CAP * BLOCK)
-    more = () if before is None else (before,)
-    return pl.pallas_call(
-        up_kernel,
-        out_shape=jax.ShapeDtypeStruct(shape, BF16),
-        in_specs=[SMEM, SMEM, VMEM, VMEM] + [VMEM] * len(more),
-        out_specs=VMEM,
-        scratch_shapes=[pltpu.VMEM((TOGETHER * GROUP, weight.shape[1]), F32)],
-        input_output_aliases={4: 0} if more else {},
+                block = pl.multiple_of(ids[group, s] * BLOCK, BLOCK)
+                picked = total[y * GROUP : (y + 1) * GROUP, pl.ds(block, BLOCK)]
+                out[y, h, :, s * BLOCK : (s + 1) * BLOCK] = picked.astype(BF16)
+
+
+def up(steps, at, ids, rows, weight, before=()):
+    shape = jax.ShapeDtypeStruct((NY, ROW // GROUP, GROUP, CAP * BLOCK), BF16)
+    return pl.pallas_call(
+        functools.partial(up_kernel, steps),
+        out_shape=[shape] * len(steps),
+        in_specs=[SMEM, SMEM, VMEM, VMEM] + [VMEM] * len(before),
+        out_specs=[VMEM] * len(steps),
+        scratch_shapes=[pltpu.VMEM((NY * GROUP, weight.shape[1]), F32)],
+        input_output_aliases={4 + i: i for i in range(len(before))},
+        cost_estimate=pl.CostEstimate(
+            flops=2 * len(steps) * NY * GROUP * weight.size, bytes_accessed=0, transcendentals=0
+        ),
         compiler_params=pltpu.CompilerParams(vmem_limit_bytes=24 * 2**20),
-        name="up_second" if more else "up_first",
-    )(half, ids, rows, weight, *more)
+        name="up_second" if before else "up_first",
+    )(at, ids, rows, weight, *before)
 
 
 def act_kernel(where, ids, valid, parts, bias, out):
@@ -121,9 +128,11 @@
     )(where, ids, valid, parts, bias)
 
 
-def down_kernel(where, ids, a0, a1, a2, a3, weight, keep, send, wide):
+def down_kernel(steps, where, ids, *rest):
+    acts, weight = rest[: len(steps)], rest[len(steps)]
+    keep, send, wide = rest[-3:]
     x, c = where[2], where[1]
-    for k, ref in enumerate((a0, a1, a2, a3)):
+    for k, ref in zip(steps, acts):
         source = lax.rem(x + NX - k, NX)
         wide[...] = jnp.zeros_like(wide)
         for y in range(NY):
@@ -148,16 +157,20 @@
             send[:, part] = value
 
 
-def down(where, ids, acts, weight):
-    return pl.pallas_call(
-        down_kernel,
+def down(steps, where, ids, acts, weight, before=()):
+    return pl.pallas_call(
+        functools.partial(down_kernel, steps),
         out_shape=[jax.ShapeDtypeStruct((NY, 2, ROW, PIECE), BF16)] * 2,
-        in_specs=[SMEM, SMEM] + [VMEM] * 5,
+        in_specs=[SMEM, SMEM] + [VMEM] * (len(steps) + 1 + len(before)),
         out_specs=[VMEM, VMEM],
         scratch_shapes=[pltpu.VMEM((NY * ROW, weight.shape[0]), BF16)],
+        input_output_aliases={3 + len(steps) + i: i for i in range(len(before))},
+        cost_estimate=pl.CostEstimate(
+            flops=2 * len(steps) * NY * ROW * weight.size, bytes_accessed=0, transcendentals=0
+        ),
         compiler_params=pltpu.CompilerParams(vmem_limit_bytes=24 * 2**20),
         name="down",
-    )(where, ids, *acts, weight)
+    )(where, ids, *acts, weight, *before)
 
 
 def body(
@@ -171,23 +184,27 @@
     where = jnp.stack([r, c, x]).astype(jnp.int32)
     width = down_bias.shape[0]
 
-    mine, others = c.reshape(1), (1 - c).reshape(1)
-    gain = norm_gain.astype(F32).reshape(-1, PIECE)
-    shift = norm_shift.astype(F32).reshape(-1, PIECE)
-    normed = norm(mine, hidden_in, gain, shift)
+    mine, others = jnp.stack([c, x]).astype(jnp.int32), jnp.stack([1 - c, x]).astype(jnp.int32)
+    normed = norm(c.reshape(1), hidden_in, norm_gain.reshape(1, -1), norm_shift.reshape(1, -1))
     own = lax.all_to_all(normed, ("y", "x"), split_axis=0, concat_axis=0, tiled=True)
     other = lax.ppermute(own, "c", around(NC, 1))
-    part = up(mine, ids, own, up_weight)
-    part = up(others, ids, other, up_weight, part).reshape(NX, NY, ROW, CAP * BLOCK)
-    part = lax.all_to_all(part, "x", split_axis=0, concat_axis=0, tiled=True)
-    part = jnp.sum(part.astype(F32), axis=0).astype(BF16)
+    own, other = (v.reshape(NY, NX, GROUP, PIECE) for v in (own, other))
+    first = up(ORDER + (0,), mine, ids, own, up_weight)
+    sums = []
+    for k, before in zip(ORDER + (0,), first):
+        (part,) = up((k,), others, ids, other, up_weight, (before,))
+        part = part.reshape(NY, ROW, CAP * BLOCK)
+        sums.append(lax.ppermute(part, "x", around(NX, k)) if k else part)
+    part = sum(v.astype(F32) for v in sums).astype(BF16)
     part = lax.all_to_all(part, "y", split_axis=0, concat_axis=0, tiled=True)
     bias = up_bias.astype(F32).reshape(-1, BLOCK)
     act = activate(where, ids, valid, part, bias)
 
     act = lax.all_to_all(act, "y", split_axis=0, concat_axis=0, tiled=True)
-    acts = [act] + [lax.ppermute(act, "x", around(NX, k)) for k in range(1, NX)]
-    keep, send = down(where, ids, acts, down_weight)
+    keep, send = down((0,), where, ids, (act,), down_weight)
+    for k in ORDER:
+        moved = lax.ppermute(act, "x", around(NX, k))
+        keep, send = down((k,), where, ids, (moved,), down_weight, (keep, send))
     got = lax.ppermute(send, "c", around(NC, 1))
     pair = (keep.astype(F32) + got.astype(F32)).astype(BF16).reshape(NZ, 2 * ROW, PIECE)
     pair = lax.all_to_all(pair, "z", split_axis=0, concat_axis=0, tiled=True)

time: 218 us -> 213 us (0.977)
  blocking collectives: 77 us -> 44.9 us
  starting transfers between devices: 50.4 us -> 70.1 us
  Pallas kernels: 14 us -> 21 us
    all_to_all x1 -> x0, blocking collectives: 28.6 us -> none  [body(): part = lax.all_to_all(part, 'x', split_axis=0, concat_axis=0, tiled=True)]
    ppermute x3 -> x6, starting transfers between devices: 8.4 us -> 22.1 us  [the longest x3 13.6 us: body(): moved = lax.ppermute(act, 'x', around(NX, k))]
    pallas_call x3 -> x9, Pallas kernels: 12.1 us -> 19.1 us  [the longest x5 9.99 us: up(): pl.pallas_call(functools.partial(up_kernel, steps), out_shape=[shape] * l...]
    ppermute x3 -> x6, waiting for transfers between devices: 21.2 us -> 25.1 us  [the longest x3 16.5 us: body(): sums.append(lax.ppermute(part, 'x', around(NX, k)) if k else part)]
    ppermute x1, starting transfers between devices: 5.65 us -> 9.12 us  [body(): first = lax.ppermute(jnp.where(odd, high, low), ALL, back[0])]
    all_to_all x1, blocking collectives: 21.5 us -> 18 us  [body(): act = lax.all_to_all(act, 'y', split_axis=0, concat_axis=0, tiled=True)]
    ppermute x1, waiting for transfers between devices: 10.1 us -> 7.36 us  [body(): first = lax.ppermute(jnp.where(odd, high, low), ALL, back[0])]
    ppermute x1, starting transfers between devices: 9.81 us -> 12.2 us  [body(): second = lax.ppermute(jnp.where(odd, low, high), ALL, back[1])]
  transfers between devices with their start and end apart: 9 -> 12, of which waited for: 8 -> 9; matrix products, arithmetic and copies ran while one was open for 0% -> 0% of each run, Pallas kernels for 1% -> 7%
where the time goes in v3:
time: 213 us; the launch traced here: 212 us
  starting transfers between devices  70.1 us (33%)
  waiting for transfers between devices  68.3 us (32%)
  blocking collectives  44.9 us (21%)
  Pallas kernels  21 us (10%)
  other arithmetic  4.13 us (2%)
  local copies, waits for them, and re-layouts  3.06 us (1%)
    all_to_all x1, blocking collectives, body(): lax.all_to_all(normed, ('y', 'x'), split_axis=0, concat_axis=0, tiled=True)  26.9 us
    all_to_all x1, waiting for transfers between devices, body(): pair = lax.all_to_all(pair, 'z', split_axis=0, concat_axis=0, tiled=True)  23.6 us
    all_to_all x1, blocking collectives, body(): act = lax.all_to_all(act, 'y', split_axis=0, concat_axis=0, tiled=True)  18 us
    ppermute x3, waiting for transfers between devices, body(): sums.append(lax.ppermute(part, 'x', around(NX, k)) if k else part)  16.5 us
    ppermute x3, starting transfers between devices, body(): moved = lax.ppermute(act, 'x', around(NX, k))  13.6 us
    ppermute x1, starting transfers between devices, body(): second = lax.ppermute(jnp.where(odd, low, high), ALL, back[1])  12.2 us
    all_to_all x1, waiting for transfers between devices, body(): part = lax.all_to_all(part, 'y', split_axis=0, concat_axis=0, tiled=True)  10.4 us
    all_to_all x1, starting transfers between devices, body(): pair = lax.all_to_all(pair, 'z', split_axis=0, concat_axis=0, tiled=True)  10.2 us
  transfers between devices with their start and end apart: 12, of which 9 were waited for; matrix products, arithmetic and copies ran while one was open for 0% of the time, Pallas kernels for 7%

profile of v3, /device:TPU:33, one launch (start us, length us, event | category | flops | bytes accessed | tf_op | source)
XLA Modules:
  0.0 211.8 jit_solution(4305966881873402322)
XLA Ops:
  3.7 26.9 %all_to_all.20 = bf16[32,32,384]{2,1,0:T(8,128)(2,1)S(1)} all-to-all(bf16[32,32,384]{2,1,0:T(8,128)(2,1)S(1)} %norm.1), channel_id=1, replica_groups=mesh['y'=8,'x'=4,'z'=8,'c'=2] {'y','x'}, dimensions={0} | all-to-all | bytes 1572864 | tf_op jit(solution)/shard_map/all_to_all | solution.py:189
  30.6 4.8 %collective-permute-start = (bf16[32,32,384]{2,1,0:T(8,128)(2,1)S(1)}, bf16[32,32,384]{2,1,0:T(8,128)(2,1)S(1)}, u32[]{:S(2)}, u32[]{:S(2)}) collective-permute-start(bf16[32,32,384]{2,1,0:T(8,128)(2,1)S(1)} %all_to_all.20), channel_id=1, source_target_pairs={{0,1},{1,0},{2,3},{3,2},{4,5},{5,4},{6,7},{7,6},{8,9},{9,8},{10,11... | collective-permute-start | bytes 2359304 | tf_op jit(solution)/shard_map/ppermute | solution.py:190
  35.6 3.2 %up_first.1 = (bf16[8,2,32,512]{3,2,1,0:T(8,128)(2,1)S(1)}, bf16[8,2,32,512]{3,2,1,0:T(8,128)(2,1)S(1)}, bf16[8,2,32,512]{3,2,1,0:T(8,128)(2,1)S(1)}, bf16[8,2,32,512]{3,2,1,0:T(8,128)(2,1)S(1)}) custom-call(s32[2]{0:T(128)S(1)} %get-tuple-element.34.at, s32[64,4]{1,0:T(8,128)S(1)} %bitcast.22, bf16[8,4,32,384]{3,2,1,0:T(8,128)(2,1)S(1)} %bitcast.32, ...), custom_call_target="tpu_custom_call" | custom-call | flops 1207959552 | tf_op jit(solution)/shard_map/up_first/pallas_call | solution.py:92
  40.5 2.1 collective-permute-start.1
  44.3 4.4 %collective-permute-start.2 = (bf16[8,64,512]{2,1,0:T(8,128)(2,1)S(1)}, bf16[8,64,512]{2,1,0:T(8,128)(2,1)S(1)}, u32[]{:S(2)}, u32[]{:S(2)}) collective-permute-start(bf16[8,64,512]{2,1,0:T(8,128)(2,1)S(1)} %bitcast.34), channel_id=1, source_target_pairs={{0,48},{16,0},{32,16},{48,32},{1,49},{17,1},{33,17},{49,33},{2,50}... | collective-permute-start | bytes 1572872 | tf_op jit(solution)/shard_map/ppermute | solution.py:197
  50.5 2.1 collective-permute-start.3
  54.3 14.1 %collective-permute-done.1 = bf16[8,64,512]{2,1,0:T(8,128)(2,1)S(1)} collective-permute-done((bf16[8,64,512]{2,1,0:T(8,128)(2,1)S(1)}, bf16[8,64,512]{2,1,0:T(8,128)(2,1)S(1)}, u32[]{:S(2)}, u32[]{:S(2)}) %collective-permute-start.1) | collective-permute-done | bytes 524320 | tf_op jit(solution)/shard_map/ppermute | solution.py:197
  68.4 2.4 %collective-permute-done.2 = bf16[8,64,512]{2,1,0:T(8,128)(2,1)S(1)} collective-permute-done((bf16[8,64,512]{2,1,0:T(8,128)(2,1)S(1)}, bf16[8,64,512]{2,1,0:T(8,128)(2,1)S(1)}, u32[]{:S(2)}, u32[]{:S(2)}) %collective-permute-start.2) | collective-permute-done | bytes 524320 | tf_op jit(solution)/shard_map/ppermute | solution.py:197
  72.0 6.8 %all-to-all-start.1 = ((bf16[8,64,512]{2,1,0:T(8,128)(2,1)}), bf16[8,64,512]{2,1,0:T(8,128)(2,1)S(1)}, u32[]{:S(2)}, u32[]{:S(2)}) async-start(bf16[8,64,512]{2,1,0:T(8,128)(2,1)} %fusion), calls=%async_computation.1 | async-start | bytes 1048576 | tf_op jit(solution)/shard_map/all_to_all | solution.py:199
  78.8 10.4 %all-to-all-done.1.parts = bf16[8,64,512]{2,1,0:T(8,128)(2,1)S(1)} async-done(((bf16[8,64,512]{2,1,0:T(8,128)(2,1)}), bf16[8,64,512]{2,1,0:T(8,128)(2,1)S(1)}, u32[]{:S(2)}, u32[]{:S(2)}) %all-to-all-start.1) | async-done | bytes 524320 | tf_op jit(solution)/shard_map/all_to_all | solution.py:199
  90.4 18.0 %all_to_all.21.rest_0_ = bf16[8,64,512]{2,1,0:T(8,128)(2,1)S(1)} all-to-all(bf16[8,64,512]{2,1,0:T(8,128)(2,1)S(1)} %act.1), channel_id=1, replica_groups=mesh['y'=8,'x'=4,'z'=8,'c'=2] {'y'}, dimensions={0} | all-to-all | bytes 1048576 | tf_op jit(solution)/shard_map/all_to_all | solution.py:203
  108.4 7.9 %collective-permute-start.6 = (bf16[8,64,512]{2,1,0:T(8,128)(2,1)S(1)}, bf16[8,64,512]{2,1,0:T(8,128)(2,1)S(1)}, u32[]{:S(2)}, u32[]{:S(2)}) collective-permute-start(bf16[8,64,512]{2,1,0:T(8,128)(2,1)S(1)} %all_to_all.21.rest_0_), channel_id=1, source_target_pairs={{0,16},{16,32},{32,48},{48,0},{1,17},{17,33},{33,49},{49,1},{2,18}... | collective-permute-start | bytes 1572872 | tf_op jit(solution)/shard_map/ppermute | solution.py:206
  118.3 3.7 %collective-permute-start.4 = (bf16[8,64,512]{2,1,0:T(8,128)(2,1)S(1)}, bf16[8,64,512]{2,1,0:T(8,128)(2,1)S(1)}, u32[]{:S(2)}, u32[]{:S(2)}) collective-permute-start(bf16[8,64,512]{2,1,0:T(8,128)(2,1)S(1)} %all_to_all.21.rest_0_), channel_id=1, source_target_pairs={{0,32},{16,48},{32,0},{48,16},{1,33},{17,49},{33,1},{49,17},{2,34}... | collective-permute-start | bytes 1572872 | tf_op jit(solution)/shard_map/ppermute | solution.py:206
  122.0 2.3 %down.4 = (bf16[8,2,64,384]{3,2,1,0:T(8,128)(2,1)S(1)}, bf16[8,2,64,384]{3,2,1,0:T(8,128)(2,1)S(1)}) custom-call(s32[3]{0:T(128)S(1)} %pad_add_fusion.where, s32[64,4]{1,0:T(8,128)S(1)} %bitcast.28, bf16[8,64,512]{2,1,0:T(8,128)(2,1)S(1)} %all_to_all.21.rest_0_, bf16[1536,384]{1,0:T(8,128)(2,1)S(1)} %copy-done.1), custom_call_target="tpu_custom_call" | custom-call | flops 603979776 | tf_op jit(solution)/shard_map/down/pallas_call | solution.py:161
  126.1 2.3 %down.5 = (bf16[8,2,64,384]{3,2,1,0:T(8,128)(2,1)S(1)}, bf16[8,2,64,384]{3,2,1,0:T(8,128)(2,1)S(1)}) custom-call(s32[3]{0:T(128)S(1)} %pad_add_fusion.where, s32[64,4]{1,0:T(8,128)S(1)} %bitcast.29, bf16[8,64,512]{2,1,0:T(8,128)(2,1)S(1)} %collective-permute-done.6.rest_0_, ...), custom_call_target="tpu_custom_call", output_to_operand_aliasing={{0}: (4, {}), {1}: (5, {})} | custom-call | flops 603979776 | tf_op jit(solution)/shard_map/down/pallas_call | solution.py:161
  130.0 2.3 %down.6 = (bf16[8,2,64,384]{3,2,1,0:T(8,128)(2,1)S(1)}, bf16[8,2,64,384]{3,2,1,0:T(8,128)(2,1)S(1)}) custom-call(s32[3]{0:T(128)S(1)} %pad_add_fusion.where, s32[64,4]{1,0:T(8,128)S(1)} %bitcast.30, bf16[8,64,512]{2,1,0:T(8,128)(2,1)S(1)} %collective-permute-done.5.rest_0_, ...), custom_call_target="tpu_custom_call", output_to_operand_aliasing={{0}: (4, {}), {1}: (5, {})} | custom-call | flops 603979776 | tf_op jit(solution)/shard_map/down/pallas_call | solution.py:161
  132.2 5.1 %collective-permute-done.4.rest_0_ = bf16[8,64,512]{2,1,0:T(8,128)(2,1)S(1)} collective-permute-done((bf16[8,64,512]{2,1,0:T(8,128)(2,1)S(1)}, bf16[8,64,512]{2,1,0:T(8,128)(2,1)S(1)}, u32[]{:S(2)}, u32[]{:S(2)}) %collective-permute-start.4) | collective-permute-done | bytes 524320 | tf_op jit(solution)/shard_map/ppermute | solution.py:206
  137.4 2.3 %down.7 = (bf16[8,2,64,384]{3,2,1,0:T(8,128)(2,1)S(1)}, bf16[8,2,64,384]{3,2,1,0:T(8,128)(2,1)S(1)}) custom-call(s32[3]{0:T(128)S(1)} %pad_add_fusion.where, s32[64,4]{1,0:T(8,128)S(1)} %bitcast.31, bf16[8,64,512]{2,1,0:T(8,128)(2,1)S(1)} %collective-permute-done.4.rest_0_, ...), custom_call_target="tpu_custom_call", output_to_operand_aliasing={{0}: (4, {}), {1}: (5, {})} | custom-call | flops 603979776 | tf_op jit(solution)/shard_map/down/pallas_call | solution.py:161
  139.7 4.8 %collective-permute-start.7 = (bf16[8,2,64,384]{3,2,1,0:T(8,128)(2,1)S(1)}, bf16[8,2,64,384]{3,2,1,0:T(8,128)(2,1)S(1)}, u32[]{:S(2)}, u32[]{:S(2)}) collective-permute-start(bf16[8,2,64,384]{3,2,1,0:T(8,128)(2,1)S(1)} %get-tuple-element.28), channel_id=1, source_target_pairs={{0,1},{1,0},{2,3},{3,2},{4,5},{5,4},{6,7},{7,6},{8,9},{9,8},{10,11... | collective-permute-start | bytes 2359304 | tf_op jit(solution)/shard_map/ppermute | solution.py:208
  147.5 10.2 %all-to-all-start.3 = ((bf16[8,128,384]{2,1,0:T(8,128)(2,1)}), bf16[8,128,384]{2,1,0:T(8,128)(2,1)S(1)}, u32[]{:S(2)}, u32[]{:S(2)}) async-start(bf16[8,128,384]{2,1,0:T(8,128)(2,1)} %bitcast.13), calls=%async_computation.3 | async-start | bytes 1572864 | tf_op jit(solution)/shard_map/all_to_all | solution.py:210
  157.7 23.6 %all-to-all-done.3 = bf16[8,128,384]{2,1,0:T(8,128)(2,1)S(1)} async-done(((bf16[8,128,384]{2,1,0:T(8,128)(2,1)}), bf16[8,128,384]{2,1,0:T(8,128)(2,1)S(1)}, u32[]{:S(2)}, u32[]{:S(2)}) %all-to-all-start.3) | async-done | bytes 786464 | tf_op jit(solution)/shard_map/all_to_all | solution.py:210
  181.4 12.2 %collective-permute-start.8 = (bf16[64,384]{1,0:T(8,128)(2,1)S(1)}, bf16[64,384]{1,0:T(8,128)(2,1)S(1)}, u32[]{:S(2)}, u32[]{:S(2)}) collective-permute-start(bf16[64,384]{1,0:T(8,128)(2,1)S(1)} %get-tuple-element.31), channel_id=1, source_target_pairs={{0,16},{1,48},{2,80},{3,112},{4,144},{5,176},{6,208},{7,240},{8,27... | collective-permute-start | bytes 147464 | tf_op jit(solution)/shard_map/ppermute | solution.py:223
  193.6 9.1 %collective-permute-start.9 = (bf16[64,384]{1,0:T(8,128)(2,1)S(1)}, bf16[64,384]{1,0:T(8,128)(2,1)S(1)}, u32[]{:S(2)}, u32[]{:S(2)}) collective-permute-start(bf16[64,384]{1,0:T(8,128)(2,1)S(1)} %get-tuple-element.32), channel_id=1, source_target_pairs={{0,0},{1,32},{2,64},{3,96},{4,128},{5,160},{6,192},{7,224},{8,256}... | collective-permute-start | bytes 147464 | tf_op jit(solution)/shard_map/ppermute | solution.py:222
  202.8 7.4 %collective-permute-done.9 = bf16[64,384]{1,0:T(8,128)(2,1)S(1)} collective-permute-done((bf16[64,384]{1,0:T(8,128)(2,1)S(1)}, bf16[64,384]{1,0:T(8,128)(2,1)S(1)}, u32[]{:S(2)}, u32[]{:S(2)}) %collective-permute-start.9) | collective-permute-done | bytes 49184 | tf_op jit(solution)/shard_map/ppermute | solution.py:222
  (40 shorter events, 23.2 us)
Async XLA Ops:
  1.5 1.4 copy-start.2
  3.0 32.5 %copy-start.5 = (s32[64,1,4]{0,2,1:T(4,128)S(1)}, s32[64,1,4]{0,2,1:T(4,128)}, u32[]{:S(2)}) copy-start(s32[64,1,4]{0,2,1:T(4,128)} %param.16) | copy-start | bytes 3076
  3.0 32.7 %copy-start = (bf16[384,1536]{1,0:T(8,128)(2,1)S(1)}, bf16[384,1536]{1,0:T(8,128)(2,1)}, u32[]{:S(2)}) copy-start(bf16[384,1536]{1,0:T(8,128)(2,1)} %weight.9) | copy-start | bytes 3538948
  30.6 8.2 %collective-permute-start = (bf16[32,32,384]{2,1,0:T(8,128)(2,1)S(1)}, bf16[32,32,384]{2,1,0:T(8,128)(2,1)S(1)}, u32[]{:S(2)}, u32[]{:S(2)}) collective-permute-start(bf16[32,32,384]{2,1,0:T(8,128)(2,1)S(1)} %all_to_all.20), channel_id=1, source_target_pairs={{0,1},{1,0},{2,3},{3,2},{4,5},{5,4},{6,7},{7,6},{8,9},{9,8},{10,11... | collective-permute-start | bytes 2359304 | tf_op jit(solution)/shard_map/ppermute | solution.py:190
  40.5 27.9 %collective-permute-start.1 = (bf16[8,64,512]{2,1,0:T(8,128)(2,1)S(1)}, bf16[8,64,512]{2,1,0:T(8,128)(2,1)S(1)}, u32[]{:S(2)}, u32[]{:S(2)}) collective-permute-start(bf16[8,64,512]{2,1,0:T(8,128)(2,1)S(1)} %bitcast.35), channel_id=1, source_target_pairs={{0,16},{16,32},{32,48},{48,0},{1,17},{17,33},{33,49},{49,1},{2,18}... | collective-permute-start | bytes 1572872 | tf_op jit(solution)/shard_map/ppermute | solution.py:197
  44.3 26.5 %collective-permute-start.2 = (bf16[8,64,512]{2,1,0:T(8,128)(2,1)S(1)}, bf16[8,64,512]{2,1,0:T(8,128)(2,1)S(1)}, u32[]{:S(2)}, u32[]{:S(2)}) collective-permute-start(bf16[8,64,512]{2,1,0:T(8,128)(2,1)S(1)} %bitcast.34), channel_id=1, source_target_pairs={{0,48},{16,0},{32,16},{48,32},{1,49},{17,1},{33,17},{49,33},{2,50}... | collective-permute-start | bytes 1572872 | tf_op jit(solution)/shard_map/ppermute | solution.py:197
  50.5 20.4 %collective-permute-start.3 = (bf16[8,64,512]{2,1,0:T(8,128)(2,1)S(1)}, bf16[8,64,512]{2,1,0:T(8,128)(2,1)S(1)}, u32[]{:S(2)}, u32[]{:S(2)}) collective-permute-start(bf16[8,64,512]{2,1,0:T(8,128)(2,1)S(1)} %bitcast.33), channel_id=1, source_target_pairs={{0,32},{16,48},{32,0},{48,16},{1,33},{17,49},{33,1},{49,17},{2,34}... | collective-permute-start | bytes 1572872 | tf_op jit(solution)/shard_map/ppermute | solution.py:197
  54.3 24.5 %copy-start.4 = (bf16[1536]{0:T(1024)(128)(2,1)S(1)}, bf16[1536]{0:T(1024)(128)(2,1)}, u32[]{:S(2)}) copy-start(bf16[1536]{0:T(1024)(128)(2,1)} %param.13) | copy-start | bytes 9220
  54.3 34.9 %copy-start.3 = (s32[64,1]{0,1:T(1,128)S(1)}, s32[64,1]{0,1:T(1,128)}, u32[]{:S(2)}) copy-start(s32[64,1]{0,1:T(1,128)} %param.17) | copy-start | bytes 772
  72.0 50.0 %copy-start.1 = (bf16[1536,384]{1,0:T(8,128)(2,1)S(1)}, bf16[1536,384]{1,0:T(8,128)(2,1)}, u32[]{:S(2)}) copy-start(bf16[1536,384]{1,0:T(8,128)(2,1)} %rest_1_.7) | copy-start | bytes 3538948
  72.0 17.2 %all-to-all-start.1 = ((bf16[8,64,512]{2,1,0:T(8,128)(2,1)}), bf16[8,64,512]{2,1,0:T(8,128)(2,1)S(1)}, u32[]{:S(2)}, u32[]{:S(2)}) async-start(bf16[8,64,512]{2,1,0:T(8,128)(2,1)} %fusion), calls=%async_computation.1 | async-start | bytes 1048576 | tf_op jit(solution)/shard_map/all_to_all | solution.py:199
  108.4 17.8 %collective-permute-start.6 = (bf16[8,64,512]{2,1,0:T(8,128)(2,1)S(1)}, bf16[8,64,512]{2,1,0:T(8,128)(2,1)S(1)}, u32[]{:S(2)}, u32[]{:S(2)}) collective-permute-start(bf16[8,64,512]{2,1,0:T(8,128)(2,1)S(1)} %all_to_all.21.rest_0_), channel_id=1, source_target_pairs={{0,16},{16,32},{32,48},{48,0},{1,17},{17,33},{33,49},{49,1},{2,18}... | collective-permute-start | bytes 1572872 | tf_op jit(solution)/shard_map/ppermute | solution.py:206
  116.3 13.6 %collective-permute-start.5 = (bf16[8,64,512]{2,1,0:T(8,128)(2,1)S(1)}, bf16[8,64,512]{2,1,0:T(8,128)(2,1)S(1)}, u32[]{:S(2)}, u32[]{:S(2)}) collective-permute-start(bf16[8,64,512]{2,1,0:T(8,128)(2,1)S(1)} %all_to_all.21.rest_0_), channel_id=1, source_target_pairs={{0,48},{16,0},{32,16},{48,32},{1,49},{17,1},{33,17},{49,33},{2,50}... | collective-permute-start | bytes 1572872 | tf_op jit(solution)/shard_map/ppermute | solution.py:206
  118.3 19.1 %collective-permute-start.4 = (bf16[8,64,512]{2,1,0:T(8,128)(2,1)S(1)}, bf16[8,64,512]{2,1,0:T(8,128)(2,1)S(1)}, u32[]{:S(2)}, u32[]{:S(2)}) collective-permute-start(bf16[8,64,512]{2,1,0:T(8,128)(2,1)S(1)} %all_to_all.21.rest_0_), channel_id=1, source_target_pairs={{0,32},{16,48},{32,0},{48,16},{1,33},{17,49},{33,1},{49,17},{2,34}... | collective-permute-start | bytes 1572872 | tf_op jit(solution)/shard_map/ppermute | solution.py:206
  139.7 6.7 %collective-permute-start.7 = (bf16[8,2,64,384]{3,2,1,0:T(8,128)(2,1)S(1)}, bf16[8,2,64,384]{3,2,1,0:T(8,128)(2,1)S(1)}, u32[]{:S(2)}, u32[]{:S(2)}) collective-permute-start(bf16[8,2,64,384]{3,2,1,0:T(8,128)(2,1)S(1)} %get-tuple-element.28), channel_id=1, source_target_pairs={{0,1},{1,0},{2,3},{3,2},{4,5},{5,4},{6,7},{7,6},{8,9},{9,8},{10,11... | collective-permute-start | bytes 2359304 | tf_op jit(solution)/shard_map/ppermute | solution.py:208
  147.5 55.3 %copy-start.6 = (bf16[768]{0:T(1024)(128)(2,1)S(1)}, bf16[768]{0:T(1024)(128)(2,1)}, u32[]{:S(2)}) copy-start(bf16[768]{0:T(1024)(128)(2,1)} %param.15) | copy-start | bytes 4612
  147.5 33.7 %all-to-all-start.3 = ((bf16[8,128,384]{2,1,0:T(8,128)(2,1)}), bf16[8,128,384]{2,1,0:T(8,128)(2,1)S(1)}, u32[]{:S(2)}, u32[]{:S(2)}) async-start(bf16[8,128,384]{2,1,0:T(8,128)(2,1)} %bitcast.13), calls=%async_computation.3 | async-start | bytes 1572864 | tf_op jit(solution)/shard_map/all_to_all | solution.py:210
  181.4 21.4 %collective-permute-start.8 = (bf16[64,384]{1,0:T(8,128)(2,1)S(1)}, bf16[64,384]{1,0:T(8,128)(2,1)S(1)}, u32[]{:S(2)}, u32[]{:S(2)}) collective-permute-start(bf16[64,384]{1,0:T(8,128)(2,1)S(1)} %get-tuple-element.31), channel_id=1, source_target_pairs={{0,16},{1,48},{2,80},{3,112},{4,144},{5,176},{6,208},{7,240},{8,27... | collective-permute-start | bytes 147464 | tf_op jit(solution)/shard_map/ppermute | solution.py:223
  193.6 16.5 %collective-permute-start.9 = (bf16[64,384]{1,0:T(8,128)(2,1)S(1)}, bf16[64,384]{1,0:T(8,128)(2,1)S(1)}, u32[]{:S(2)}, u32[]{:S(2)}) collective-permute-start(bf16[64,384]{1,0:T(8,128)(2,1)S(1)} %get-tuple-element.32), channel_id=1, source_target_pairs={{0,0},{1,32},{2,64},{3,96},{4,128},{5,160},{6,192},{7,224},{8,256}... | collective-permute-start | bytes 147464 | tf_op jit(solution)/shard_map/ppermute | solution.py:222

commit v4 on v3

--- a/solution.py
+++ b/solution.py
@@ -1,4 +1,5 @@
 import functools
+import itertools
 
 import jax
 import jax.numpy as jnp
@@ -25,6 +26,8 @@
 def norm_kernel(half, hidden, gain, shift, out):
     rows, features = hidden.shape
     pieces = features // PIECE
+    gains = gain[...].astype(F32).reshape(1, features)
+    shifts = shift[...].astype(F32).reshape(1, features)
 
     def piece(p):
         return hidden[:, p * PIECE : (p + 1) * PIECE].astype(F32)
@@ -41,7 +44,7 @@
     scale = lax.rsqrt(spread + 1e-05)
     for p in range(pieces):
         at = slice(p * PIECE, (p + 1) * PIECE)
-        value = (piece(p) - mean) * scale * gain[:, at].astype(F32) + shift[:, at].astype(F32)
+        value = (piece(p) - mean) * scale * gains[:, at] + shifts[:, at]
         out[p] = value.astype(BF16)
 
 
@@ -56,8 +59,8 @@
             grid=(1,),
             in_specs=[
                 pl.BlockSpec((GROUP, features), lambda i, half: (half[0], 0)),
-                pl.BlockSpec((1, features), lambda i, half: (0, 0)),
-                pl.BlockSpec((1, features), lambda i, half: (0, 0)),
+                pl.BlockSpec((features,), lambda i, half: (0,)),
+                pl.BlockSpec((features,), lambda i, half: (0,)),
             ],
             out_specs=pl.BlockSpec((pieces, GROUP, PIECE), lambda i, half: (0, 0, 0)),
         ),
@@ -128,11 +131,15 @@
     )(where, ids, valid, parts, bias)
 
 
-def down_kernel(steps, where, ids, *rest):
-    acts, weight = rest[: len(steps)], rest[len(steps)]
-    keep, send, wide = rest[-3:]
-    x, c = where[2], where[1]
-    for k, ref in zip(steps, acts):
+TURNS = ((0, 0), (3, 1), (2, 3), (1, 2))
+
+
+def down_kernel(turns, outs, where, ids, *rest):
+    acts, weight = rest[: len(turns)], rest[len(turns)]
+    (keep, *send), wide = rest[-1 - outs : -1], rest[-1]
+    c, x, high = where[1], where[2], where[3]
+    for turn, ref in zip(turns, acts):
+        k = jnp.where(c == 0, TURNS[turn][0], TURNS[turn][1])
         source = lax.rem(x + NX - k, NX)
         wide[...] = jnp.zeros_like(wide)
         for y in range(NY):
@@ -146,31 +153,43 @@
                     ]
         value = jnp.dot(wide[...], weight[...], preferred_element_type=F32).astype(BF16)
         value = value.reshape(NY, ROW, PIECE)
-        own, part = source // 2 == c, lax.rem(source, 2)
-
-        @pl.when(own)
-        def _():
-            keep[:, part] = value
-
-        @pl.when(jnp.logical_not(own))
-        def _():
-            send[:, part] = value
-
-
-def down(steps, where, ids, acts, weight, before=()):
-    return pl.pallas_call(
-        functools.partial(down_kernel, steps),
-        out_shape=[jax.ShapeDtypeStruct((NY, 2, ROW, PIECE), BF16)] * 2,
-        in_specs=[SMEM, SMEM] + [VMEM] * (len(steps) + 1 + len(before)),
-        out_specs=[VMEM, VMEM],
+        part = lax.rem(k, 2)
+
+        def put(ref, value=value, part=part):
+            for y in range(NY):
+                ref[lax.rem(y + NZ - high, NZ), part] = value[y]
+
+        own = [k_of // 2 == core for core, k_of in enumerate(TURNS[turn])]
+        if own[0] == own[1]:
+            put(keep if own[0] else send[0])
+        else:
+            pl.when(c == own.index(True))(functools.partial(put, keep))
+            pl.when(c == own.index(False))(functools.partial(put, send[0]))
+
+
+def down(turns, where, ids, acts, weight, before=()):
+    outs = len(before) or 2
+    return pl.pallas_call(
+        functools.partial(down_kernel, turns, outs),
+        out_shape=[jax.ShapeDtypeStruct((NY, 2, ROW, PIECE), BF16)] * outs,
+        in_specs=[SMEM, SMEM] + [VMEM] * (len(turns) + 1 + len(before)),
+        out_specs=[VMEM] * outs,
         scratch_shapes=[pltpu.VMEM((NY * ROW, weight.shape[0]), BF16)],
-        input_output_aliases={3 + len(steps) + i: i for i in range(len(before))},
+        input_output_aliases={3 + len(turns) + i: i for i in range(len(before))},
         cost_estimate=pl.CostEstimate(
-            flops=2 * len(steps) * NY * ROW * weight.size, bytes_accessed=0, transcendentals=0
+            flops=(32 if outs == 1 else 1) * 2 * len(turns) * NY * ROW * weight.size,
+            bytes_accessed=0,
+            transcendentals=0,
         ),
         compiler_params=pltpu.CompilerParams(vmem_limit_bytes=24 * 2**20),
         name="down",
     )(where, ids, *acts, weight, *before)
+
+
+def turn_pairs(turn):
+    return [
+        (x * NC + c, (x + TURNS[turn][c]) % NX * NC + c) for x in range(NX) for c in range(NC)
+    ]
 
 
 def body(
@@ -181,11 +200,11 @@
     r, t = y * NX + x, z * NC + c
     odd = lax.rem(r, 2) == 1
     ids, valid = active[:, 0, :], counts[:, 0]
-    where = jnp.stack([r, c, x]).astype(jnp.int32)
+    where = jnp.stack([r, c, x, y]).astype(jnp.int32)
     width = down_bias.shape[0]
 
     mine, others = jnp.stack([c, x]).astype(jnp.int32), jnp.stack([1 - c, x]).astype(jnp.int32)
-    normed = norm(c.reshape(1), hidden_in, norm_gain.reshape(1, -1), norm_shift.reshape(1, -1))
+    normed = norm(c.reshape(1), hidden_in, norm_gain, norm_shift)
     own = lax.all_to_all(normed, ("y", "x"), split_axis=0, concat_axis=0, tiled=True)
     other = lax.ppermute(own, "c", around(NC, 1))
     own, other = (v.reshape(NY, NX, GROUP, PIECE) for v in (own, other))
@@ -202,25 +221,23 @@
 
     act = lax.all_to_all(act, "y", split_axis=0, concat_axis=0, tiled=True)
     keep, send = down((0,), where, ids, (act,), down_weight)
-    for k in ORDER:
-        moved = lax.ppermute(act, "x", around(NX, k))
-        keep, send = down((k,), where, ids, (moved,), down_weight, (keep, send))
+    for turn in (1, 2):
+        moved = lax.ppermute(act, ("x", "c"), turn_pairs(turn))
+        keep, send = down((turn,), where, ids, (moved,), down_weight, (keep, send))
     got = lax.ppermute(send, "c", around(NC, 1))
+    moved = lax.ppermute(act, ("x", "c"), turn_pairs(3))
+    (keep,) = down((3,), where, ids, (moved,), down_weight, (keep,))
     pair = (keep.astype(F32) + got.astype(F32)).astype(BF16).reshape(NZ, 2 * ROW, PIECE)
     pair = lax.all_to_all(pair, "z", split_axis=0, concat_axis=0, tiled=True)
     branch = jnp.sum(pair.astype(F32), axis=0).astype(BF16)
 
-    back = [
-        [
-            (p * 16 + q, (2 * q + (j ^ (p & 1))) * 16 + p // 2)
-            for p in range(32)
-            for q in range(16)
-        ]
-        for j in range(2)
-    ]
-    low, high = branch[:ROW], branch[ROW:]
-    first = lax.ppermute(jnp.where(odd, high, low), ALL, back[0])
-    second = lax.ppermute(jnp.where(odd, low, high), ALL, back[1])
+    back = [[], []]
+    for j, ys, xs, zs, cs in itertools.product(range(2), *map(range, (NY, NX, NZ, NC))):
+        row = (zs + ys) % NY * NX + (xs - 2 * cs - j) % NX
+        source = ((ys * NX + xs) * NZ + zs) * NC + cs
+        back[j].append((source, row * NZ * NC + (ys * NX + xs) // 2))
+    first = lax.ppermute(branch[:ROW], ALL, back[0])
+    second = lax.ppermute(branch[ROW:], ALL, back[1])
     summed = jnp.concatenate(
         [jnp.where(odd, second, first), jnp.where(odd, first, second)], axis=1
     ).astype(F32)

time: 213 us -> 208 us (0.977)
  the two profiles are of different devices: /device:TPU:33 before, /device:TPU:176 now
where the time goes in v4:
time: 208 us; the launch traced here: 204 us
  blocking collectives  83.3 us (40%)
  starting transfers between devices  50.4 us (24%)
  waiting for transfers between devices  42.9 us (21%)
  Pallas kernels  20.9 us (10%)
  other arithmetic  3.23 us (2%)
  local copies, waits for them, and re-layouts  3.02 us (1%)
    all_to_all x1, blocking collectives, body(): pair = lax.all_to_all(pair, 'z', split_axis=0, concat_axis=0, tiled=True)  35.4 us
    all_to_all x1, blocking collectives, body(): lax.all_to_all(normed, ('y', 'x'), split_axis=0, concat_axis=0, tiled=True)  29.1 us
    all_to_all x1, blocking collectives, body(): act = lax.all_to_all(act, 'y', split_axis=0, concat_axis=0, tiled=True)  18.8 us
    ppermute x3, waiting for transfers between devices, body(): sums.append(lax.ppermute(part, 'x', around(NX, k)) if k else part)  16 us
    all_to_all x1, waiting for transfers between devices, body(): part = lax.all_to_all(part, 'y', split_axis=0, concat_axis=0, tiled=True)  13 us
    ppermute x3, starting transfers between devices, body(): sums.append(lax.ppermute(part, 'x', around(NX, k)) if k else part)  10.5 us
    ppermute x2, starting transfers between devices, body(): moved = lax.ppermute(act, ('x', 'c'), turn_pairs(turn))  10.2 us
    pallas_call x5, Pallas kernels, up(): pl.pallas_call(functools.partial(up_kernel, steps), out_shape=[shape] * l...  9.96 us
  transfers between devices with their start and end apart: 11, of which 7 were waited for; matrix products, arithmetic and copies ran while one was open for 0% of the time, Pallas kernels for 8%

profile of v4, /device:TPU:176, one launch (start us, length us, event | category | flops | bytes accessed | tf_op | source)
XLA Modules:
  0.0 204.1 jit_solution(3742406649014999147)
XLA Ops:
  3.6 29.1 %all_to_all.20 = bf16[32,32,384]{2,1,0:T(8,128)(2,1)S(1)} all-to-all(bf16[32,32,384]{2,1,0:T(8,128)(2,1)S(1)} %norm.1), channel_id=1, replica_groups=mesh['y'=8,'x'=4,'z'=8,'c'=2] {'y','x'}, dimensions={0} | all-to-all | bytes 1572864 | tf_op jit(solution)/shard_map/all_to_all | solution.py:208
  32.8 1.9 collective-permute-start
  34.9 3.1 %up_first.1 = (bf16[8,2,32,512]{3,2,1,0:T(8,128)(2,1)S(1)}, bf16[8,2,32,512]{3,2,1,0:T(8,128)(2,1)S(1)}, bf16[8,2,32,512]{3,2,1,0:T(8,128)(2,1)S(1)}, bf16[8,2,32,512]{3,2,1,0:T(8,128)(2,1)S(1)}) custom-call(s32[2]{0:T(128)S(1)} %get-tuple-element.30.at, s32[64,4]{1,0:T(8,128)S(1)} %bitcast.23, bf16[8,4,32,384]{3,2,1,0:T(8,128)(2,1)S(1)} %bitcast.33, ...), custom_call_target="tpu_custom_call" | custom-call | flops 1207959552 | tf_op jit(solution)/shard_map/up_first/pallas_call | solution.py:95
  39.7 3.1 %collective-permute-start.1 = (bf16[8,64,512]{2,1,0:T(8,128)(2,1)S(1)}, bf16[8,64,512]{2,1,0:T(8,128)(2,1)S(1)}, u32[]{:S(2)}, u32[]{:S(2)}) collective-permute-start(bf16[8,64,512]{2,1,0:T(8,128)(2,1)S(1)} %bitcast.36), channel_id=1, source_target_pairs={{0,16},{16,32},{32,48},{48,0},{1,17},{17,33},{33,49},{49,1},{2,18}... | collective-permute-start | bytes 1572872 | tf_op jit(solution)/shard_map/ppermute | solution.py:216
  44.6 3.9 %collective-permute-start.2 = (bf16[8,64,512]{2,1,0:T(8,128)(2,1)S(1)}, bf16[8,64,512]{2,1,0:T(8,128)(2,1)S(1)}, u32[]{:S(2)}, u32[]{:S(2)}) collective-permute-start(bf16[8,64,512]{2,1,0:T(8,128)(2,1)S(1)} %bitcast.35), channel_id=1, source_target_pairs={{0,48},{16,0},{32,16},{48,32},{1,49},{17,1},{33,17},{49,33},{2,50}... | collective-permute-start | bytes 1572872 | tf_op jit(solution)/shard_map/ppermute | solution.py:216
  50.2 3.4 %collective-permute-start.3 = (bf16[8,64,512]{2,1,0:T(8,128)(2,1)S(1)}, bf16[8,64,512]{2,1,0:T(8,128)(2,1)S(1)}, u32[]{:S(2)}, u32[]{:S(2)}) collective-permute-start(bf16[8,64,512]{2,1,0:T(8,128)(2,1)S(1)} %bitcast.34), channel_id=1, source_target_pairs={{0,32},{16,48},{32,0},{48,16},{1,33},{17,49},{33,1},{49,17},{2,34}... | collective-permute-start | bytes 1572872 | tf_op jit(solution)/shard_map/ppermute | solution.py:216
  57.2 14.2 %collective-permute-done.2 = bf16[8,64,512]{2,1,0:T(8,128)(2,1)S(1)} collective-permute-done((bf16[8,64,512]{2,1,0:T(8,128)(2,1)S(1)}, bf16[8,64,512]{2,1,0:T(8,128)(2,1)S(1)}, u32[]{:S(2)}, u32[]{:S(2)}) %collective-permute-start.2) | collective-permute-done | bytes 524320 | tf_op jit(solution)/shard_map/ppermute | solution.py:216
  72.5 7.2 %all-to-all-start.1 = ((bf16[8,64,512]{2,1,0:T(8,128)(2,1)}), bf16[8,64,512]{2,1,0:T(8,128)(2,1)S(1)}, u32[]{:S(2)}, u32[]{:S(2)}) async-start(bf16[8,64,512]{2,1,0:T(8,128)(2,1)} %fusion), calls=%async_computation.1 | async-start | bytes 1048576 | tf_op jit(solution)/shard_map/all_to_all | solution.py:218
  79.7 13.0 %all-to-all-done.1.parts = bf16[8,64,512]{2,1,0:T(8,128)(2,1)S(1)} async-done(((bf16[8,64,512]{2,1,0:T(8,128)(2,1)}), bf16[8,64,512]{2,1,0:T(8,128)(2,1)S(1)}, u32[]{:S(2)}, u32[]{:S(2)}) %all-to-all-start.1) | async-done | bytes 524320 | tf_op jit(solution)/shard_map/all_to_all | solution.py:218
  93.9 18.8 %all_to_all.21.rest_0_ = bf16[8,64,512]{2,1,0:T(8,128)(2,1)S(1)} all-to-all(bf16[8,64,512]{2,1,0:T(8,128)(2,1)S(1)} %act.1), channel_id=1, replica_groups=mesh['y'=8,'x'=4,'z'=8,'c'=2] {'y'}, dimensions={0} | all-to-all | bytes 1048576 | tf_op jit(solution)/shard_map/all_to_all | solution.py:222
  112.8 6.0 %collective-permute-start.6 = (bf16[8,64,512]{2,1,0:T(8,128)(2,1)S(1)}, bf16[8,64,512]{2,1,0:T(8,128)(2,1)S(1)}, u32[]{:S(2)}, u32[]{:S(2)}) collective-permute-start(bf16[8,64,512]{2,1,0:T(8,128)(2,1)S(1)} %all_to_all.21.rest_0_), channel_id=1, source_target_pairs={{0,48},{1,17},{16,0},{17,33},{32,16},{33,49},{48,32},{49,1},{2,50}... | collective-permute-start | bytes 1572872 | tf_op jit(solution)/shard_map/ppermute | solution.py:225
  118.8 4.2 %collective-permute-start.5 = (bf16[8,64,512]{2,1,0:T(8,128)(2,1)S(1)}, bf16[8,64,512]{2,1,0:T(8,128)(2,1)S(1)}, u32[]{:S(2)}, u32[]{:S(2)}) collective-permute-start(bf16[8,64,512]{2,1,0:T(8,128)(2,1)S(1)} %all_to_all.21.rest_0_), channel_id=1, source_target_pairs={{0,32},{1,49},{16,48},{17,1},{32,0},{33,17},{48,16},{49,33},{2,34}... | collective-permute-start | bytes 1572872 | tf_op jit(solution)/shard_map/ppermute | solution.py:225
  123.0 1.9 collective-permute-start.4
  124.9 2.3 %down.4 = (bf16[8,2,64,384]{3,2,1,0:T(8,128)(2,1)S(1)}, bf16[8,2,64,384]{3,2,1,0:T(8,128)(2,1)S(1)}) custom-call(s32[4]{0:T(128)S(1)} %pad_add_fusion.where, s32[64,4]{1,0:T(8,128)S(1)} %bitcast.29, bf16[8,64,512]{2,1,0:T(8,128)(2,1)S(1)} %all_to_all.21.rest_0_, bf16[1536,384]{1,0:T(8,128)(2,1)S(1)} %copy-done.1), custom_call_target="tpu_custom_call" | custom-call | flops 603979776 | tf_op jit(solution)/shard_map/down/pallas_call | solution.py:172
  127.2 4.6 %collective-permute-done.6.rest_0_ = bf16[8,64,512]{2,1,0:T(8,128)(2,1)S(1)} collective-permute-done((bf16[8,64,512]{2,1,0:T(8,128)(2,1)S(1)}, bf16[8,64,512]{2,1,0:T(8,128)(2,1)S(1)}, u32[]{:S(2)}, u32[]{:S(2)}) %collective-permute-start.6) | collective-permute-done | bytes 524320 | tf_op jit(solution)/shard_map/ppermute | solution.py:225
  131.8 2.2 %down.5 = (bf16[8,2,64,384]{3,2,1,0:T(8,128)(2,1)S(1)}, bf16[8,2,64,384]{3,2,1,0:T(8,128)(2,1)S(1)}) custom-call(s32[4]{0:T(128)S(1)} %pad_add_fusion.where, s32[64,4]{1,0:T(8,128)S(1)} %bitcast.30, bf16[8,64,512]{2,1,0:T(8,128)(2,1)S(1)} %collective-permute-done.6.rest_0_, ...), custom_call_target="tpu_custom_call", output_to_operand_aliasing={{0}: (4, {}), {1}: (5, {})} | custom-call | flops 603979776 | tf_op jit(solution)/shard_map/down/pallas_call | solution.py:172
  134.1 2.7 %collective-permute-done.5.rest_0_ = bf16[8,64,512]{2,1,0:T(8,128)(2,1)S(1)} collective-permute-done((bf16[8,64,512]{2,1,0:T(8,128)(2,1)S(1)}, bf16[8,64,512]{2,1,0:T(8,128)(2,1)S(1)}, u32[]{:S(2)}, u32[]{:S(2)}) %collective-permute-start.5) | collective-permute-done | bytes 524320 | tf_op jit(solution)/shard_map/ppermute | solution.py:225
  136.8 2.3 %down.6 = (bf16[8,2,64,384]{3,2,1,0:T(8,128)(2,1)S(1)}, bf16[8,2,64,384]{3,2,1,0:T(8,128)(2,1)S(1)}) custom-call(s32[4]{0:T(128)S(1)} %pad_add_fusion.where, s32[64,4]{1,0:T(8,128)S(1)} %bitcast.31, bf16[8,64,512]{2,1,0:T(8,128)(2,1)S(1)} %collective-permute-done.5.rest_0_, ...), custom_call_target="tpu_custom_call", output_to_operand_aliasing={{0}: (4, {}), {1}: (5, {})} | custom-call | flops 603979776 | tf_op jit(solution)/shard_map/down/pallas_call | solution.py:172
  139.1 1.9 collective-permute-start.7
  142.6 2.2 %down.7 = bf16[8,2,64,384]{3,2,1,0:T(8,128)(2,1)S(1)} custom-call(s32[4]{0:T(128)S(1)} %pad_add_fusion.where, s32[64,4]{1,0:T(8,128)S(1)} %bitcast.32, bf16[8,64,512]{2,1,0:T(8,128)(2,1)S(1)} %collective-permute-done.4.rest_0_, bf16[1536,384]{1,0:T(8,128)(2,1)S(1)} %copy-done.1, ...), custom_call_target="tpu_custom_call", output_to_operand_aliasing={{}: (4, {})} | custom-call | flops 19327352832 | tf_op jit(solution)/shard_map/down/pallas_call | solution.py:172
  145.1 35.4 %all_to_all.22 = bf16[8,128,384]{2,1,0:T(8,128)(2,1)S(1)} all-to-all(bf16[8,128,384]{2,1,0:T(8,128)(2,1)S(1)} %bitcast.38), channel_id=1, replica_groups=mesh['y'=8,'x'=4,'z'=8,'c'=2] {'z'}, dimensions={0} | all-to-all | bytes 1572864 | tf_op jit(solution)/shard_map/all_to_all | solution.py:231
  180.7 8.4 %collective-permute-start.8 = (bf16[64,384]{1,0:T(8,128)(2,1)S(1)}, bf16[64,384]{1,0:T(8,128)(2,1)S(1)}, u32[]{:S(2)}, u32[]{:S(2)}) collective-permute-start(bf16[64,384]{1,0:T(8,128)(2,1)S(1)} %get-tuple-element.27), channel_id=1, source_target_pairs={{0,48},{1,16},{2,112},{3,80},{4,176},{5,144},{6,240},{7,208},{8,30... | collective-permute-start | bytes 147464 | tf_op jit(solution)/shard_map/ppermute | solution.py:240
  189.1 8.3 %collective-permute-start.9 = (bf16[64,384]{1,0:T(8,128)(2,1)S(1)}, bf16[64,384]{1,0:T(8,128)(2,1)S(1)}, u32[]{:S(2)}, u32[]{:S(2)}) collective-permute-start(bf16[64,384]{1,0:T(8,128)(2,1)S(1)} %get-tuple-element.28), channel_id=1, source_target_pairs={{0,0},{1,32},{2,64},{3,96},{4,128},{5,160},{6,192},{7,224},{8,256}... | collective-permute-start | bytes 147464 | tf_op jit(solution)/shard_map/ppermute | solution.py:239
  197.4 5.0 %collective-permute-done.9 = bf16[64,384]{1,0:T(8,128)(2,1)S(1)} collective-permute-done((bf16[64,384]{1,0:T(8,128)(2,1)S(1)}, bf16[64,384]{1,0:T(8,128)(2,1)S(1)}, u32[]{:S(2)}, u32[]{:S(2)}) %collective-permute-start.9) | collective-permute-done | bytes 49184 | tf_op jit(solution)/shard_map/ppermute | solution.py:239
  (41 shorter events, 18.4 us)
Async XLA Ops:
  0.0 1.4 copy-start.2
  1.4 0.7 copy-start.3
  2.1 0.7 copy-start.4
  2.9 31.8 %copy-start.7 = (s32[64,1,4]{0,2,1:T(4,128)S(1)}, s32[64,1,4]{0,2,1:T(4,128)}, u32[]{:S(2)}) copy-start(s32[64,1,4]{0,2,1:T(4,128)} %param.16) | copy-start | bytes 3076
  2.9 32.0 %copy-start = (bf16[384,1536]{1,0:T(8,128)(2,1)S(1)}, bf16[384,1536]{1,0:T(8,128)(2,1)}, u32[]{:S(2)}) copy-start(bf16[384,1536]{1,0:T(8,128)(2,1)} %weight.9) | copy-start | bytes 3538948
  32.8 5.2 %collective-permute-start = (bf16[32,32,384]{2,1,0:T(8,128)(2,1)S(1)}, bf16[32,32,384]{2,1,0:T(8,128)(2,1)S(1)}, u32[]{:S(2)}, u32[]{:S(2)}) collective-permute-start(bf16[32,32,384]{2,1,0:T(8,128)(2,1)S(1)} %all_to_all.20), channel_id=1, source_target_pairs={{0,1},{1,0},{2,3},{3,2},{4,5},{5,4},{6,7},{7,6},{8,9},{9,8},{10,11... | collective-permute-start | bytes 2359304 | tf_op jit(solution)/shard_map/ppermute | solution.py:209
  39.7 17.4 %collective-permute-start.1 = (bf16[8,64,512]{2,1,0:T(8,128)(2,1)S(1)}, bf16[8,64,512]{2,1,0:T(8,128)(2,1)S(1)}, u32[]{:S(2)}, u32[]{:S(2)}) collective-permute-start(bf16[8,64,512]{2,1,0:T(8,128)(2,1)S(1)} %bitcast.36), channel_id=1, source_target_pairs={{0,16},{16,32},{32,48},{48,0},{1,17},{17,33},{33,49},{49,1},{2,18}... | collective-permute-start | bytes 1572872 | tf_op jit(solution)/shard_map/ppermute | solution.py:216
  44.6 26.8 %collective-permute-start.2 = (bf16[8,64,512]{2,1,0:T(8,128)(2,1)S(1)}, bf16[8,64,512]{2,1,0:T(8,128)(2,1)S(1)}, u32[]{:S(2)}, u32[]{:S(2)}) collective-permute-start(bf16[8,64,512]{2,1,0:T(8,128)(2,1)S(1)} %bitcast.35), channel_id=1, source_target_pairs={{0,48},{16,0},{32,16},{48,32},{1,49},{17,1},{33,17},{49,33},{2,50}... | collective-permute-start | bytes 1572872 | tf_op jit(solution)/shard_map/ppermute | solution.py:216
  50.2 21.1 %collective-permute-start.3 = (bf16[8,64,512]{2,1,0:T(8,128)(2,1)S(1)}, bf16[8,64,512]{2,1,0:T(8,128)(2,1)S(1)}, u32[]{:S(2)}, u32[]{:S(2)}) collective-permute-start(bf16[8,64,512]{2,1,0:T(8,128)(2,1)S(1)} %bitcast.34), channel_id=1, source_target_pairs={{0,32},{16,48},{32,0},{48,16},{1,33},{17,49},{33,1},{49,17},{2,34}... | collective-permute-start | bytes 1572872 | tf_op jit(solution)/shard_map/ppermute | solution.py:216
  55.4 24.4 %copy-start.6 = (bf16[1536]{0:T(1024)(128)(2,1)S(1)}, bf16[1536]{0:T(1024)(128)(2,1)}, u32[]{:S(2)}) copy-start(bf16[1536]{0:T(1024)(128)(2,1)} %param.13) | copy-start | bytes 9220
  55.4 37.4 %copy-start.5 = (s32[64,1]{0,1:T(1,128)S(1)}, s32[64,1]{0,1:T(1,128)}, u32[]{:S(2)}) copy-start(s32[64,1]{0,1:T(1,128)} %param.17) | copy-start | bytes 772
  72.5 52.5 %copy-start.1 = (bf16[1536,384]{1,0:T(8,128)(2,1)S(1)}, bf16[1536,384]{1,0:T(8,128)(2,1)}, u32[]{:S(2)}) copy-start(bf16[1536,384]{1,0:T(8,128)(2,1)} %rest_1_.7) | copy-start | bytes 3538948
  72.5 20.3 %all-to-all-start.1 = ((bf16[8,64,512]{2,1,0:T(8,128)(2,1)}), bf16[8,64,512]{2,1,0:T(8,128)(2,1)S(1)}, u32[]{:S(2)}, u32[]{:S(2)}) async-start(bf16[8,64,512]{2,1,0:T(8,128)(2,1)} %fusion), calls=%async_computation.1 | async-start | bytes 1048576 | tf_op jit(solution)/shard_map/all_to_all | solution.py:218
  112.8 19.1 %collective-permute-start.6 = (bf16[8,64,512]{2,1,0:T(8,128)(2,1)S(1)}, bf16[8,64,512]{2,1,0:T(8,128)(2,1)S(1)}, u32[]{:S(2)}, u32[]{:S(2)}) collective-permute-start(bf16[8,64,512]{2,1,0:T(8,128)(2,1)S(1)} %all_to_all.21.rest_0_), channel_id=1, source_target_pairs={{0,48},{1,17},{16,0},{17,33},{32,16},{33,49},{48,32},{49,1},{2,50}... | collective-permute-start | bytes 1572872 | tf_op jit(solution)/shard_map/ppermute | solution.py:225
  118.8 18.0 %collective-permute-start.5 = (bf16[8,64,512]{2,1,0:T(8,128)(2,1)S(1)}, bf16[8,64,512]{2,1,0:T(8,128)(2,1)S(1)}, u32[]{:S(2)}, u32[]{:S(2)}) collective-permute-start(bf16[8,64,512]{2,1,0:T(8,128)(2,1)S(1)} %all_to_all.21.rest_0_), channel_id=1, source_target_pairs={{0,32},{1,49},{16,48},{17,1},{32,0},{33,17},{48,16},{49,33},{2,34}... | collective-permute-start | bytes 1572872 | tf_op jit(solution)/shard_map/ppermute | solution.py:225
  123.0 19.6 %collective-permute-start.4 = (bf16[8,64,512]{2,1,0:T(8,128)(2,1)S(1)}, bf16[8,64,512]{2,1,0:T(8,128)(2,1)S(1)}, u32[]{:S(2)}, u32[]{:S(2)}) collective-permute-start(bf16[8,64,512]{2,1,0:T(8,128)(2,1)S(1)} %all_to_all.21.rest_0_), channel_id=1, source_target_pairs={{0,16},{1,33},{16,32},{17,49},{32,48},{33,1},{48,0},{49,17},{2,18}... | collective-permute-start | bytes 1572872 | tf_op jit(solution)/shard_map/ppermute | solution.py:228
  139.1 5.7 %collective-permute-start.7 = (bf16[8,2,64,384]{3,2,1,0:T(8,128)(2,1)S(1)}, bf16[8,2,64,384]{3,2,1,0:T(8,128)(2,1)S(1)}, u32[]{:S(2)}, u32[]{:S(2)}) collective-permute-start(bf16[8,2,64,384]{3,2,1,0:T(8,128)(2,1)S(1)} %get-tuple-element.24), channel_id=1, source_target_pairs={{0,1},{1,0},{2,3},{3,2},{4,5},{5,4},{6,7},{7,6},{8,9},{9,8},{10,11... | collective-permute-start | bytes 2359304 | tf_op jit(solution)/shard_map/ppermute | solution.py:227
  145.1 52.3 %copy-start.8 = (bf16[768]{0:T(1024)(128)(2,1)S(1)}, bf16[768]{0:T(1024)(128)(2,1)}, u32[]{:S(2)}) copy-start(bf16[768]{0:T(1024)(128)(2,1)} %param.15) | copy-start | bytes 4612
  180.7 16.8 %collective-permute-start.8 = (bf16[64,384]{1,0:T(8,128)(2,1)S(1)}, bf16[64,384]{1,0:T(8,128)(2,1)S(1)}, u32[]{:S(2)}, u32[]{:S(2)}) collective-permute-start(bf16[64,384]{1,0:T(8,128)(2,1)S(1)} %get-tuple-element.27), channel_id=1, source_target_pairs={{0,48},{1,16},{2,112},{3,80},{4,176},{5,144},{6,240},{7,208},{8,30... | collective-permute-start | bytes 147464 | tf_op jit(solution)/shard_map/ppermute | solution.py:240
  189.1 13.4 %collective-permute-start.9 = (bf16[64,384]{1,0:T(8,128)(2,1)S(1)}, bf16[64,384]{1,0:T(8,128)(2,1)S(1)}, u32[]{:S(2)}, u32[]{:S(2)}) collective-permute-start(bf16[64,384]{1,0:T(8,128)(2,1)S(1)} %get-tuple-element.28), channel_id=1, source_target_pairs={{0,0},{1,32},{2,64},{3,96},{4,128},{5,160},{6,192},{7,224},{8,256}... | collective-permute-start | bytes 147464 | tf_op jit(solution)/shard_map/ppermute | solution.py:239

commit v5 on v4

--- a/solution.py
+++ b/solution.py
@@ -23,11 +23,9 @@
     return [(i, (i + k) % size) for i in range(size)]
 
 
-def norm_kernel(half, hidden, gain, shift, out):
+def norm_kernel(half, hidden, scales, out):
     rows, features = hidden.shape
     pieces = features // PIECE
-    gains = gain[...].astype(F32).reshape(1, features)
-    shifts = shift[...].astype(F32).reshape(1, features)
 
     def piece(p):
         return hidden[:, p * PIECE : (p + 1) * PIECE].astype(F32)
@@ -44,11 +42,11 @@
     scale = lax.rsqrt(spread + 1e-05)
     for p in range(pieces):
         at = slice(p * PIECE, (p + 1) * PIECE)
-        value = (piece(p) - mean) * scale * gains[:, at] + shifts[:, at]
+        value = (piece(p) - mean) * scale * scales[0:1, at] + scales[1:2, at]
         out[p] = value.astype(BF16)
 
 
-def norm(half, hidden, gain, shift):
+def norm(half, hidden, scales):
     features = hidden.shape[1]
     pieces = features // PIECE
     return pl.pallas_call(
@@ -59,26 +57,26 @@
             grid=(1,),
             in_specs=[
                 pl.BlockSpec((GROUP, features), lambda i, half: (half[0], 0)),
-                pl.BlockSpec((features,), lambda i, half: (0,)),
-                pl.BlockSpec((features,), lambda i, half: (0,)),
+                pl.BlockSpec((2, features), lambda i, half: (0, 0)),
             ],
             out_specs=pl.BlockSpec((pieces, GROUP, PIECE), lambda i, half: (0, 0, 0)),
         ),
         compiler_params=pltpu.CompilerParams(vmem_limit_bytes=32 * 2**20),
         name="norm",
-    )(half, hidden, gain, shift)
+    )(half, hidden, scales)
 
 
 SMEM = pl.BlockSpec(memory_space=pltpu.SMEM)
 VMEM = pl.BlockSpec(memory_space=pltpu.VMEM)
-ORDER = (1, 3, 2)
-
-
-def up_kernel(steps, at, ids, rows, weight, *rest):
+LEAVES = ((1, 3), (3, 1), (2, 2), (0, 0))
+
+
+def up_kernel(turns, at, ids, rows, weight, *rest):
     total = rest[-1]
-    outs = rest[-1 - len(steps) : -1]
-    h, x = at[0], at[1]
-    for k, out in zip(steps, outs):
+    outs = rest[-1 - len(turns) : -1]
+    h, x, c = at[0], at[1], at[2]
+    for turn, out in zip(turns, outs):
+        k = jnp.where(c == 0, LEAVES[turn][0], LEAVES[turn][1])
         target = lax.rem(x + k, NX)
         block_rows = rows[:, target].reshape(NY * GROUP, PIECE)
         total[...] = jnp.dot(block_rows, weight[...], preferred_element_type=F32)
@@ -90,17 +88,19 @@
                 out[y, h, :, s * BLOCK : (s + 1) * BLOCK] = picked.astype(BF16)
 
 
-def up(steps, at, ids, rows, weight, before=()):
+def up(turns, at, ids, rows, weight, before=()):
     shape = jax.ShapeDtypeStruct((NY, ROW // GROUP, GROUP, CAP * BLOCK), BF16)
     return pl.pallas_call(
-        functools.partial(up_kernel, steps),
-        out_shape=[shape] * len(steps),
+        functools.partial(up_kernel, turns),
+        out_shape=[shape] * len(turns),
         in_specs=[SMEM, SMEM, VMEM, VMEM] + [VMEM] * len(before),
-        out_specs=[VMEM] * len(steps),
+        out_specs=[VMEM] * len(turns),
         scratch_shapes=[pltpu.VMEM((NY * GROUP, weight.shape[1]), F32)],
         input_output_aliases={4 + i: i for i in range(len(before))},
         cost_estimate=pl.CostEstimate(
-            flops=2 * len(steps) * NY * GROUP * weight.size, bytes_accessed=0, transcendentals=0
+            flops=2 * len(turns) * NY * GROUP * weight.size,
+            bytes_accessed=0,
+            transcendentals=0,
         ),
         compiler_params=pltpu.CompilerParams(vmem_limit_bytes=24 * 2**20),
         name="up_second" if before else "up_first",
@@ -186,10 +186,8 @@
     )(where, ids, *acts, weight, *before)
 
 
-def turn_pairs(turn):
-    return [
-        (x * NC + c, (x + TURNS[turn][c]) % NX * NC + c) for x in range(NX) for c in range(NC)
-    ]
+def pairs(steps):
+    return [(x * NC + c, (x + steps[c]) % NX * NC + c) for x in range(NX) for c in range(NC)]
 
 
 def body(
@@ -203,18 +201,21 @@
     where = jnp.stack([r, c, x, y]).astype(jnp.int32)
     width = down_bias.shape[0]
 
-    mine, others = jnp.stack([c, x]).astype(jnp.int32), jnp.stack([1 - c, x]).astype(jnp.int32)
-    normed = norm(c.reshape(1), hidden_in, norm_gain, norm_shift)
+    mine = jnp.stack([c, x, c]).astype(jnp.int32)
+    others = jnp.stack([1 - c, x, c]).astype(jnp.int32)
+    scales = jnp.stack([norm_gain, norm_shift]).astype(F32)
+    normed = norm(c.reshape(1), hidden_in, scales)
     own = lax.all_to_all(normed, ("y", "x"), split_axis=0, concat_axis=0, tiled=True)
     other = lax.ppermute(own, "c", around(NC, 1))
     own, other = (v.reshape(NY, NX, GROUP, PIECE) for v in (own, other))
-    first = up(ORDER + (0,), mine, ids, own, up_weight)
-    sums = []
-    for k, before in zip(ORDER + (0,), first):
-        (part,) = up((k,), others, ids, other, up_weight, (before,))
+    first = up((0, 1, 2, 3), mine, ids, own, up_weight)
+    parts = []
+    for turn, before in enumerate(first):
+        (part,) = up((turn,), others, ids, other, up_weight, (before,))
         part = part.reshape(NY, ROW, CAP * BLOCK)
-        sums.append(lax.ppermute(part, "x", around(NX, k)) if k else part)
-    part = sum(v.astype(F32) for v in sums).astype(BF16)
+        leaves = LEAVES[turn]
+        parts.append(lax.ppermute(part, ("x", "c"), pairs(leaves)) if any(leaves) else part)
+    part = sum(v.astype(F32) for v in parts).astype(BF16)
     part = lax.all_to_all(part, "y", split_axis=0, concat_axis=0, tiled=True)
     bias = up_bias.astype(F32).reshape(-1, BLOCK)
     act = activate(where, ids, valid, part, bias)
@@ -222,10 +223,10 @@
     act = lax.all_to_all(act, "y", split_axis=0, concat_axis=0, tiled=True)
     keep, send = down((0,), where, ids, (act,), down_weight)
     for turn in (1, 2):
-        moved = lax.ppermute(act, ("x", "c"), turn_pairs(turn))
+        moved = lax.ppermute(act, ("x", "c"), pairs(TURNS[turn]))
         keep, send = down((turn,), where, ids, (moved,), down_weight, (keep, send))
     got = lax.ppermute(send, "c", around(NC, 1))
-    moved = lax.ppermute(act, ("x", "c"), turn_pairs(3))
+    moved = lax.ppermute(act, ("x", "c"), pairs(TURNS[3]))
     (keep,) = down((3,), where, ids, (moved,), down_weight, (keep,))
     pair = (keep.astype(F32) + got.astype(F32)).astype(BF16).reshape(NZ, 2 * ROW, PIECE)
     pair = lax.all_to_all(pair, "z", split_axis=0, concat_axis=0, tiled=True)

time: 208 us -> 203 us (0.976)
  the two profiles are of different devices: /device:TPU:176 before, /device:TPU:32 now
where the time goes in v5:
time: 203 us; the launch traced here: 202 us
  blocking collectives  83.1 us (41%)
  starting transfers between devices  49.8 us (25%)
  waiting for transfers between devices  41.4 us (20%)
  Pallas kernels  20.9 us (10%)
  other arithmetic  3.35 us (2%)
  local copies, waits for them, and re-layouts  3.07 us (2%)
    all_to_all x1, blocking collectives, body(): pair = lax.all_to_all(pair, 'z', split_axis=0, concat_axis=0, tiled=True)  33.4 us
    all_to_all x1, blocking collectives, body(): lax.all_to_all(normed, ('y', 'x'), split_axis=0, concat_axis=0, tiled=True)  29.2 us
    all_to_all x1, blocking collectives, body(): act = lax.all_to_all(act, 'y', split_axis=0, concat_axis=0, tiled=True)  20.5 us
    all_to_all x1, waiting for transfers between devices, body(): part = lax.all_to_all(part, 'y', split_axis=0, concat_axis=0, tiled=True)  13.4 us
    ppermute x3, waiting for transfers between devices, body(): lax.ppermute(part, ('x', 'c'), pairs(leaves))  13.1 us
    pallas_call x5, Pallas kernels, up(): pl.pallas_call(functools.partial(up_kernel, turns), out_shape=[shape] * l...  9.99 us
    ppermute x3, starting transfers between devices, body(): lax.ppermute(part, ('x', 'c'), pairs(leaves))  9.4 us
    pallas_call x4, Pallas kernels, down(): pl.pallas_call(functools.partial(down_kernel, turns, outs), out_shape=[ja...  9.03 us
  transfers between devices with their start and end apart: 11, of which 7 were waited for; matrix products, arithmetic and copies ran while one was open for 0% of the time, Pallas kernels for 9%

profile of v5, /device:TPU:32, one launch (start us, length us, event | category | flops | bytes accessed | tf_op | source)
XLA Modules:
  0.0 201.8 jit_solution(18271446722730149380)
XLA Ops:
  3.8 29.2 %all_to_all.20 = bf16[32,32,384]{2,1,0:T(8,128)(2,1)S(1)} all-to-all(bf16[32,32,384]{2,1,0:T(8,128)(2,1)S(1)} %norm.1), channel_id=1, replica_groups=mesh['y'=8,'x'=4,'z'=8,'c'=2] {'y','x'}, dimensions={0} | all-to-all | bytes 1572864 | tf_op jit(solution)/shard_map/all_to_all | solution.py:208
  32.9 1.9 collective-permute-start
  35.0 3.2 %up_first.1 = (bf16[8,2,32,512]{3,2,1,0:T(8,128)(2,1)S(1)}, bf16[8,2,32,512]{3,2,1,0:T(8,128)(2,1)S(1)}, bf16[8,2,32,512]{3,2,1,0:T(8,128)(2,1)S(1)}, bf16[8,2,32,512]{3,2,1,0:T(8,128)(2,1)S(1)}) custom-call(s32[3]{0:T(128)S(1)} %get-tuple-element.30.at, s32[64,4]{1,0:T(8,128)S(1)} %bitcast.23, bf16[8,4,32,384]{3,2,1,0:T(8,128)(2,1)S(1)} %bitcast.33, ...), custom_call_target="tpu_custom_call" | custom-call | flops 1207959552 | tf_op jit(solution)/shard_map/up_first/pallas_call | solution.py:93
  39.9 2.4 %collective-permute-start.1 = (bf16[8,64,512]{2,1,0:T(8,128)(2,1)S(1)}, bf16[8,64,512]{2,1,0:T(8,128)(2,1)S(1)}, u32[]{:S(2)}, u32[]{:S(2)}) collective-permute-start(bf16[8,64,512]{2,1,0:T(8,128)(2,1)S(1)} %bitcast.36), channel_id=1, source_target_pairs={{0,16},{1,49},{16,32},{17,1},{32,48},{33,17},{48,0},{49,33},{2,18}... | collective-permute-start | bytes 1572872 | tf_op jit(solution)/shard_map/ppermute | solution.py:217
  44.0 4.7 %collective-permute-start.2 = (bf16[8,64,512]{2,1,0:T(8,128)(2,1)S(1)}, bf16[8,64,512]{2,1,0:T(8,128)(2,1)S(1)}, u32[]{:S(2)}, u32[]{:S(2)}) collective-permute-start(bf16[8,64,512]{2,1,0:T(8,128)(2,1)S(1)} %bitcast.35), channel_id=1, source_target_pairs={{0,48},{1,17},{16,0},{17,33},{32,16},{33,49},{48,32},{49,1},{2,50}... | collective-permute-start | bytes 1572872 | tf_op jit(solution)/shard_map/ppermute | solution.py:217
  50.4 2.3 %collective-permute-start.3 = (bf16[8,64,512]{2,1,0:T(8,128)(2,1)S(1)}, bf16[8,64,512]{2,1,0:T(8,128)(2,1)S(1)}, u32[]{:S(2)}, u32[]{:S(2)}) collective-permute-start(bf16[8,64,512]{2,1,0:T(8,128)(2,1)S(1)} %bitcast.34), channel_id=1, source_target_pairs={{0,32},{1,33},{16,48},{17,49},{32,0},{33,1},{48,16},{49,17},{2,34}... | collective-permute-start | bytes 1572872 | tf_op jit(solution)/shard_map/ppermute | solution.py:217
  54.6 3.6 %collective-permute-done.2 = bf16[8,64,512]{2,1,0:T(8,128)(2,1)S(1)} collective-permute-done((bf16[8,64,512]{2,1,0:T(8,128)(2,1)S(1)}, bf16[8,64,512]{2,1,0:T(8,128)(2,1)S(1)}, u32[]{:S(2)}, u32[]{:S(2)}) %collective-permute-start.2) | collective-permute-done | bytes 524320 | tf_op jit(solution)/shard_map/ppermute | solution.py:217
  58.2 9.4 %collective-permute-done.3 = bf16[8,64,512]{2,1,0:T(8,128)(2,1)S(1)} collective-permute-done((bf16[8,64,512]{2,1,0:T(8,128)(2,1)S(1)}, bf16[8,64,512]{2,1,0:T(8,128)(2,1)S(1)}, u32[]{:S(2)}, u32[]{:S(2)}) %collective-permute-start.3) | collective-permute-done | bytes 524320 | tf_op jit(solution)/shard_map/ppermute | solution.py:217
  68.7 8.3 %all-to-all-start.1 = ((bf16[8,64,512]{2,1,0:T(8,128)(2,1)}), bf16[8,64,512]{2,1,0:T(8,128)(2,1)S(1)}, u32[]{:S(2)}, u32[]{:S(2)}) async-start(bf16[8,64,512]{2,1,0:T(8,128)(2,1)} %fusion), calls=%async_computation.1 | async-start | bytes 1048576 | tf_op jit(solution)/shard_map/all_to_all | solution.py:219
  77.1 13.4 %all-to-all-done.1.parts = bf16[8,64,512]{2,1,0:T(8,128)(2,1)S(1)} async-done(((bf16[8,64,512]{2,1,0:T(8,128)(2,1)}), bf16[8,64,512]{2,1,0:T(8,128)(2,1)S(1)}, u32[]{:S(2)}, u32[]{:S(2)}) %all-to-all-start.1) | async-done | bytes 524320 | tf_op jit(solution)/shard_map/all_to_all | solution.py:219
  91.7 20.5 %all_to_all.21.rest_0_ = bf16[8,64,512]{2,1,0:T(8,128)(2,1)S(1)} all-to-all(bf16[8,64,512]{2,1,0:T(8,128)(2,1)S(1)} %act.1), channel_id=1, replica_groups=mesh['y'=8,'x'=4,'z'=8,'c'=2] {'y'}, dimensions={0} | all-to-all | bytes 1048576 | tf_op jit(solution)/shard_map/all_to_all | solution.py:223
  112.2 1.9 collective-permute-start.6
  114.1 2.7 %collective-permute-start.5 = (bf16[8,64,512]{2,1,0:T(8,128)(2,1)S(1)}, bf16[8,64,512]{2,1,0:T(8,128)(2,1)S(1)}, u32[]{:S(2)}, u32[]{:S(2)}) collective-permute-start(bf16[8,64,512]{2,1,0:T(8,128)(2,1)S(1)} %all_to_all.21.rest_0_), channel_id=1, source_target_pairs={{0,32},{1,49},{16,48},{17,1},{32,0},{33,17},{48,16},{49,33},{2,34}... | collective-permute-start | bytes 1572872 | tf_op jit(solution)/shard_map/ppermute | solution.py:226
  116.8 3.3 %collective-permute-start.4 = (bf16[8,64,512]{2,1,0:T(8,128)(2,1)S(1)}, bf16[8,64,512]{2,1,0:T(8,128)(2,1)S(1)}, u32[]{:S(2)}, u32[]{:S(2)}) collective-permute-start(bf16[8,64,512]{2,1,0:T(8,128)(2,1)S(1)} %all_to_all.21.rest_0_), channel_id=1, source_target_pairs={{0,16},{1,33},{16,32},{17,49},{32,48},{33,1},{48,0},{49,17},{2,18}... | collective-permute-start | bytes 1572872 | tf_op jit(solution)/shard_map/ppermute | solution.py:229
  120.1 2.3 %down.4 = (bf16[8,2,64,384]{3,2,1,0:T(8,128)(2,1)S(1)}, bf16[8,2,64,384]{3,2,1,0:T(8,128)(2,1)S(1)}) custom-call(s32[4]{0:T(128)S(1)} %pad_add_fusion.where, s32[64,4]{1,0:T(8,128)S(1)} %bitcast.29, bf16[8,64,512]{2,1,0:T(8,128)(2,1)S(1)} %all_to_all.21.rest_0_, bf16[1536,384]{1,0:T(8,128)(2,1)S(1)} %copy-done.1), custom_call_target="tpu_custom_call" | custom-call | flops 603979776 | tf_op jit(solution)/shard_map/down/pallas_call | solution.py:172
  122.4 6.4 %collective-permute-done.6.rest_0_ = bf16[8,64,512]{2,1,0:T(8,128)(2,1)S(1)} collective-permute-done((bf16[8,64,512]{2,1,0:T(8,128)(2,1)S(1)}, bf16[8,64,512]{2,1,0:T(8,128)(2,1)S(1)}, u32[]{:S(2)}, u32[]{:S(2)}) %collective-permute-start.6) | collective-permute-done | bytes 524320 | tf_op jit(solution)/shard_map/ppermute | solution.py:226
  128.9 2.2 %down.5 = (bf16[8,2,64,384]{3,2,1,0:T(8,128)(2,1)S(1)}, bf16[8,2,64,384]{3,2,1,0:T(8,128)(2,1)S(1)}) custom-call(s32[4]{0:T(128)S(1)} %pad_add_fusion.where, s32[64,4]{1,0:T(8,128)S(1)} %bitcast.30, bf16[8,64,512]{2,1,0:T(8,128)(2,1)S(1)} %collective-permute-done.6.rest_0_, ...), custom_call_target="tpu_custom_call", output_to_operand_aliasing={{0}: (4, {}), {1}: (5, {})} | custom-call | flops 603979776 | tf_op jit(solution)/shard_map/down/pallas_call | solution.py:172
  131.1 2.3 %down.6 = (bf16[8,2,64,384]{3,2,1,0:T(8,128)(2,1)S(1)}, bf16[8,2,64,384]{3,2,1,0:T(8,128)(2,1)S(1)}) custom-call(s32[4]{0:T(128)S(1)} %pad_add_fusion.where, s32[64,4]{1,0:T(8,128)S(1)} %bitcast.31, bf16[8,64,512]{2,1,0:T(8,128)(2,1)S(1)} %collective-permute-done.5.rest_0_, ...), custom_call_target="tpu_custom_call", output_to_operand_aliasing={{0}: (4, {}), {1}: (5, {})} | custom-call | flops 603979776 | tf_op jit(solution)/shard_map/down/pallas_call | solution.py:172
  133.4 8.2 %collective-permute-start.7 = (bf16[8,2,64,384]{3,2,1,0:T(8,128)(2,1)S(1)}, bf16[8,2,64,384]{3,2,1,0:T(8,128)(2,1)S(1)}, u32[]{:S(2)}, u32[]{:S(2)}) collective-permute-start(bf16[8,2,64,384]{3,2,1,0:T(8,128)(2,1)S(1)} %get-tuple-element.24), channel_id=1, source_target_pairs={{0,1},{1,0},{2,3},{3,2},{4,5},{5,4},{6,7},{7,6},{8,9},{9,8},{10,11... | collective-permute-start | bytes 2359304 | tf_op jit(solution)/shard_map/ppermute | solution.py:228
  141.6 2.2 %down.7 = bf16[8,2,64,384]{3,2,1,0:T(8,128)(2,1)S(1)} custom-call(s32[4]{0:T(128)S(1)} %pad_add_fusion.where, s32[64,4]{1,0:T(8,128)S(1)} %bitcast.32, bf16[8,64,512]{2,1,0:T(8,128)(2,1)S(1)} %collective-permute-done.4.rest_0_, bf16[1536,384]{1,0:T(8,128)(2,1)S(1)} %copy-done.1, ...), custom_call_target="tpu_custom_call", output_to_operand_aliasing={{}: (4, {})} | custom-call | flops 19327352832 | tf_op jit(solution)/shard_map/down/pallas_call | solution.py:172
  144.1 33.4 %all_to_all.22 = bf16[8,128,384]{2,1,0:T(8,128)(2,1)S(1)} all-to-all(bf16[8,128,384]{2,1,0:T(8,128)(2,1)S(1)} %bitcast.38), channel_id=1, replica_groups=mesh['y'=8,'x'=4,'z'=8,'c'=2] {'z'}, dimensions={0} | all-to-all | bytes 1572864 | tf_op jit(solution)/shard_map/all_to_all | solution.py:232
  177.6 7.8 %collective-permute-start.8 = (bf16[64,384]{1,0:T(8,128)(2,1)S(1)}, bf16[64,384]{1,0:T(8,128)(2,1)S(1)}, u32[]{:S(2)}, u32[]{:S(2)}) collective-permute-start(bf16[64,384]{1,0:T(8,128)(2,1)S(1)} %get-tuple-element.27), channel_id=1, source_target_pairs={{0,48},{1,16},{2,112},{3,80},{4,176},{5,144},{6,240},{7,208},{8,30... | collective-permute-start | bytes 147464 | tf_op jit(solution)/shard_map/ppermute | solution.py:241
  185.4 6.3 %collective-permute-start.9 = (bf16[64,384]{1,0:T(8,128)(2,1)S(1)}, bf16[64,384]{1,0:T(8,128)(2,1)S(1)}, u32[]{:S(2)}, u32[]{:S(2)}) collective-permute-start(bf16[64,384]{1,0:T(8,128)(2,1)S(1)} %get-tuple-element.28), channel_id=1, source_target_pairs={{0,0},{1,32},{2,64},{3,96},{4,128},{5,160},{6,192},{7,224},{8,256}... | collective-permute-start | bytes 147464 | tf_op jit(solution)/shard_map/ppermute | solution.py:240
  193.2 7.0 %collective-permute-done.9 = bf16[64,384]{1,0:T(8,128)(2,1)S(1)} collective-permute-done((bf16[64,384]{1,0:T(8,128)(2,1)S(1)}, bf16[64,384]{1,0:T(8,128)(2,1)S(1)}, u32[]{:S(2)}, u32[]{:S(2)}) %collective-permute-start.9) | collective-permute-done | bytes 49184 | tf_op jit(solution)/shard_map/ppermute | solution.py:240
  (40 shorter events, 16.6 us)
Async XLA Ops:
  1.7 1.4 copy-start.2
  3.1 31.8 %copy-start.5 = (s32[64,1,4]{0,2,1:T(4,128)S(1)}, s32[64,1,4]{0,2,1:T(4,128)}, u32[]{:S(2)}) copy-start(s32[64,1,4]{0,2,1:T(4,128)} %param.16) | copy-start | bytes 3076
  3.1 32.0 %copy-start = (bf16[384,1536]{1,0:T(8,128)(2,1)S(1)}, bf16[384,1536]{1,0:T(8,128)(2,1)}, u32[]{:S(2)}) copy-start(bf16[384,1536]{1,0:T(8,128)(2,1)} %weight.9) | copy-start | bytes 3538948
  32.9 5.3 %collective-permute-start = (bf16[32,32,384]{2,1,0:T(8,128)(2,1)S(1)}, bf16[32,32,384]{2,1,0:T(8,128)(2,1)S(1)}, u32[]{:S(2)}, u32[]{:S(2)}) collective-permute-start(bf16[32,32,384]{2,1,0:T(8,128)(2,1)S(1)} %all_to_all.20), channel_id=1, source_target_pairs={{0,1},{1,0},{2,3},{3,2},{4,5},{5,4},{6,7},{7,6},{8,9},{9,8},{10,11... | collective-permute-start | bytes 2359304 | tf_op jit(solution)/shard_map/ppermute | solution.py:209
  39.9 14.7 %collective-permute-start.1 = (bf16[8,64,512]{2,1,0:T(8,128)(2,1)S(1)}, bf16[8,64,512]{2,1,0:T(8,128)(2,1)S(1)}, u32[]{:S(2)}, u32[]{:S(2)}) collective-permute-start(bf16[8,64,512]{2,1,0:T(8,128)(2,1)S(1)} %bitcast.36), channel_id=1, source_target_pairs={{0,16},{1,49},{16,32},{17,1},{32,48},{33,17},{48,0},{49,33},{2,18}... | collective-permute-start | bytes 1572872 | tf_op jit(solution)/shard_map/ppermute | solution.py:217
  44.0 14.2 %collective-permute-start.2 = (bf16[8,64,512]{2,1,0:T(8,128)(2,1)S(1)}, bf16[8,64,512]{2,1,0:T(8,128)(2,1)S(1)}, u32[]{:S(2)}, u32[]{:S(2)}) collective-permute-start(bf16[8,64,512]{2,1,0:T(8,128)(2,1)S(1)} %bitcast.35), channel_id=1, source_target_pairs={{0,48},{1,17},{16,0},{17,33},{32,16},{33,49},{48,32},{49,1},{2,50}... | collective-permute-start | bytes 1572872 | tf_op jit(solution)/shard_map/ppermute | solution.py:217
  50.4 17.2 %collective-permute-start.3 = (bf16[8,64,512]{2,1,0:T(8,128)(2,1)S(1)}, bf16[8,64,512]{2,1,0:T(8,128)(2,1)S(1)}, u32[]{:S(2)}, u32[]{:S(2)}) collective-permute-start(bf16[8,64,512]{2,1,0:T(8,128)(2,1)S(1)} %bitcast.34), channel_id=1, source_target_pairs={{0,32},{1,33},{16,48},{17,49},{32,0},{33,1},{48,16},{49,17},{2,34}... | collective-permute-start | bytes 1572872 | tf_op jit(solution)/shard_map/ppermute | solution.py:217
  54.5 22.6 %copy-start.4 = (bf16[1536]{0:T(1024)(128)(2,1)S(1)}, bf16[1536]{0:T(1024)(128)(2,1)}, u32[]{:S(2)}) copy-start(bf16[1536]{0:T(1024)(128)(2,1)} %param.13) | copy-start | bytes 9220
  54.5 36.0 %copy-start.3 = (s32[64,1]{0,1:T(1,128)S(1)}, s32[64,1]{0,1:T(1,128)}, u32[]{:S(2)}) copy-start(s32[64,1]{0,1:T(1,128)} %param.17) | copy-start | bytes 772
  68.7 51.4 %copy-start.1 = (bf16[1536,384]{1,0:T(8,128)(2,1)S(1)}, bf16[1536,384]{1,0:T(8,128)(2,1)}, u32[]{:S(2)}) copy-start(bf16[1536,384]{1,0:T(8,128)(2,1)} %rest_1_.7) | copy-start | bytes 3538948
  68.7 21.8 %all-to-all-start.1 = ((bf16[8,64,512]{2,1,0:T(8,128)(2,1)}), bf16[8,64,512]{2,1,0:T(8,128)(2,1)S(1)}, u32[]{:S(2)}, u32[]{:S(2)}) async-start(bf16[8,64,512]{2,1,0:T(8,128)(2,1)} %fusion), calls=%async_computation.1 | async-start | bytes 1048576 | tf_op jit(solution)/shard_map/all_to_all | solution.py:219
  112.2 16.7 %collective-permute-start.6 = (bf16[8,64,512]{2,1,0:T(8,128)(2,1)S(1)}, bf16[8,64,512]{2,1,0:T(8,128)(2,1)S(1)}, u32[]{:S(2)}, u32[]{:S(2)}) collective-permute-start(bf16[8,64,512]{2,1,0:T(8,128)(2,1)S(1)} %all_to_all.21.rest_0_), channel_id=1, source_target_pairs={{0,48},{1,17},{16,0},{17,33},{32,16},{33,49},{48,32},{49,1},{2,50}... | collective-permute-start | bytes 1572872 | tf_op jit(solution)/shard_map/ppermute | solution.py:226
  114.1 17.0 %collective-permute-start.5 = (bf16[8,64,512]{2,1,0:T(8,128)(2,1)S(1)}, bf16[8,64,512]{2,1,0:T(8,128)(2,1)S(1)}, u32[]{:S(2)}, u32[]{:S(2)}) collective-permute-start(bf16[8,64,512]{2,1,0:T(8,128)(2,1)S(1)} %all_to_all.21.rest_0_), channel_id=1, source_target_pairs={{0,32},{1,49},{16,48},{17,1},{32,0},{33,17},{48,16},{49,33},{2,34}... | collective-permute-start | bytes 1572872 | tf_op jit(solution)/shard_map/ppermute | solution.py:226
  116.8 24.8 %collective-permute-start.4 = (bf16[8,64,512]{2,1,0:T(8,128)(2,1)S(1)}, bf16[8,64,512]{2,1,0:T(8,128)(2,1)S(1)}, u32[]{:S(2)}, u32[]{:S(2)}) collective-permute-start(bf16[8,64,512]{2,1,0:T(8,128)(2,1)S(1)} %all_to_all.21.rest_0_), channel_id=1, source_target_pairs={{0,16},{1,33},{16,32},{17,49},{32,48},{33,1},{48,0},{49,17},{2,18}... | collective-permute-start | bytes 1572872 | tf_op jit(solution)/shard_map/ppermute | solution.py:229
  133.4 10.4 %collective-permute-start.7 = (bf16[8,2,64,384]{3,2,1,0:T(8,128)(2,1)S(1)}, bf16[8,2,64,384]{3,2,1,0:T(8,128)(2,1)S(1)}, u32[]{:S(2)}, u32[]{:S(2)}) collective-permute-start(bf16[8,2,64,384]{3,2,1,0:T(8,128)(2,1)S(1)} %get-tuple-element.24), channel_id=1, source_target_pairs={{0,1},{1,0},{2,3},{3,2},{4,5},{5,4},{6,7},{7,6},{8,9},{9,8},{10,11... | collective-permute-start | bytes 2359304 | tf_op jit(solution)/shard_map/ppermute | solution.py:228
  144.1 47.7 %copy-start.6 = (bf16[768]{0:T(1024)(128)(2,1)S(1)}, bf16[768]{0:T(1024)(128)(2,1)}, u32[]{:S(2)}) copy-start(bf16[768]{0:T(1024)(128)(2,1)} %param.15) | copy-start | bytes 4612
  177.6 15.6 %collective-permute-start.8 = (bf16[64,384]{1,0:T(8,128)(2,1)S(1)}, bf16[64,384]{1,0:T(8,128)(2,1)S(1)}, u32[]{:S(2)}, u32[]{:S(2)}) collective-permute-start(bf16[64,384]{1,0:T(8,128)(2,1)S(1)} %get-tuple-element.27), channel_id=1, source_target_pairs={{0,48},{1,16},{2,112},{3,80},{4,176},{5,144},{6,240},{7,208},{8,30... | collective-permute-start | bytes 147464 | tf_op jit(solution)/shard_map/ppermute | solution.py:241
  185.4 14.8 %collective-permute-start.9 = (bf16[64,384]{1,0:T(8,128)(2,1)S(1)}, bf16[64,384]{1,0:T(8,128)(2,1)S(1)}, u32[]{:S(2)}, u32[]{:S(2)}) collective-permute-start(bf16[64,384]{1,0:T(8,128)(2,1)S(1)} %get-tuple-element.28), channel_id=1, source_target_pairs={{0,0},{1,32},{2,64},{3,96},{4,128},{5,160},{6,192},{7,224},{8,256}... | collective-permute-start | bytes 147464 | tf_op jit(solution)/shard_map/ppermute | solution.py:240

commit v6 on v5

--- a/solution.py
+++ b/solution.py
@@ -68,7 +68,7 @@
 
 SMEM = pl.BlockSpec(memory_space=pltpu.SMEM)
 VMEM = pl.BlockSpec(memory_space=pltpu.VMEM)
-LEAVES = ((1, 3), (3, 1), (2, 2), (0, 0))
+LEAVES = ((2, 2), (3, 1), (1, 3), (0, 0))
 
 
 def up_kernel(turns, at, ids, rows, weight, *rest):
@@ -212,10 +212,12 @@
     parts = []
     for turn, before in enumerate(first):
         (part,) = up((turn,), others, ids, other, up_weight, (before,))
-        part = part.reshape(NY, ROW, CAP * BLOCK)
-        leaves = LEAVES[turn]
-        parts.append(lax.ppermute(part, ("x", "c"), pairs(leaves)) if any(leaves) else part)
-    part = sum(v.astype(F32) for v in parts).astype(BF16)
+        parts.append(part.reshape(NY, ROW, CAP * BLOCK))
+    passed = lax.ppermute(parts[0], ("x", "c"), pairs(LEAVES[2]))
+    direct = lax.ppermute(parts[1], ("x", "c"), pairs(LEAVES[1]))
+    joined = (parts[2].astype(F32) + passed.astype(F32)).astype(BF16)
+    joined = lax.ppermute(joined, ("x", "c"), pairs(LEAVES[2]))
+    part = (parts[3].astype(F32) + direct.astype(F32) + joined.astype(F32)).astype(BF16)
     part = lax.all_to_all(part, "y", split_axis=0, concat_axis=0, tiled=True)
     bias = up_bias.astype(F32).reshape(-1, BLOCK)
     act = activate(where, ids, valid, part, bias)

time: 203 us -> 200 us (0.985)
  the two profiles are of different devices: /device:TPU:32 before, /device:TPU:176 now
where the time goes in v6:
time: 200 us; the launch traced here: 199 us
  blocking collectives  74.3 us (37%)
  starting transfers between devices  54.2 us (27%)
  waiting for transfers between devices  42.9 us (21%)
  Pallas kernels  20.9 us (10%)
  other arithmetic  3.45 us (2%)
  local copies, waits for them, and re-layouts  3.07 us (2%)
    all_to_all x1, blocking collectives, body(): pair = lax.all_to_all(pair, 'z', split_axis=0, concat_axis=0, tiled=True)  29.6 us
    all_to_all x1, blocking collectives, body(): lax.all_to_all(normed, ('y', 'x'), split_axis=0, concat_axis=0, tiled=True)  29.1 us
    ppermute x2, waiting for transfers between devices, body(): moved = lax.ppermute(act, ('x', 'c'), pairs(TURNS[turn]))  15.9 us
    all_to_all x1, blocking collectives, body(): act = lax.all_to_all(act, 'y', split_axis=0, concat_axis=0, tiled=True)  15.7 us
    ppermute x2, starting transfers between devices, body(): moved = lax.ppermute(act, ('x', 'c'), pairs(TURNS[turn]))  11.9 us
    ppermute x1, starting transfers between devices, body(): second = lax.ppermute(branch[ROW:], ALL, back[1])  11 us
    pallas_call x5, Pallas kernels, up(): pl.pallas_call(functools.partial(up_kernel, turns), out_shape=[shape] * l...  9.97 us
    all_to_all x1, waiting for transfers between devices, body(): part = lax.all_to_all(part, 'y', split_axis=0, concat_axis=0, tiled=True)  9.92 us
  transfers between devices with their start and end apart: 11, of which 5 were waited for; matrix products, arithmetic and copies ran while one was open for 0% of the time, Pallas kernels for 9%

profile of v6, /device:TPU:176, one launch (start us, length us, event | category | flops | bytes accessed | tf_op | source)
XLA Modules:
  0.0 199.1 jit_solution(204762935014905973)
XLA Ops:
  3.8 29.1 %all_to_all.20 = bf16[32,32,384]{2,1,0:T(8,128)(2,1)S(1)} all-to-all(bf16[32,32,384]{2,1,0:T(8,128)(2,1)S(1)} %norm.1), channel_id=1, replica_groups=mesh['y'=8,'x'=4,'z'=8,'c'=2] {'y','x'}, dimensions={0} | all-to-all | bytes 1572864 | tf_op jit(solution)/shard_map/all_to_all | solution.py:208
  32.9 1.9 collective-permute-start
  35.0 3.1 %up_first.1 = (bf16[8,2,32,512]{3,2,1,0:T(8,128)(2,1)S(1)}, bf16[8,2,32,512]{3,2,1,0:T(8,128)(2,1)S(1)}, bf16[8,2,32,512]{3,2,1,0:T(8,128)(2,1)S(1)}, bf16[8,2,32,512]{3,2,1,0:T(8,128)(2,1)S(1)}) custom-call(s32[3]{0:T(128)S(1)} %get-tuple-element.30.at, s32[64,4]{1,0:T(8,128)S(1)} %bitcast.25, bf16[8,4,32,384]{3,2,1,0:T(8,128)(2,1)S(1)} %bitcast.35, ...), custom_call_target="tpu_custom_call" | custom-call | flops 1207959552 | tf_op jit(solution)/shard_map/up_first/pallas_call | solution.py:93
  39.9 3.1 %collective-permute-start.2 = (bf16[8,64,512]{2,1,0:T(8,128)(2,1)S(1)}, bf16[8,64,512]{2,1,0:T(8,128)(2,1)S(1)}, u32[]{:S(2)}, u32[]{:S(2)}) collective-permute-start(bf16[8,64,512]{2,1,0:T(8,128)(2,1)S(1)} %bitcast.37), channel_id=1, source_target_pairs={{0,16},{1,49},{16,32},{17,1},{32,48},{33,17},{48,0},{49,33},{2,18}... | collective-permute-start | bytes 1572872 | tf_op jit(solution)/shard_map/ppermute | solution.py:216
  44.7 3.9 %collective-permute-start.1 = (bf16[8,64,512]{2,1,0:T(8,128)(2,1)S(1)}, bf16[8,64,512]{2,1,0:T(8,128)(2,1)S(1)}, u32[]{:S(2)}, u32[]{:S(2)}) collective-permute-start(bf16[8,64,512]{2,1,0:T(8,128)(2,1)S(1)} %bitcast.36), channel_id=1, source_target_pairs={{0,48},{1,17},{16,0},{17,33},{32,16},{33,49},{48,32},{49,1},{2,50}... | collective-permute-start | bytes 1572872 | tf_op jit(solution)/shard_map/ppermute | solution.py:217
  50.3 2.0 %collective-permute-done.2 = bf16[8,64,512]{2,1,0:T(8,128)(2,1)S(1)} collective-permute-done((bf16[8,64,512]{2,1,0:T(8,128)(2,1)S(1)}, bf16[8,64,512]{2,1,0:T(8,128)(2,1)S(1)}, u32[]{:S(2)}, u32[]{:S(2)}) %collective-permute-start.2) | collective-permute-done | bytes 524320 | tf_op jit(solution)/shard_map/ppermute | solution.py:216
  52.6 2.8 %collective-permute-start.3 = (bf16[8,64,512]{2,1,0:T(8,128)(2,1)S(1)}, bf16[8,64,512]{2,1,0:T(8,128)(2,1)S(1)}, u32[]{:S(2)}, u32[]{:S(2)}) collective-permute-start(bf16[8,64,512]{2,1,0:T(8,128)(2,1)S(1)} %fusion), channel_id=1, source_target_pairs={{0,16},{1,49},{16,32},{17,1},{32,48},{33,17},{48,0},{49,33},{2,18}... | collective-permute-start | bytes 1572872 | tf_op jit(solution)/shard_map/ppermute | solution.py:219
  57.1 7.7 %collective-permute-done.3 = bf16[8,64,512]{2,1,0:T(8,128)(2,1)S(1)} collective-permute-done((bf16[8,64,512]{2,1,0:T(8,128)(2,1)S(1)}, bf16[8,64,512]{2,1,0:T(8,128)(2,1)S(1)}, u32[]{:S(2)}, u32[]{:S(2)}) %collective-permute-start.3) | collective-permute-done | bytes 524320 | tf_op jit(solution)/shard_map/ppermute | solution.py:219
  65.9 9.3 %all-to-all-start.1 = ((bf16[8,64,512]{2,1,0:T(8,128)(2,1)}), bf16[8,64,512]{2,1,0:T(8,128)(2,1)S(1)}, u32[]{:S(2)}, u32[]{:S(2)}) async-start(bf16[8,64,512]{2,1,0:T(8,128)(2,1)} %fusion.2), calls=%async_computation.1 | async-start | bytes 1048576 | tf_op jit(solution)/shard_map/all_to_all | solution.py:221
  75.3 9.9 %all-to-all-done.1.parts = bf16[8,64,512]{2,1,0:T(8,128)(2,1)S(1)} async-done(((bf16[8,64,512]{2,1,0:T(8,128)(2,1)}), bf16[8,64,512]{2,1,0:T(8,128)(2,1)S(1)}, u32[]{:S(2)}, u32[]{:S(2)}) %all-to-all-start.1) | async-done | bytes 524320 | tf_op jit(solution)/shard_map/all_to_all | solution.py:221
  86.4 15.7 %all_to_all.21.rest_0_ = bf16[8,64,512]{2,1,0:T(8,128)(2,1)S(1)} all-to-all(bf16[8,64,512]{2,1,0:T(8,128)(2,1)S(1)} %act.1), channel_id=1, replica_groups=mesh['y'=8,'x'=4,'z'=8,'c'=2] {'y'}, dimensions={0} | all-to-all | bytes 1048576 | tf_op jit(solution)/shard_map/all_to_all | solution.py:225
  102.1 10.0 %collective-permute-start.6 = (bf16[8,64,512]{2,1,0:T(8,128)(2,1)S(1)}, bf16[8,64,512]{2,1,0:T(8,128)(2,1)S(1)}, u32[]{:S(2)}, u32[]{:S(2)}) collective-permute-start(bf16[8,64,512]{2,1,0:T(8,128)(2,1)S(1)} %all_to_all.21.rest_0_), channel_id=1, source_target_pairs={{0,48},{1,17},{16,0},{17,33},{32,16},{33,49},{48,32},{49,1},{2,50}... | collective-permute-start | bytes 1572872 | tf_op jit(solution)/shard_map/ppermute | solution.py:228
  112.1 1.9 collective-permute-start.5
  114.0 2.8 %collective-permute-start.4 = (bf16[8,64,512]{2,1,0:T(8,128)(2,1)S(1)}, bf16[8,64,512]{2,1,0:T(8,128)(2,1)S(1)}, u32[]{:S(2)}, u32[]{:S(2)}) collective-permute-start(bf16[8,64,512]{2,1,0:T(8,128)(2,1)S(1)} %all_to_all.21.rest_0_), channel_id=1, source_target_pairs={{0,16},{1,33},{16,32},{17,49},{32,48},{33,1},{48,0},{49,17},{2,18}... | collective-permute-start | bytes 1572872 | tf_op jit(solution)/shard_map/ppermute | solution.py:231
  116.8 2.3 %down.4 = (bf16[8,2,64,384]{3,2,1,0:T(8,128)(2,1)S(1)}, bf16[8,2,64,384]{3,2,1,0:T(8,128)(2,1)S(1)}) custom-call(s32[4]{0:T(128)S(1)} %pad_add_fusion.where, s32[64,4]{1,0:T(8,128)S(1)} %bitcast.31, bf16[8,64,512]{2,1,0:T(8,128)(2,1)S(1)} %all_to_all.21.rest_0_, bf16[1536,384]{1,0:T(8,128)(2,1)S(1)} %copy-done.1), custom_call_target="tpu_custom_call" | custom-call | flops 603979776 | tf_op jit(solution)/shard_map/down/pallas_call | solution.py:172
  119.0 15.9 %collective-permute-done.6.rest_0_ = bf16[8,64,512]{2,1,0:T(8,128)(2,1)S(1)} collective-permute-done((bf16[8,64,512]{2,1,0:T(8,128)(2,1)S(1)}, bf16[8,64,512]{2,1,0:T(8,128)(2,1)S(1)}, u32[]{:S(2)}, u32[]{:S(2)}) %collective-permute-start.6) | collective-permute-done | bytes 524320 | tf_op jit(solution)/shard_map/ppermute | solution.py:228
  134.9 2.2 %down.5 = (bf16[8,2,64,384]{3,2,1,0:T(8,128)(2,1)S(1)}, bf16[8,2,64,384]{3,2,1,0:T(8,128)(2,1)S(1)}) custom-call(s32[4]{0:T(128)S(1)} %pad_add_fusion.where, s32[64,4]{1,0:T(8,128)S(1)} %bitcast.32, bf16[8,64,512]{2,1,0:T(8,128)(2,1)S(1)} %collective-permute-done.6.rest_0_, ...), custom_call_target="tpu_custom_call", output_to_operand_aliasing={{0}: (4, {}), {1}: (5, {})} | custom-call | flops 603979776 | tf_op jit(solution)/shard_map/down/pallas_call | solution.py:172
  137.2 2.3 %down.6 = (bf16[8,2,64,384]{3,2,1,0:T(8,128)(2,1)S(1)}, bf16[8,2,64,384]{3,2,1,0:T(8,128)(2,1)S(1)}) custom-call(s32[4]{0:T(128)S(1)} %pad_add_fusion.where, s32[64,4]{1,0:T(8,128)S(1)} %bitcast.33, bf16[8,64,512]{2,1,0:T(8,128)(2,1)S(1)} %collective-permute-done.5.rest_0_, ...), custom_call_target="tpu_custom_call", output_to_operand_aliasing={{0}: (4, {}), {1}: (5, {})} | custom-call | flops 603979776 | tf_op jit(solution)/shard_map/down/pallas_call | solution.py:172
  139.5 1.9 collective-permute-start.7
  141.4 2.2 %down.7 = bf16[8,2,64,384]{3,2,1,0:T(8,128)(2,1)S(1)} custom-call(s32[4]{0:T(128)S(1)} %pad_add_fusion.where, s32[64,4]{1,0:T(8,128)S(1)} %bitcast.34, bf16[8,64,512]{2,1,0:T(8,128)(2,1)S(1)} %collective-permute-done.4.rest_0_, bf16[1536,384]{1,0:T(8,128)(2,1)S(1)} %copy-done.1, ...), custom_call_target="tpu_custom_call", output_to_operand_aliasing={{}: (4, {})} | custom-call | flops 19327352832 | tf_op jit(solution)/shard_map/down/pallas_call | solution.py:172
  143.9 29.6 %all_to_all.22 = bf16[8,128,384]{2,1,0:T(8,128)(2,1)S(1)} all-to-all(bf16[8,128,384]{2,1,0:T(8,128)(2,1)S(1)} %bitcast.39), channel_id=1, replica_groups=mesh['y'=8,'x'=4,'z'=8,'c'=2] {'z'}, dimensions={0} | all-to-all | bytes 1572864 | tf_op jit(solution)/shard_map/all_to_all | solution.py:234
  173.6 11.0 %collective-permute-start.8 = (bf16[64,384]{1,0:T(8,128)(2,1)S(1)}, bf16[64,384]{1,0:T(8,128)(2,1)S(1)}, u32[]{:S(2)}, u32[]{:S(2)}) collective-permute-start(bf16[64,384]{1,0:T(8,128)(2,1)S(1)} %get-tuple-element.27), channel_id=1, source_target_pairs={{0,48},{1,16},{2,112},{3,80},{4,176},{5,144},{6,240},{7,208},{8,30... | collective-permute-start | bytes 147464 | tf_op jit(solution)/shard_map/ppermute | solution.py:243
  184.6 5.6 %collective-permute-start.9 = (bf16[64,384]{1,0:T(8,128)(2,1)S(1)}, bf16[64,384]{1,0:T(8,128)(2,1)S(1)}, u32[]{:S(2)}, u32[]{:S(2)}) collective-permute-start(bf16[64,384]{1,0:T(8,128)(2,1)S(1)} %get-tuple-element.28), channel_id=1, source_target_pairs={{0,0},{1,32},{2,64},{3,96},{4,128},{5,160},{6,192},{7,224},{8,256}... | collective-permute-start | bytes 147464 | tf_op jit(solution)/shard_map/ppermute | solution.py:242
  190.3 7.3 %collective-permute-done.9 = bf16[64,384]{1,0:T(8,128)(2,1)S(1)} collective-permute-done((bf16[64,384]{1,0:T(8,128)(2,1)S(1)}, bf16[64,384]{1,0:T(8,128)(2,1)S(1)}, u32[]{:S(2)}, u32[]{:S(2)}) %collective-permute-start.9) | collective-permute-done | bytes 49184 | tf_op jit(solution)/shard_map/ppermute | solution.py:242
  (41 shorter events, 15.2 us)
Async XLA Ops:
  1.7 1.4 copy-start.2
  3.1 31.7 %copy-start.5 = (s32[64,1,4]{0,2,1:T(4,128)S(1)}, s32[64,1,4]{0,2,1:T(4,128)}, u32[]{:S(2)}) copy-start(s32[64,1,4]{0,2,1:T(4,128)} %param.16) | copy-start | bytes 3076
  3.1 31.9 %copy-start = (bf16[384,1536]{1,0:T(8,128)(2,1)S(1)}, bf16[384,1536]{1,0:T(8,128)(2,1)}, u32[]{:S(2)}) copy-start(bf16[384,1536]{1,0:T(8,128)(2,1)} %weight.9) | copy-start | bytes 3538948
  32.9 5.3 %collective-permute-start = (bf16[32,32,384]{2,1,0:T(8,128)(2,1)S(1)}, bf16[32,32,384]{2,1,0:T(8,128)(2,1)S(1)}, u32[]{:S(2)}, u32[]{:S(2)}) collective-permute-start(bf16[32,32,384]{2,1,0:T(8,128)(2,1)S(1)} %all_to_all.20), channel_id=1, source_target_pairs={{0,1},{1,0},{2,3},{3,2},{4,5},{5,4},{6,7},{7,6},{8,9},{9,8},{10,11... | collective-permute-start | bytes 2359304 | tf_op jit(solution)/shard_map/ppermute | solution.py:209
  39.9 12.5 %collective-permute-start.2 = (bf16[8,64,512]{2,1,0:T(8,128)(2,1)S(1)}, bf16[8,64,512]{2,1,0:T(8,128)(2,1)S(1)}, u32[]{:S(2)}, u32[]{:S(2)}) collective-permute-start(bf16[8,64,512]{2,1,0:T(8,128)(2,1)S(1)} %bitcast.37), channel_id=1, source_target_pairs={{0,16},{1,49},{16,32},{17,1},{32,48},{33,17},{48,0},{49,33},{2,18}... | collective-permute-start | bytes 1572872 | tf_op jit(solution)/shard_map/ppermute | solution.py:216
  44.7 12.4 %collective-permute-start.1 = (bf16[8,64,512]{2,1,0:T(8,128)(2,1)S(1)}, bf16[8,64,512]{2,1,0:T(8,128)(2,1)S(1)}, u32[]{:S(2)}, u32[]{:S(2)}) collective-permute-start(bf16[8,64,512]{2,1,0:T(8,128)(2,1)S(1)} %bitcast.36), channel_id=1, source_target_pairs={{0,48},{1,17},{16,0},{17,33},{32,16},{33,49},{48,32},{49,1},{2,50}... | collective-permute-start | bytes 1572872 | tf_op jit(solution)/shard_map/ppermute | solution.py:217
  52.6 12.3 %collective-permute-start.3 = (bf16[8,64,512]{2,1,0:T(8,128)(2,1)S(1)}, bf16[8,64,512]{2,1,0:T(8,128)(2,1)S(1)}, u32[]{:S(2)}, u32[]{:S(2)}) collective-permute-start(bf16[8,64,512]{2,1,0:T(8,128)(2,1)S(1)} %fusion), channel_id=1, source_target_pairs={{0,16},{1,49},{16,32},{17,1},{32,48},{33,17},{48,0},{49,33},{2,18}... | collective-permute-start | bytes 1572872 | tf_op jit(solution)/shard_map/ppermute | solution.py:219
  57.1 18.2 %copy-start.4 = (bf16[1536]{0:T(1024)(128)(2,1)S(1)}, bf16[1536]{0:T(1024)(128)(2,1)}, u32[]{:S(2)}) copy-start(bf16[1536]{0:T(1024)(128)(2,1)} %param.13) | copy-start | bytes 9220
  57.1 28.1 %copy-start.3 = (s32[64,1]{0,1:T(1,128)S(1)}, s32[64,1]{0,1:T(1,128)}, u32[]{:S(2)}) copy-start(s32[64,1]{0,1:T(1,128)} %param.17) | copy-start | bytes 772
  65.9 50.8 %copy-start.1 = (bf16[1536,384]{1,0:T(8,128)(2,1)S(1)}, bf16[1536,384]{1,0:T(8,128)(2,1)}, u32[]{:S(2)}) copy-start(bf16[1536,384]{1,0:T(8,128)(2,1)} %rest_1_.7) | copy-start | bytes 3538948
  65.9 19.3 %all-to-all-start.1 = ((bf16[8,64,512]{2,1,0:T(8,128)(2,1)}), bf16[8,64,512]{2,1,0:T(8,128)(2,1)S(1)}, u32[]{:S(2)}, u32[]{:S(2)}) async-start(bf16[8,64,512]{2,1,0:T(8,128)(2,1)} %fusion.2), calls=%async_computation.1 | async-start | bytes 1048576 | tf_op jit(solution)/shard_map/all_to_all | solution.py:221
  102.1 32.9 %collective-permute-start.6 = (bf16[8,64,512]{2,1,0:T(8,128)(2,1)S(1)}, bf16[8,64,512]{2,1,0:T(8,128)(2,1)S(1)}, u32[]{:S(2)}, u32[]{:S(2)}) collective-permute-start(bf16[8,64,512]{2,1,0:T(8,128)(2,1)S(1)} %all_to_all.21.rest_0_), channel_id=1, source_target_pairs={{0,48},{1,17},{16,0},{17,33},{32,16},{33,49},{48,32},{49,1},{2,50}... | collective-permute-start | bytes 1572872 | tf_op jit(solution)/shard_map/ppermute | solution.py:228
  112.1 25.1 %collective-permute-start.5 = (bf16[8,64,512]{2,1,0:T(8,128)(2,1)S(1)}, bf16[8,64,512]{2,1,0:T(8,128)(2,1)S(1)}, u32[]{:S(2)}, u32[]{:S(2)}) collective-permute-start(bf16[8,64,512]{2,1,0:T(8,128)(2,1)S(1)} %all_to_all.21.rest_0_), channel_id=1, source_target_pairs={{0,32},{1,49},{16,48},{17,1},{32,0},{33,17},{48,16},{49,33},{2,34}... | collective-permute-start | bytes 1572872 | tf_op jit(solution)/shard_map/ppermute | solution.py:228
  114.0 27.4 %collective-permute-start.4 = (bf16[8,64,512]{2,1,0:T(8,128)(2,1)S(1)}, bf16[8,64,512]{2,1,0:T(8,128)(2,1)S(1)}, u32[]{:S(2)}, u32[]{:S(2)}) collective-permute-start(bf16[8,64,512]{2,1,0:T(8,128)(2,1)S(1)} %all_to_all.21.rest_0_), channel_id=1, source_target_pairs={{0,16},{1,33},{16,32},{17,49},{32,48},{33,1},{48,0},{49,17},{2,18}... | collective-permute-start | bytes 1572872 | tf_op jit(solution)/shard_map/ppermute | solution.py:231
  139.5 4.2 %collective-permute-start.7 = (bf16[8,2,64,384]{3,2,1,0:T(8,128)(2,1)S(1)}, bf16[8,2,64,384]{3,2,1,0:T(8,128)(2,1)S(1)}, u32[]{:S(2)}, u32[]{:S(2)}) collective-permute-start(bf16[8,2,64,384]{3,2,1,0:T(8,128)(2,1)S(1)} %get-tuple-element.24), channel_id=1, source_target_pairs={{0,1},{1,0},{2,3},{3,2},{4,5},{5,4},{6,7},{7,6},{8,9},{9,8},{10,11... | collective-permute-start | bytes 2359304 | tf_op jit(solution)/shard_map/ppermute | solution.py:230
  143.9 46.3 %copy-start.6 = (bf16[768]{0:T(1024)(128)(2,1)S(1)}, bf16[768]{0:T(1024)(128)(2,1)}, u32[]{:S(2)}) copy-start(bf16[768]{0:T(1024)(128)(2,1)} %param.15) | copy-start | bytes 4612
  173.6 16.6 %collective-permute-start.8 = (bf16[64,384]{1,0:T(8,128)(2,1)S(1)}, bf16[64,384]{1,0:T(8,128)(2,1)S(1)}, u32[]{:S(2)}, u32[]{:S(2)}) collective-permute-start(bf16[64,384]{1,0:T(8,128)(2,1)S(1)} %get-tuple-element.27), channel_id=1, source_target_pairs={{0,48},{1,16},{2,112},{3,80},{4,176},{5,144},{6,240},{7,208},{8,30... | collective-permute-start | bytes 147464 | tf_op jit(solution)/shard_map/ppermute | solution.py:243
  184.6 12.9 %collective-permute-start.9 = (bf16[64,384]{1,0:T(8,128)(2,1)S(1)}, bf16[64,384]{1,0:T(8,128)(2,1)S(1)}, u32[]{:S(2)}, u32[]{:S(2)}) collective-permute-start(bf16[64,384]{1,0:T(8,128)(2,1)S(1)} %get-tuple-element.28), channel_id=1, source_target_pairs={{0,0},{1,32},{2,64},{3,96},{4,128},{5,160},{6,192},{7,224},{8,256}... | collective-permute-start | bytes 147464 | tf_op jit(solution)/shard_map/ppermute | solution.py:242

commit v7 on v6

--- a/solution.py
+++ b/solution.py
@@ -131,59 +131,52 @@
     )(where, ids, valid, parts, bias)
 
 
-TURNS = ((0, 0), (3, 1), (2, 3), (1, 2))
-
-
-def down_kernel(turns, outs, where, ids, *rest):
-    acts, weight = rest[: len(turns)], rest[len(turns)]
+TURNS = ((0, 0), (1, 3), (3, 1), (2, 2))
+
+
+def down_kernel(turn, outs, where, ids, act, weight, *rest):
     (keep, *send), wide = rest[-1 - outs : -1], rest[-1]
     c, x, high = where[1], where[2], where[3]
-    for turn, ref in zip(turns, acts):
-        k = jnp.where(c == 0, TURNS[turn][0], TURNS[turn][1])
-        source = lax.rem(x + NX - k, NX)
-        wide[...] = jnp.zeros_like(wide)
+    k = jnp.where(c == 0, TURNS[turn][0], TURNS[turn][1])
+    source = lax.rem(x + NX - k, NX)
+    wide[...] = jnp.zeros_like(wide)
+    for y in range(NY):
+        for g in range(ROW // GROUP):
+            group = (y * NX + source) * (ROW // GROUP) + g
+            low = y * ROW + g * GROUP
+            for s in range(CAP):
+                at = pl.multiple_of(ids[group, s] * BLOCK, BLOCK)
+                wide[low : low + GROUP, pl.ds(at, BLOCK)] = act[
+                    y, g * GROUP : (g + 1) * GROUP, s * BLOCK : (s + 1) * BLOCK
+                ]
+    value = jnp.dot(wide[...], weight[...], preferred_element_type=F32).astype(BF16)
+    value = value.reshape(NY, ROW, PIECE)
+
+    def put(ref):
         for y in range(NY):
-            for g in range(ROW // GROUP):
-                group = (y * NX + source) * (ROW // GROUP) + g
-                low = y * ROW + g * GROUP
-                for s in range(CAP):
-                    at = pl.multiple_of(ids[group, s] * BLOCK, BLOCK)
-                    wide[low : low + GROUP, pl.ds(at, BLOCK)] = ref[
-                        y, g * GROUP : (g + 1) * GROUP, s * BLOCK : (s + 1) * BLOCK
-                    ]
-        value = jnp.dot(wide[...], weight[...], preferred_element_type=F32).astype(BF16)
-        value = value.reshape(NY, ROW, PIECE)
-        part = lax.rem(k, 2)
-
-        def put(ref, value=value, part=part):
-            for y in range(NY):
-                ref[lax.rem(y + NZ - high, NZ), part] = value[y]
-
-        own = [k_of // 2 == core for core, k_of in enumerate(TURNS[turn])]
-        if own[0] == own[1]:
-            put(keep if own[0] else send[0])
-        else:
-            pl.when(c == own.index(True))(functools.partial(put, keep))
-            pl.when(c == own.index(False))(functools.partial(put, send[0]))
-
-
-def down(turns, where, ids, acts, weight, before=()):
-    outs = len(before) or 2
-    return pl.pallas_call(
-        functools.partial(down_kernel, turns, outs),
-        out_shape=[jax.ShapeDtypeStruct((NY, 2, ROW, PIECE), BF16)] * outs,
-        in_specs=[SMEM, SMEM] + [VMEM] * (len(turns) + 1 + len(before)),
+            ref[lax.rem(y + NZ - high, NZ)] = value[y]
+
+    if send:
+        pl.when(k // 2 == c)(functools.partial(put, keep))
+        pl.when(k // 2 != c)(functools.partial(put, send[0]))
+    else:
+        put(keep)
+
+
+def down(turn, outs, where, ids, act, weight, before=()):
+    return pl.pallas_call(
+        functools.partial(down_kernel, turn, outs),
+        out_shape=[jax.ShapeDtypeStruct((NZ, ROW, PIECE), BF16)] * outs,
+        in_specs=[SMEM, SMEM] + [VMEM] * (2 + len(before)),
         out_specs=[VMEM] * outs,
         scratch_shapes=[pltpu.VMEM((NY * ROW, weight.shape[0]), BF16)],
-        input_output_aliases={3 + len(turns) + i: i for i in range(len(before))},
+        input_output_aliases={4 + i: i for i in range(len(before))},
         cost_estimate=pl.CostEstimate(
-            flops=(32 if outs == 1 else 1) * 2 * len(turns) * NY * ROW * weight.size,
-            bytes_accessed=0,
-            transcendentals=0,
+            flops=2 * NY * ROW * weight.size, bytes_accessed=0, transcendentals=0
         ),
         compiler_params=pltpu.CompilerParams(vmem_limit_bytes=24 * 2**20),
         name="down",
-    )(where, ids, *acts, weight, *before)
+    )(where, ids, act, weight, *before)
 
 
 def pairs(steps):
@@ -223,14 +216,22 @@
     act = activate(where, ids, valid, part, bias)
 
     act = lax.all_to_all(act, "y", split_axis=0, concat_axis=0, tiled=True)
-    keep, send = down((0,), where, ids, (act,), down_weight)
-    for turn in (1, 2):
-        moved = lax.ppermute(act, ("x", "c"), pairs(TURNS[turn]))
-        keep, send = down((turn,), where, ids, (moved,), down_weight, (keep, send))
-    got = lax.ppermute(send, "c", around(NC, 1))
-    moved = lax.ppermute(act, ("x", "c"), pairs(TURNS[3]))
-    (keep,) = down((3,), where, ids, (moved,), down_weight, (keep,))
-    pair = (keep.astype(F32) + got.astype(F32)).astype(BF16).reshape(NZ, 2 * ROW, PIECE)
+    near = lax.ppermute(act, ("x", "c"), pairs(TURNS[1]))
+    other_side = lax.ppermute(act, ("x", "c"), pairs(TURNS[2]))
+    far = lax.ppermute(near, ("x", "c"), pairs(TURNS[1]))
+    even = down(0, 2, where, ids, act, down_weight)
+    (odd_keep,) = down(1, 1, where, ids, near, down_weight)
+    (odd_send,) = down(2, 1, where, ids, other_side, down_weight)
+    odd_got = lax.ppermute(odd_send, "c", around(NC, 1))
+    even_keep, even_send = down(3, 2, where, ids, far, down_weight, even)
+    even_got = lax.ppermute(even_send, "c", around(NC, 1))
+    pair = jnp.stack(
+        [
+            (kept.astype(F32) + got.astype(F32)).astype(BF16)
+            for kept, got in ((even_keep, even_got), (odd_keep, odd_got))
+        ],
+        axis=1,
+    ).reshape(NZ, 2 * ROW, PIECE)
     pair = lax.all_to_all(pair, "z", split_axis=0, concat_axis=0, tiled=True)
     branch = jnp.sum(pair.astype(F32), axis=0).astype(BF16)
 

time: 200 us -> 196 us (0.980)
  waiting for transfers between devices: 42.9 us -> 37.6 us
    ppermute x4 -> x5, waiting for transfers between devices: 15.9 us -> 10.7 us  [the longest x1 7.14 us: body(): near = lax.ppermute(act, ('x', 'c'), pairs(TURNS[1]))]
    ppermute x4 -> x5, starting transfers between devices: 16.6 us -> 19.8 us  [the longest x1 8.93 us: body(): other_side = lax.ppermute(act, ('x', 'c'), pairs(TURNS[2]))]
  transfers between devices with their start and end apart: 11 -> 12, of which waited for: 5 -> 7; matrix products, arithmetic and copies ran while one was open for 0% -> 0% of each run, Pallas kernels for 9% -> 9%
where the time goes in v7:
time: 196 us
  blocking collectives  74.3 us (38%)
  starting transfers between devices  55.8 us (28%)
  waiting for transfers between devices  37.6 us (19%)
  Pallas kernels  20.8 us (11%)
  other arithmetic  3.5 us (2%)
  local copies, waits for them, and re-layouts  3.16 us (2%)
    all_to_all x1, blocking collectives, body(): pair = lax.all_to_all(pair, 'z', split_axis=0, concat_axis=0, tiled=True)  29.6 us
    all_to_all x1, blocking collectives, body(): lax.all_to_all(normed, ('y', 'x'), split_axis=0, concat_axis=0, tiled=True)  29.1 us
    all_to_all x1, blocking collectives, body(): act = lax.all_to_all(act, 'y', split_axis=0, concat_axis=0, tiled=True)  15.7 us
    pallas_call x5, Pallas kernels, up(): pl.pallas_call(functools.partial(up_kernel, turns), out_shape=[shape] * l...  9.97 us
    all_to_all x1, waiting for transfers between devices, body(): part = lax.all_to_all(part, 'y', split_axis=0, concat_axis=0, tiled=True)  9.9 us
    ppermute x1, starting transfers between devices, body(): second = lax.ppermute(branch[ROW:], ALL, back[1])  9.33 us
    all_to_all x1, starting transfers between devices, body(): part = lax.all_to_all(part, 'y', split_axis=0, concat_axis=0, tiled=True)  9.3 us
    pallas_call x4, Pallas kernels, down(): pl.pallas_call(functools.partial(down_kernel, turn, outs), out_shape=[jax...  9.02 us
  transfers between devices with their start and end apart: 12, of which 7 were waited for; matrix products, arithmetic and copies ran while one was open for 0% of the time, Pallas kernels for 9%

profile of v7, /device:TPU:176, one launch (start us, length us, event | category | flops | bytes accessed | tf_op | source)
XLA Modules:
  0.0 195.6 jit_solution(10665332145251438963)
XLA Ops:
  3.8 29.1 %all_to_all.20 = bf16[32,32,384]{2,1,0:T(8,128)(2,1)S(1)} all-to-all(bf16[32,32,384]{2,1,0:T(8,128)(2,1)S(1)} %norm.1), channel_id=1, replica_groups=mesh['y'=8,'x'=4,'z'=8,'c'=2] {'y','x'}, dimensions={0} | all-to-all | bytes 1572864 | tf_op jit(solution)/shard_map/all_to_all | solution.py:201
  35.0 3.1 %up_first.1 = (bf16[8,2,32,512]{3,2,1,0:T(8,128)(2,1)S(1)}, bf16[8,2,32,512]{3,2,1,0:T(8,128)(2,1)S(1)}, bf16[8,2,32,512]{3,2,1,0:T(8,128)(2,1)S(1)}, bf16[8,2,32,512]{3,2,1,0:T(8,128)(2,1)S(1)}) custom-call(s32[3]{0:T(128)S(1)} %get-tuple-element.26.at, s32[64,4]{1,0:T(8,128)S(1)} %bitcast.29, bf16[8,4,32,384]{3,2,1,0:T(8,128)(2,1)S(1)} %bitcast.39, ...), custom_call_target="tpu_custom_call" | custom-call | flops 1207959552 | tf_op jit(solution)/shard_map/up_first/pallas_call | solution.py:93
  39.9 3.1 %collective-permute-start.2 = (bf16[8,64,512]{2,1,0:T(8,128)(2,1)S(1)}, bf16[8,64,512]{2,1,0:T(8,128)(2,1)S(1)}, u32[]{:S(2)}, u32[]{:S(2)}) collective-permute-start(bf16[8,64,512]{2,1,0:T(8,128)(2,1)S(1)} %bitcast.41), channel_id=1, source_target_pairs={{0,16},{1,49},{16,32},{17,1},{32,48},{33,17},{48,0},{49,33},{2,18}... | collective-permute-start | bytes 1572872 | tf_op jit(solution)/shard_map/ppermute | solution.py:209
  44.7 4.0 %collective-permute-start.1 = (bf16[8,64,512]{2,1,0:T(8,128)(2,1)S(1)}, bf16[8,64,512]{2,1,0:T(8,128)(2,1)S(1)}, u32[]{:S(2)}, u32[]{:S(2)}) collective-permute-start(bf16[8,64,512]{2,1,0:T(8,128)(2,1)S(1)} %bitcast.40), channel_id=1, source_target_pairs={{0,48},{1,17},{16,0},{17,33},{32,16},{33,49},{48,32},{49,1},{2,50}... | collective-permute-start | bytes 1572872 | tf_op jit(solution)/shard_map/ppermute | solution.py:210
  50.4 2.0 %collective-permute-done.2 = bf16[8,64,512]{2,1,0:T(8,128)(2,1)S(1)} collective-permute-done((bf16[8,64,512]{2,1,0:T(8,128)(2,1)S(1)}, bf16[8,64,512]{2,1,0:T(8,128)(2,1)S(1)}, u32[]{:S(2)}, u32[]{:S(2)}) %collective-permute-start.2) | collective-permute-done | bytes 524320 | tf_op jit(solution)/shard_map/ppermute | solution.py:209
  52.6 2.8 %collective-permute-start.3 = (bf16[8,64,512]{2,1,0:T(8,128)(2,1)S(1)}, bf16[8,64,512]{2,1,0:T(8,128)(2,1)S(1)}, u32[]{:S(2)}, u32[]{:S(2)}) collective-permute-start(bf16[8,64,512]{2,1,0:T(8,128)(2,1)S(1)} %fusion), channel_id=1, source_target_pairs={{0,16},{1,49},{16,32},{17,1},{32,48},{33,17},{48,0},{49,33},{2,18}... | collective-permute-start | bytes 1572872 | tf_op jit(solution)/shard_map/ppermute | solution.py:212
  57.1 7.8 %collective-permute-done.3 = bf16[8,64,512]{2,1,0:T(8,128)(2,1)S(1)} collective-permute-done((bf16[8,64,512]{2,1,0:T(8,128)(2,1)S(1)}, bf16[8,64,512]{2,1,0:T(8,128)(2,1)S(1)}, u32[]{:S(2)}, u32[]{:S(2)}) %collective-permute-start.3) | collective-permute-done | bytes 524320 | tf_op jit(solution)/shard_map/ppermute | solution.py:212
  65.9 9.3 %all-to-all-start.1 = ((bf16[8,64,512]{2,1,0:T(8,128)(2,1)}), bf16[8,64,512]{2,1,0:T(8,128)(2,1)S(1)}, u32[]{:S(2)}, u32[]{:S(2)}) async-start(bf16[8,64,512]{2,1,0:T(8,128)(2,1)} %fusion.2), calls=%async_computation.1 | async-start | bytes 1048576 | tf_op jit(solution)/shard_map/all_to_all | solution.py:214
  75.3 9.9 %all-to-all-done.1.parts = bf16[8,64,512]{2,1,0:T(8,128)(2,1)S(1)} async-done(((bf16[8,64,512]{2,1,0:T(8,128)(2,1)}), bf16[8,64,512]{2,1,0:T(8,128)(2,1)S(1)}, u32[]{:S(2)}, u32[]{:S(2)}) %all-to-all-start.1) | async-done | bytes 524320 | tf_op jit(solution)/shard_map/all_to_all | solution.py:214
  86.4 15.7 %all_to_all.21.act = bf16[8,64,512]{2,1,0:T(8,128)(2,1)S(1)} all-to-all(bf16[8,64,512]{2,1,0:T(8,128)(2,1)S(1)} %act.1), channel_id=1, replica_groups=mesh['y'=8,'x'=4,'z'=8,'c'=2] {'y'}, dimensions={0} | all-to-all | bytes 1048576 | tf_op jit(solution)/shard_map/all_to_all | solution.py:218
  102.0 3.0 %collective-permute-start.4 = (bf16[8,64,512]{2,1,0:T(8,128)(2,1)S(1)}, bf16[8,64,512]{2,1,0:T(8,128)(2,1)S(1)}, u32[]{:S(2)}, u32[]{:S(2)}) collective-permute-start(bf16[8,64,512]{2,1,0:T(8,128)(2,1)S(1)} %all_to_all.21.act), channel_id=1, source_target_pairs={{0,16},{1,49},{16,32},{17,1},{32,48},{33,17},{48,0},{49,33},{2,18}... | collective-permute-start | bytes 1572872 | tf_op jit(solution)/shard_map/ppermute | solution.py:219
  105.0 8.9 %collective-permute-start.7 = (bf16[8,64,512]{2,1,0:T(8,128)(2,1)S(1)}, bf16[8,64,512]{2,1,0:T(8,128)(2,1)S(1)}, u32[]{:S(2)}, u32[]{:S(2)}) collective-permute-start(bf16[8,64,512]{2,1,0:T(8,128)(2,1)S(1)} %all_to_all.21.act), channel_id=1, source_target_pairs={{0,48},{1,17},{16,0},{17,33},{32,16},{33,49},{48,32},{49,1},{2,50}... | collective-permute-start | bytes 1572872 | tf_op jit(solution)/shard_map/ppermute | solution.py:220
  114.0 7.1 %collective-permute-done.4.act = bf16[8,64,512]{2,1,0:T(8,128)(2,1)S(1)} collective-permute-done((bf16[8,64,512]{2,1,0:T(8,128)(2,1)S(1)}, bf16[8,64,512]{2,1,0:T(8,128)(2,1)S(1)}, u32[]{:S(2)}, u32[]{:S(2)}) %collective-permute-start.4) | collective-permute-done | bytes 524320 | tf_op jit(solution)/shard_map/ppermute | solution.py:219
  123.1 2.2 %down.7 = bf16[8,64,384]{2,1,0:T(8,128)(2,1)S(1)} custom-call(s32[4]{0:T(128)S(1)} %pad_add_fusion.where, s32[64,4]{1,0:T(8,128)S(1)} %bitcast.35, bf16[8,64,512]{2,1,0:T(8,128)(2,1)S(1)} %collective-permute-done.7.act, bf16[1536,384]{1,0:T(8,128)(2,1)S(1)} %copy-done.2), custom_call_target="tpu_custom_call" | custom-call | flops 603979776 | tf_op jit(solution)/shard_map/down/pallas_call | solution.py:167
  125.3 4.1 %collective-permute-start.8 = (bf16[8,64,384]{2,1,0:T(8,128)(2,1)S(1)}, bf16[8,64,384]{2,1,0:T(8,128)(2,1)S(1)}, u32[]{:S(2)}, u32[]{:S(2)}) collective-permute-start(bf16[8,64,384]{2,1,0:T(8,128)(2,1)S(1)} %down.7), channel_id=1, source_target_pairs={{0,1},{1,0},{2,3},{3,2},{4,5},{5,4},{6,7},{7,6},{8,9},{9,8},{10,11... | collective-permute-start | bytes 1179656 | tf_op jit(solution)/shard_map/ppermute | solution.py:225
  129.5 2.3 %down.4 = (bf16[8,64,384]{2,1,0:T(8,128)(2,1)S(1)}, bf16[8,64,384]{2,1,0:T(8,128)(2,1)S(1)}) custom-call(s32[4]{0:T(128)S(1)} %pad_add_fusion.where, s32[64,4]{1,0:T(8,128)S(1)} %bitcast.36, bf16[8,64,512]{2,1,0:T(8,128)(2,1)S(1)} %all_to_all.21.act, bf16[1536,384]{1,0:T(8,128)(2,1)S(1)} %copy-done.2), custom_call_target="tpu_custom_call" | custom-call | flops 603979776 | tf_op jit(solution)/shard_map/down/pallas_call | solution.py:167
  131.7 3.5 %collective-permute-done.5.act = bf16[8,64,512]{2,1,0:T(8,128)(2,1)S(1)} collective-permute-done((bf16[8,64,512]{2,1,0:T(8,128)(2,1)S(1)}, bf16[8,64,512]{2,1,0:T(8,128)(2,1)S(1)}, u32[]{:S(2)}, u32[]{:S(2)}) %collective-permute-start.5) | collective-permute-done | bytes 524320 | tf_op jit(solution)/shard_map/ppermute | solution.py:221
  135.2 2.3 %down.5 = (bf16[8,64,384]{2,1,0:T(8,128)(2,1)S(1)}, bf16[8,64,384]{2,1,0:T(8,128)(2,1)S(1)}) custom-call(s32[4]{0:T(128)S(1)} %pad_add_fusion.where, s32[64,4]{1,0:T(8,128)S(1)} %bitcast.37, bf16[8,64,512]{2,1,0:T(8,128)(2,1)S(1)} %collective-permute-done.5.act, bf16[1536,384]{1,0:T(8,128)(2,1)S(1)} %copy-done.2, ...), custom_call_target="tpu_custom_call", output_to_operand_aliasing={{0}: (4, {}), {1}: (5, {})} | custom-call | flops 603979776 | tf_op jit(solution)/shard_map/down/pallas_call | solution.py:167
  137.5 1.9 collective-permute-start.6
  139.4 2.2 %down.6 = bf16[8,64,384]{2,1,0:T(8,128)(2,1)S(1)} custom-call(s32[4]{0:T(128)S(1)} %pad_add_fusion.where, s32[64,4]{1,0:T(8,128)S(1)} %bitcast.38, bf16[8,64,512]{2,1,0:T(8,128)(2,1)S(1)} %collective-permute-done.4.act, bf16[1536,384]{1,0:T(8,128)(2,1)S(1)} %copy-done.2), custom_call_target="tpu_custom_call" | custom-call | flops 603979776 | tf_op jit(solution)/shard_map/down/pallas_call | solution.py:167
  142.1 29.6 %all_to_all.22 = bf16[8,128,384]{2,1,0:T(8,128)(2,1)S(1)} all-to-all(bf16[8,128,384]{2,1,0:T(8,128)(2,1)S(1)} %bitcast.43), channel_id=1, replica_groups=mesh['y'=8,'x'=4,'z'=8,'c'=2] {'z'}, dimensions={0} | all-to-all | bytes 1572864 | tf_op jit(solution)/shard_map/all_to_all | solution.py:235
  171.8 9.3 %collective-permute-start.9 = (bf16[64,384]{1,0:T(8,128)(2,1)S(1)}, bf16[64,384]{1,0:T(8,128)(2,1)S(1)}, u32[]{:S(2)}, u32[]{:S(2)}) collective-permute-start(bf16[64,384]{1,0:T(8,128)(2,1)S(1)} %get-tuple-element.23), channel_id=1, source_target_pairs={{0,48},{1,16},{2,112},{3,80},{4,176},{5,144},{6,240},{7,208},{8,30... | collective-permute-start | bytes 147464 | tf_op jit(solution)/shard_map/ppermute | solution.py:244
  181.1 5.6 %collective-permute-start.10 = (bf16[64,384]{1,0:T(8,128)(2,1)S(1)}, bf16[64,384]{1,0:T(8,128)(2,1)S(1)}, u32[]{:S(2)}, u32[]{:S(2)}) collective-permute-start(bf16[64,384]{1,0:T(8,128)(2,1)S(1)} %get-tuple-element.24), channel_id=1, source_target_pairs={{0,0},{1,32},{2,64},{3,96},{4,128},{5,160},{6,192},{7,224},{8,256}... | collective-permute-start | bytes 147464 | tf_op jit(solution)/shard_map/ppermute | solution.py:243
  186.8 7.3 %collective-permute-done.10 = bf16[64,384]{1,0:T(8,128)(2,1)S(1)} collective-permute-done((bf16[64,384]{1,0:T(8,128)(2,1)S(1)}, bf16[64,384]{1,0:T(8,128)(2,1)S(1)}, u32[]{:S(2)}, u32[]{:S(2)}) %collective-permute-start.10) | collective-permute-done | bytes 49184 | tf_op jit(solution)/shard_map/ppermute | solution.py:243
  (46 shorter events, 19.3 us)
Async XLA Ops:
  1.7 1.4 copy-start.1
  3.1 31.7 %copy-start.5 = (s32[64,1,4]{0,2,1:T(4,128)S(1)}, s32[64,1,4]{0,2,1:T(4,128)}, u32[]{:S(2)}) copy-start(s32[64,1,4]{0,2,1:T(4,128)} %param.16) | copy-start | bytes 3076
  3.1 31.9 %copy-start = (bf16[384,1536]{1,0:T(8,128)(2,1)S(1)}, bf16[384,1536]{1,0:T(8,128)(2,1)}, u32[]{:S(2)}) copy-start(bf16[384,1536]{1,0:T(8,128)(2,1)} %weight.13) | copy-start | bytes 3538948
  32.9 5.3 %collective-permute-start = (bf16[32,32,384]{2,1,0:T(8,128)(2,1)S(1)}, bf16[32,32,384]{2,1,0:T(8,128)(2,1)S(1)}, u32[]{:S(2)}, u32[]{:S(2)}) collective-permute-start(bf16[32,32,384]{2,1,0:T(8,128)(2,1)S(1)} %all_to_all.20), channel_id=1, source_target_pairs={{0,1},{1,0},{2,3},{3,2},{4,5},{5,4},{6,7},{7,6},{8,9},{9,8},{10,11... | collective-permute-start | bytes 2359304 | tf_op jit(solution)/shard_map/ppermute | solution.py:202
  39.9 12.5 %collective-permute-start.2 = (bf16[8,64,512]{2,1,0:T(8,128)(2,1)S(1)}, bf16[8,64,512]{2,1,0:T(8,128)(2,1)S(1)}, u32[]{:S(2)}, u32[]{:S(2)}) collective-permute-start(bf16[8,64,512]{2,1,0:T(8,128)(2,1)S(1)} %bitcast.41), channel_id=1, source_target_pairs={{0,16},{1,49},{16,32},{17,1},{32,48},{33,17},{48,0},{49,33},{2,18}... | collective-permute-start | bytes 1572872 | tf_op jit(solution)/shard_map/ppermute | solution.py:209
  44.7 12.4 %collective-permute-start.1 = (bf16[8,64,512]{2,1,0:T(8,128)(2,1)S(1)}, bf16[8,64,512]{2,1,0:T(8,128)(2,1)S(1)}, u32[]{:S(2)}, u32[]{:S(2)}) collective-permute-start(bf16[8,64,512]{2,1,0:T(8,128)(2,1)S(1)} %bitcast.40), channel_id=1, source_target_pairs={{0,48},{1,17},{16,0},{17,33},{32,16},{33,49},{48,32},{49,1},{2,50}... | collective-permute-start | bytes 1572872 | tf_op jit(solution)/shard_map/ppermute | solution.py:210
  52.6 12.3 %collective-permute-start.3 = (bf16[8,64,512]{2,1,0:T(8,128)(2,1)S(1)}, bf16[8,64,512]{2,1,0:T(8,128)(2,1)S(1)}, u32[]{:S(2)}, u32[]{:S(2)}) collective-permute-start(bf16[8,64,512]{2,1,0:T(8,128)(2,1)S(1)} %fusion), channel_id=1, source_target_pairs={{0,16},{1,49},{16,32},{17,1},{32,48},{33,17},{48,0},{49,33},{2,18}... | collective-permute-start | bytes 1572872 | tf_op jit(solution)/shard_map/ppermute | solution.py:212
  57.1 18.2 %copy-start.4 = (bf16[1536]{0:T(1024)(128)(2,1)S(1)}, bf16[1536]{0:T(1024)(128)(2,1)}, u32[]{:S(2)}) copy-start(bf16[1536]{0:T(1024)(128)(2,1)} %param.13) | copy-start | bytes 9220
  57.1 28.1 %copy-start.3 = (s32[64,1]{0,1:T(1,128)S(1)}, s32[64,1]{0,1:T(1,128)}, u32[]{:S(2)}) copy-start(s32[64,1]{0,1:T(1,128)} %param.17) | copy-start | bytes 772
  65.9 57.2 %copy-start.2 = (bf16[1536,384]{1,0:T(8,128)(2,1)S(1)}, bf16[1536,384]{1,0:T(8,128)(2,1)}, u32[]{:S(2)}) copy-start(bf16[1536,384]{1,0:T(8,128)(2,1)} %weight.17) | copy-start | bytes 3538948
  65.9 19.3 %all-to-all-start.1 = ((bf16[8,64,512]{2,1,0:T(8,128)(2,1)}), bf16[8,64,512]{2,1,0:T(8,128)(2,1)S(1)}, u32[]{:S(2)}, u32[]{:S(2)}) async-start(bf16[8,64,512]{2,1,0:T(8,128)(2,1)} %fusion.2), calls=%async_computation.1 | async-start | bytes 1048576 | tf_op jit(solution)/shard_map/all_to_all | solution.py:214
  102.0 19.1 %collective-permute-start.4 = (bf16[8,64,512]{2,1,0:T(8,128)(2,1)S(1)}, bf16[8,64,512]{2,1,0:T(8,128)(2,1)S(1)}, u32[]{:S(2)}, u32[]{:S(2)}) collective-permute-start(bf16[8,64,512]{2,1,0:T(8,128)(2,1)S(1)} %all_to_all.21.act), channel_id=1, source_target_pairs={{0,16},{1,49},{16,32},{17,1},{32,48},{33,17},{48,0},{49,33},{2,18}... | collective-permute-start | bytes 1572872 | tf_op jit(solution)/shard_map/ppermute | solution.py:219
  105.0 18.1 %collective-permute-start.7 = (bf16[8,64,512]{2,1,0:T(8,128)(2,1)S(1)}, bf16[8,64,512]{2,1,0:T(8,128)(2,1)S(1)}, u32[]{:S(2)}, u32[]{:S(2)}) collective-permute-start(bf16[8,64,512]{2,1,0:T(8,128)(2,1)S(1)} %all_to_all.21.act), channel_id=1, source_target_pairs={{0,48},{1,17},{16,0},{17,33},{32,16},{33,49},{48,32},{49,1},{2,50}... | collective-permute-start | bytes 1572872 | tf_op jit(solution)/shard_map/ppermute | solution.py:220
  121.1 14.1 %collective-permute-start.5 = (bf16[8,64,512]{2,1,0:T(8,128)(2,1)S(1)}, bf16[8,64,512]{2,1,0:T(8,128)(2,1)S(1)}, u32[]{:S(2)}, u32[]{:S(2)}) collective-permute-start(bf16[8,64,512]{2,1,0:T(8,128)(2,1)S(1)} %collective-permute-done.4.act), channel_id=1, source_target_pairs={{0,16},{1,49},{16,32},{17,1},{32,48},{33,17},{48,0},{49,33},{2,18}... | collective-permute-start | bytes 1572872 | tf_op jit(solution)/shard_map/ppermute | solution.py:221
  125.3 16.3 %collective-permute-start.8 = (bf16[8,64,384]{2,1,0:T(8,128)(2,1)S(1)}, bf16[8,64,384]{2,1,0:T(8,128)(2,1)S(1)}, u32[]{:S(2)}, u32[]{:S(2)}) collective-permute-start(bf16[8,64,384]{2,1,0:T(8,128)(2,1)S(1)} %down.7), channel_id=1, source_target_pairs={{0,1},{1,0},{2,3},{3,2},{4,5},{5,4},{6,7},{7,6},{8,9},{9,8},{10,11... | collective-permute-start | bytes 1179656 | tf_op jit(solution)/shard_map/ppermute | solution.py:225
  137.5 4.3 %collective-permute-start.6 = (bf16[8,64,384]{2,1,0:T(8,128)(2,1)S(1)}, bf16[8,64,384]{2,1,0:T(8,128)(2,1)S(1)}, u32[]{:S(2)}, u32[]{:S(2)}) collective-permute-start(bf16[8,64,384]{2,1,0:T(8,128)(2,1)S(1)} %get-tuple-element.20), channel_id=1, source_target_pairs={{0,1},{1,0},{2,3},{3,2},{4,5},{5,4},{6,7},{7,6},{8,9},{9,8},{10,11... | collective-permute-start | bytes 1179656 | tf_op jit(solution)/shard_map/ppermute | solution.py:227
  142.1 44.6 %copy-start.6 = (bf16[768]{0:T(1024)(128)(2,1)S(1)}, bf16[768]{0:T(1024)(128)(2,1)}, u32[]{:S(2)}) copy-start(bf16[768]{0:T(1024)(128)(2,1)} %param.15) | copy-start | bytes 4612
  171.8 15.0 %collective-permute-start.9 = (bf16[64,384]{1,0:T(8,128)(2,1)S(1)}, bf16[64,384]{1,0:T(8,128)(2,1)S(1)}, u32[]{:S(2)}, u32[]{:S(2)}) collective-permute-start(bf16[64,384]{1,0:T(8,128)(2,1)S(1)} %get-tuple-element.23), channel_id=1, source_target_pairs={{0,48},{1,16},{2,112},{3,80},{4,176},{5,144},{6,240},{7,208},{8,30... | collective-permute-start | bytes 147464 | tf_op jit(solution)/shard_map/ppermute | solution.py:244
  181.1 12.9 %collective-permute-start.10 = (bf16[64,384]{1,0:T(8,128)(2,1)S(1)}, bf16[64,384]{1,0:T(8,128)(2,1)S(1)}, u32[]{:S(2)}, u32[]{:S(2)}) collective-permute-start(bf16[64,384]{1,0:T(8,128)(2,1)S(1)} %get-tuple-element.24), channel_id=1, source_target_pairs={{0,0},{1,32},{2,64},{3,96},{4,128},{5,160},{6,192},{7,224},{8,256}... | collective-permute-start | bytes 147464 | tf_op jit(solution)/shard_map/ppermute | solution.py:243

commit v8 on v7

--- a/solution.py
+++ b/solution.py
@@ -11,6 +11,7 @@
 BLOCK = 128
 GROUP = 32
 CAP = 4
+GROUPS = 64
 NY, NX, NZ, NC = 8, 4, 8, 2
 ROW = 64
 PIECE = 384
@@ -23,7 +24,11 @@
     return [(i, (i + k) % size) for i in range(size)]
 
 
-def norm_kernel(half, hidden, scales, out):
+SMEM = pl.BlockSpec(memory_space=pltpu.SMEM)
+VMEM = pl.BlockSpec(memory_space=pltpu.VMEM)
+
+
+def norm_kernel(hidden, scales, out):
     rows, features = hidden.shape
     pieces = features // PIECE
 
@@ -46,28 +51,19 @@
         out[p] = value.astype(BF16)
 
 
-def norm(half, hidden, scales):
+def norm(hidden, scales):
     features = hidden.shape[1]
     pieces = features // PIECE
     return pl.pallas_call(
         norm_kernel,
         out_shape=jax.ShapeDtypeStruct((pieces, GROUP, PIECE), BF16),
-        grid_spec=pltpu.PrefetchScalarGridSpec(
-            num_scalar_prefetch=1,
-            grid=(1,),
-            in_specs=[
-                pl.BlockSpec((GROUP, features), lambda i, half: (half[0], 0)),
-                pl.BlockSpec((2, features), lambda i, half: (0, 0)),
-            ],
-            out_specs=pl.BlockSpec((pieces, GROUP, PIECE), lambda i, half: (0, 0, 0)),
-        ),
+        in_specs=[VMEM, VMEM],
+        out_specs=VMEM,
         compiler_params=pltpu.CompilerParams(vmem_limit_bytes=32 * 2**20),
         name="norm",
-    )(half, hidden, scales)
-
-
-SMEM = pl.BlockSpec(memory_space=pltpu.SMEM)
-VMEM = pl.BlockSpec(memory_space=pltpu.VMEM)
+    )(hidden, scales)
+
+
 LEAVES = ((2, 2), (3, 1), (1, 3), (0, 0))
 
 
@@ -83,7 +79,7 @@
         for y in range(NY):
             group = (y * NX + target) * (ROW // GROUP) + h
             for s in range(CAP):
-                block = pl.multiple_of(ids[group, s] * BLOCK, BLOCK)
+                block = pl.multiple_of(ids[s * GROUPS + group] * BLOCK, BLOCK)
                 picked = total[y * GROUP : (y + 1) * GROUP, pl.ds(block, BLOCK)]
                 out[y, h, :, s * BLOCK : (s + 1) * BLOCK] = picked.astype(BF16)
 
@@ -112,7 +108,7 @@
     for g in range(ROW // GROUP):
         group = where[0] * (ROW // GROUP) + g
         for s in range(CAP):
-            block = ids[group, s]
+            block = ids[s * GROUPS + group]
             keep = (s < valid[group]).astype(F32)
             mine = pre[g * GROUP : (g + 1) * GROUP, s * BLOCK : (s + 1) * BLOCK]
             value = (jnp.maximum(mine + bias[pl.ds(block, 1), :], 0.0) * keep).astype(BF16)
@@ -145,7 +141,7 @@
             group = (y * NX + source) * (ROW // GROUP) + g
             low = y * ROW + g * GROUP
             for s in range(CAP):
-                at = pl.multiple_of(ids[group, s] * BLOCK, BLOCK)
+                at = pl.multiple_of(ids[s * GROUPS + group] * BLOCK, BLOCK)
                 wide[low : low + GROUP, pl.ds(at, BLOCK)] = act[
                     y, g * GROUP : (g + 1) * GROUP, s * BLOCK : (s + 1) * BLOCK
                 ]
@@ -190,14 +186,14 @@
     z, c = lax.axis_index("z"), lax.axis_index("c")
     r, t = y * NX + x, z * NC + c
     odd = lax.rem(r, 2) == 1
-    ids, valid = active[:, 0, :], counts[:, 0]
+    ids, valid = active[:, 0, :].T.reshape(-1), counts.reshape(-1)
     where = jnp.stack([r, c, x, y]).astype(jnp.int32)
     width = down_bias.shape[0]
 
     mine = jnp.stack([c, x, c]).astype(jnp.int32)
     others = jnp.stack([1 - c, x, c]).astype(jnp.int32)
     scales = jnp.stack([norm_gain, norm_shift]).astype(F32)
-    normed = norm(c.reshape(1), hidden_in, scales)
+    normed = norm(lax.dynamic_slice_in_dim(hidden_in, c * GROUP, GROUP, 0), scales)
     own = lax.all_to_all(normed, ("y", "x"), split_axis=0, concat_axis=0, tiled=True)
     other = lax.ppermute(own, "c", around(NC, 1))
     own, other = (v.reshape(NY, NX, GROUP, PIECE) for v in (own, other))
@@ -218,8 +214,9 @@
     act = lax.all_to_all(act, "y", split_axis=0, concat_axis=0, tiled=True)
     near = lax.ppermute(act, ("x", "c"), pairs(TURNS[1]))
     other_side = lax.ppermute(act, ("x", "c"), pairs(TURNS[2]))
+    even = down(0, 2, where, ids, act, down_weight)
+    near, even = lax.optimization_barrier((near, even))
     far = lax.ppermute(near, ("x", "c"), pairs(TURNS[1]))
-    even = down(0, 2, where, ids, act, down_weight)
     (odd_keep,) = down(1, 1, where, ids, near, down_weight)
     (odd_send,) = down(2, 1, where, ids, other_side, down_weight)
     odd_got = lax.ppermute(odd_send, "c", around(NC, 1))

time: 196 us -> 194 us (0.990)
  Pallas kernels: 20.8 us -> 15.6 us
  waiting for transfers between devices: 37.6 us -> 40.8 us
    ppermute x1, waiting for transfers between devices: 3.46 us -> 6.28 us  [body(): far = lax.ppermute(near, ('x', 'c'), pairs(TURNS[1]))]
    pallas_call x5, Pallas kernels: 9.97 us -> 7.37 us  [up(): pl.pallas_call(functools.partial(up_kernel, turns), out_shape=[shape] * l...]
    pallas_call x4, Pallas kernels: 9.02 us -> 6.93 us  [down(): pl.pallas_call(functools.partial(down_kernel, turn, outs), out_shape=[jax...]
  transfers between devices with their start and end apart: 12 -> 12, of which waited for: 7 -> 7; matrix products, arithmetic and copies ran while one was open for 0% -> 0% of each run, Pallas kernels for 9% -> 7%
where the time goes in v8:
time: 194 us; the launch traced here: 193 us
  blocking collectives  74.4 us (38%)
  starting transfers between devices  55.8 us (29%)
  waiting for transfers between devices  40.8 us (21%)
  Pallas kernels  15.6 us (8%)
  other arithmetic  3.57 us (2%)
  local copies, waits for them, and re-layouts  2.94 us (2%)
    all_to_all x1, blocking collectives, body(): pair = lax.all_to_all(pair, 'z', split_axis=0, concat_axis=0, tiled=True)  29.6 us
    all_to_all x1, blocking collectives, body(): lax.all_to_all(normed, ('y', 'x'), split_axis=0, concat_axis=0, tiled=True)  29.1 us
    all_to_all x1, blocking collectives, body(): act = lax.all_to_all(act, 'y', split_axis=0, concat_axis=0, tiled=True)  15.7 us
    ppermute x1, starting transfers between devices, body(): other_side = lax.ppermute(act, ('x', 'c'), pairs(TURNS[2]))  9.97 us
    all_to_all x1, waiting for transfers between devices, body(): part = lax.all_to_all(part, 'y', split_axis=0, concat_axis=0, tiled=True)  9.89 us
    ppermute x1, starting transfers between devices, body(): second = lax.ppermute(branch[ROW:], ALL, back[1])  9.33 us
    all_to_all x1, starting transfers between devices, body(): part = lax.all_to_all(part, 'y', split_axis=0, concat_axis=0, tiled=True)  9.28 us
    ppermute x1, waiting for transfers between devices, body(): joined = lax.ppermute(joined, ('x', 'c'), pairs(LEAVES[2]))  8.27 us
  transfers between devices with their start and end apart: 12, of which 7 were waited for; matrix products, arithmetic and copies ran while one was open for 0% of the time, Pallas kernels for 7%

profile of v8, /device:TPU:176, one launch (start us, length us, event | category | flops | bytes accessed | tf_op | source)
XLA Modules:
  0.0 193.4 jit_solution(17001050795393435330)
XLA Ops:
  3.6 29.1 %all_to_all.20 = bf16[32,32,384]{2,1,0:T(8,128)(2,1)S(1)} all-to-all(bf16[32,32,384]{2,1,0:T(8,128)(2,1)S(1)} %norm.1), channel_id=1, replica_groups=mesh['y'=8,'x'=4,'z'=8,'c'=2] {'y','x'}, dimensions={0} | all-to-all | bytes 1572864 | tf_op jit(solution)/shard_map/all_to_all | solution.py:197
  32.7 1.9 collective-permute-start
  34.8 2.6 %up_first.1 = (bf16[8,2,32,512]{3,2,1,0:T(8,128)(2,1)S(1)}, bf16[8,2,32,512]{3,2,1,0:T(8,128)(2,1)S(1)}, bf16[8,2,32,512]{3,2,1,0:T(8,128)(2,1)S(1)}, bf16[8,2,32,512]{3,2,1,0:T(8,128)(2,1)S(1)}) custom-call(s32[3]{0:T(128)S(1)} %add_add_fusion.1.at, s32[256]{0:T(256)S(1)} %reshape.33.ids, bf16[8,4,32,384]{3,2,1,0:T(8,128)(2,1)S(1)} %bitcast.31, ...), custom_call_target="tpu_custom_call" | custom-call | flops 1207959552 | tf_op jit(solution)/shard_map/up_first/pallas_call | solution.py:89
  38.7 3.1 %collective-permute-start.2 = (bf16[8,64,512]{2,1,0:T(8,128)(2,1)S(1)}, bf16[8,64,512]{2,1,0:T(8,128)(2,1)S(1)}, u32[]{:S(2)}, u32[]{:S(2)}) collective-permute-start(bf16[8,64,512]{2,1,0:T(8,128)(2,1)S(1)} %bitcast.33), channel_id=1, source_target_pairs={{0,16},{1,49},{16,32},{17,1},{32,48},{33,17},{48,0},{49,33},{2,18}... | collective-permute-start | bytes 1572872 | tf_op jit(solution)/shard_map/ppermute | solution.py:205
  43.0 4.0 %collective-permute-start.1 = (bf16[8,64,512]{2,1,0:T(8,128)(2,1)S(1)}, bf16[8,64,512]{2,1,0:T(8,128)(2,1)S(1)}, u32[]{:S(2)}, u32[]{:S(2)}) collective-permute-start(bf16[8,64,512]{2,1,0:T(8,128)(2,1)S(1)} %bitcast.32), channel_id=1, source_target_pairs={{0,48},{1,17},{16,0},{17,33},{32,16},{33,49},{48,32},{49,1},{2,50}... | collective-permute-start | bytes 1572872 | tf_op jit(solution)/shard_map/ppermute | solution.py:206
  48.1 3.6 %collective-permute-done.2 = bf16[8,64,512]{2,1,0:T(8,128)(2,1)S(1)} collective-permute-done((bf16[8,64,512]{2,1,0:T(8,128)(2,1)S(1)}, bf16[8,64,512]{2,1,0:T(8,128)(2,1)S(1)}, u32[]{:S(2)}, u32[]{:S(2)}) %collective-permute-start.2) | collective-permute-done | bytes 524320 | tf_op jit(solution)/shard_map/ppermute | solution.py:205
  51.9 2.8 %collective-permute-start.3 = (bf16[8,64,512]{2,1,0:T(8,128)(2,1)S(1)}, bf16[8,64,512]{2,1,0:T(8,128)(2,1)S(1)}, u32[]{:S(2)}, u32[]{:S(2)}) collective-permute-start(bf16[8,64,512]{2,1,0:T(8,128)(2,1)S(1)} %fusion), channel_id=1, source_target_pairs={{0,16},{1,49},{16,32},{17,1},{32,48},{33,17},{48,0},{49,33},{2,18}... | collective-permute-start | bytes 1572872 | tf_op jit(solution)/shard_map/ppermute | solution.py:208
  56.0 8.3 %collective-permute-done.3 = bf16[8,64,512]{2,1,0:T(8,128)(2,1)S(1)} collective-permute-done((bf16[8,64,512]{2,1,0:T(8,128)(2,1)S(1)}, bf16[8,64,512]{2,1,0:T(8,128)(2,1)S(1)}, u32[]{:S(2)}, u32[]{:S(2)}) %collective-permute-start.3) | collective-permute-done | bytes 524320 | tf_op jit(solution)/shard_map/ppermute | solution.py:208
  65.3 9.3 %all-to-all-start.1 = ((bf16[8,64,512]{2,1,0:T(8,128)(2,1)}), bf16[8,64,512]{2,1,0:T(8,128)(2,1)S(1)}, u32[]{:S(2)}, u32[]{:S(2)}) async-start(bf16[8,64,512]{2,1,0:T(8,128)(2,1)} %fusion.2), calls=%async_computation.1 | async-start | bytes 1048576 | tf_op jit(solution)/shard_map/all_to_all | solution.py:210
  74.6 9.9 %all-to-all-done.1.parts = bf16[8,64,512]{2,1,0:T(8,128)(2,1)S(1)} async-done(((bf16[8,64,512]{2,1,0:T(8,128)(2,1)}), bf16[8,64,512]{2,1,0:T(8,128)(2,1)S(1)}, u32[]{:S(2)}, u32[]{:S(2)}) %all-to-all-start.1) | async-done | bytes 524320 | tf_op jit(solution)/shard_map/all_to_all | solution.py:210
  85.2 15.7 %all_to_all.21.act = bf16[8,64,512]{2,1,0:T(8,128)(2,1)S(1)} all-to-all(bf16[8,64,512]{2,1,0:T(8,128)(2,1)S(1)} %act.1), channel_id=1, replica_groups=mesh['y'=8,'x'=4,'z'=8,'c'=2] {'y'}, dimensions={0} | all-to-all | bytes 1048576 | tf_op jit(solution)/shard_map/all_to_all | solution.py:214
  100.9 1.9 collective-permute-start.4
  102.8 10.0 %collective-permute-start.7 = (bf16[8,64,512]{2,1,0:T(8,128)(2,1)S(1)}, bf16[8,64,512]{2,1,0:T(8,128)(2,1)S(1)}, u32[]{:S(2)}, u32[]{:S(2)}) collective-permute-start(bf16[8,64,512]{2,1,0:T(8,128)(2,1)S(1)} %all_to_all.21.act), channel_id=1, source_target_pairs={{0,48},{1,17},{16,0},{17,33},{32,16},{33,49},{48,32},{49,1},{2,50}... | collective-permute-start | bytes 1572872 | tf_op jit(solution)/shard_map/ppermute | solution.py:216
  112.8 1.8 down.4
  114.5 5.4 %collective-permute-done.4.act = bf16[8,64,512]{2,1,0:T(8,128)(2,1)S(1)} collective-permute-done((bf16[8,64,512]{2,1,0:T(8,128)(2,1)S(1)}, bf16[8,64,512]{2,1,0:T(8,128)(2,1)S(1)}, u32[]{:S(2)}, u32[]{:S(2)}) %collective-permute-start.4) | collective-permute-done | bytes 524320 | tf_op jit(solution)/shard_map/ppermute | solution.py:215
  119.9 1.9 collective-permute-start.5
  123.6 4.1 %collective-permute-start.8 = (bf16[8,64,384]{2,1,0:T(8,128)(2,1)S(1)}, bf16[8,64,384]{2,1,0:T(8,128)(2,1)S(1)}, u32[]{:S(2)}, u32[]{:S(2)}) collective-permute-start(bf16[8,64,384]{2,1,0:T(8,128)(2,1)S(1)} %down.7), channel_id=1, source_target_pairs={{0,1},{1,0},{2,3},{3,2},{4,5},{5,4},{6,7},{7,6},{8,9},{9,8},{10,11... | collective-permute-start | bytes 1179656 | tf_op jit(solution)/shard_map/ppermute | solution.py:222
  127.7 6.3 %collective-permute-done.5.act = bf16[8,64,512]{2,1,0:T(8,128)(2,1)S(1)} collective-permute-done((bf16[8,64,512]{2,1,0:T(8,128)(2,1)S(1)}, bf16[8,64,512]{2,1,0:T(8,128)(2,1)S(1)}, u32[]{:S(2)}, u32[]{:S(2)}) %collective-permute-start.5) | collective-permute-done | bytes 524320 | tf_op jit(solution)/shard_map/ppermute | solution.py:219
  134.0 1.8 down.5
  135.8 1.9 collective-permute-start.6
  139.9 29.6 %all_to_all.22 = bf16[8,128,384]{2,1,0:T(8,128)(2,1)S(1)} all-to-all(bf16[8,128,384]{2,1,0:T(8,128)(2,1)S(1)} %bitcast.35), channel_id=1, replica_groups=mesh['y'=8,'x'=4,'z'=8,'c'=2] {'z'}, dimensions={0} | all-to-all | bytes 1572864 | tf_op jit(solution)/shard_map/all_to_all | solution.py:232
  169.6 9.3 %collective-permute-start.9 = (bf16[64,384]{1,0:T(8,128)(2,1)S(1)}, bf16[64,384]{1,0:T(8,128)(2,1)S(1)}, u32[]{:S(2)}, u32[]{:S(2)}) collective-permute-start(bf16[64,384]{1,0:T(8,128)(2,1)S(1)} %get-tuple-element.29), channel_id=1, source_target_pairs={{0,48},{1,16},{2,112},{3,80},{4,176},{5,144},{6,240},{7,208},{8,30... | collective-permute-start | bytes 147464 | tf_op jit(solution)/shard_map/ppermute | solution.py:241
  178.9 5.6 %collective-permute-start.10 = (bf16[64,384]{1,0:T(8,128)(2,1)S(1)}, bf16[64,384]{1,0:T(8,128)(2,1)S(1)}, u32[]{:S(2)}, u32[]{:S(2)}) collective-permute-start(bf16[64,384]{1,0:T(8,128)(2,1)S(1)} %get-tuple-element.30), channel_id=1, source_target_pairs={{0,0},{1,32},{2,64},{3,96},{4,128},{5,160},{6,192},{7,224},{8,256}... | collective-permute-start | bytes 147464 | tf_op jit(solution)/shard_map/ppermute | solution.py:240
  184.6 7.3 %collective-permute-done.10 = bf16[64,384]{1,0:T(8,128)(2,1)S(1)} collective-permute-done((bf16[64,384]{1,0:T(8,128)(2,1)S(1)}, bf16[64,384]{1,0:T(8,128)(2,1)S(1)}, u32[]{:S(2)}, u32[]{:S(2)}) %collective-permute-start.10) | collective-permute-done | bytes 49184 | tf_op jit(solution)/shard_map/ppermute | solution.py:240
  (46 shorter events, 16.1 us)
Async XLA Ops:
  2.9 31.7 %copy-start.5 = (s32[64,1,4]{0,2,1:T(4,128)S(1)}, s32[64,1,4]{0,2,1:T(4,128)}, u32[]{:S(2)}) copy-start(s32[64,1,4]{0,2,1:T(4,128)} %param.16) | copy-start | bytes 3076
  2.9 32.0 %copy-start = (bf16[384,1536]{1,0:T(8,128)(2,1)S(1)}, bf16[384,1536]{1,0:T(8,128)(2,1)}, u32[]{:S(2)}) copy-start(bf16[384,1536]{1,0:T(8,128)(2,1)} %weight.13) | copy-start | bytes 3538948
  32.7 4.8 %collective-permute-start = (bf16[32,32,384]{2,1,0:T(8,128)(2,1)S(1)}, bf16[32,32,384]{2,1,0:T(8,128)(2,1)S(1)}, u32[]{:S(2)}, u32[]{:S(2)}) collective-permute-start(bf16[32,32,384]{2,1,0:T(8,128)(2,1)S(1)} %all_to_all.20), channel_id=1, source_target_pairs={{0,1},{1,0},{2,3},{3,2},{4,5},{5,4},{6,7},{7,6},{8,9},{9,8},{10,11... | collective-permute-start | bytes 2359304 | tf_op jit(solution)/shard_map/ppermute | solution.py:198
  38.7 13.1 %collective-permute-start.2 = (bf16[8,64,512]{2,1,0:T(8,128)(2,1)S(1)}, bf16[8,64,512]{2,1,0:T(8,128)(2,1)S(1)}, u32[]{:S(2)}, u32[]{:S(2)}) collective-permute-start(bf16[8,64,512]{2,1,0:T(8,128)(2,1)S(1)} %bitcast.33), channel_id=1, source_target_pairs={{0,16},{1,49},{16,32},{17,1},{32,48},{33,17},{48,0},{49,33},{2,18}... | collective-permute-start | bytes 1572872 | tf_op jit(solution)/shard_map/ppermute | solution.py:205
  43.0 13.0 %collective-permute-start.1 = (bf16[8,64,512]{2,1,0:T(8,128)(2,1)S(1)}, bf16[8,64,512]{2,1,0:T(8,128)(2,1)S(1)}, u32[]{:S(2)}, u32[]{:S(2)}) collective-permute-start(bf16[8,64,512]{2,1,0:T(8,128)(2,1)S(1)} %bitcast.32), channel_id=1, source_target_pairs={{0,48},{1,17},{16,0},{17,33},{32,16},{33,49},{48,32},{49,1},{2,50}... | collective-permute-start | bytes 1572872 | tf_op jit(solution)/shard_map/ppermute | solution.py:206
  51.9 12.3 %collective-permute-start.3 = (bf16[8,64,512]{2,1,0:T(8,128)(2,1)S(1)}, bf16[8,64,512]{2,1,0:T(8,128)(2,1)S(1)}, u32[]{:S(2)}, u32[]{:S(2)}) collective-permute-start(bf16[8,64,512]{2,1,0:T(8,128)(2,1)S(1)} %fusion), channel_id=1, source_target_pairs={{0,16},{1,49},{16,32},{17,1},{32,48},{33,17},{48,0},{49,33},{2,18}... | collective-permute-start | bytes 1572872 | tf_op jit(solution)/shard_map/ppermute | solution.py:208
  55.9 18.7 %copy-start.3 = (bf16[1536]{0:T(1024)(128)(2,1)S(1)}, bf16[1536]{0:T(1024)(128)(2,1)}, u32[]{:S(2)}) copy-start(bf16[1536]{0:T(1024)(128)(2,1)} %param.13) | copy-start | bytes 9220
  55.9 28.6 %copy-start.2 = (s32[64,1]{0,1:T(1,128)S(1)}, s32[64,1]{0,1:T(1,128)}, u32[]{:S(2)}) copy-start(s32[64,1]{0,1:T(1,128)} %param.17) | copy-start | bytes 772
  65.3 47.5 %copy-start.1 = (bf16[1536,384]{1,0:T(8,128)(2,1)S(1)}, bf16[1536,384]{1,0:T(8,128)(2,1)}, u32[]{:S(2)}) copy-start(bf16[1536,384]{1,0:T(8,128)(2,1)} %weight.17) | copy-start | bytes 3538948
  65.3 19.2 %all-to-all-start.1 = ((bf16[8,64,512]{2,1,0:T(8,128)(2,1)}), bf16[8,64,512]{2,1,0:T(8,128)(2,1)S(1)}, u32[]{:S(2)}, u32[]{:S(2)}) async-start(bf16[8,64,512]{2,1,0:T(8,128)(2,1)} %fusion.2), calls=%async_computation.1 | async-start | bytes 1048576 | tf_op jit(solution)/shard_map/all_to_all | solution.py:210
  100.9 19.0 %collective-permute-start.4 = (bf16[8,64,512]{2,1,0:T(8,128)(2,1)S(1)}, bf16[8,64,512]{2,1,0:T(8,128)(2,1)S(1)}, u32[]{:S(2)}, u32[]{:S(2)}) collective-permute-start(bf16[8,64,512]{2,1,0:T(8,128)(2,1)S(1)} %all_to_all.21.act), channel_id=1, source_target_pairs={{0,16},{1,49},{16,32},{17,1},{32,48},{33,17},{48,0},{49,33},{2,18}... | collective-permute-start | bytes 1572872 | tf_op jit(solution)/shard_map/ppermute | solution.py:215
  102.8 19.1 %collective-permute-start.7 = (bf16[8,64,512]{2,1,0:T(8,128)(2,1)S(1)}, bf16[8,64,512]{2,1,0:T(8,128)(2,1)S(1)}, u32[]{:S(2)}, u32[]{:S(2)}) collective-permute-start(bf16[8,64,512]{2,1,0:T(8,128)(2,1)S(1)} %all_to_all.21.act), channel_id=1, source_target_pairs={{0,48},{1,17},{16,0},{17,33},{32,16},{33,49},{48,32},{49,1},{2,50}... | collective-permute-start | bytes 1572872 | tf_op jit(solution)/shard_map/ppermute | solution.py:216
  119.9 14.1 %collective-permute-start.5 = (bf16[8,64,512]{2,1,0:T(8,128)(2,1)S(1)}, bf16[8,64,512]{2,1,0:T(8,128)(2,1)S(1)}, u32[]{:S(2)}, u32[]{:S(2)}) collective-permute-start(bf16[8,64,512]{2,1,0:T(8,128)(2,1)S(1)} %collective-permute-done.4.act), channel_id=1, source_target_pairs={{0,16},{1,49},{16,32},{17,1},{32,48},{33,17},{48,0},{49,33},{2,18}... | collective-permute-start | bytes 1572872 | tf_op jit(solution)/shard_map/ppermute | solution.py:219
  123.6 15.8 %collective-permute-start.8 = (bf16[8,64,384]{2,1,0:T(8,128)(2,1)S(1)}, bf16[8,64,384]{2,1,0:T(8,128)(2,1)S(1)}, u32[]{:S(2)}, u32[]{:S(2)}) collective-permute-start(bf16[8,64,384]{2,1,0:T(8,128)(2,1)S(1)} %down.7), channel_id=1, source_target_pairs={{0,1},{1,0},{2,3},{3,2},{4,5},{5,4},{6,7},{7,6},{8,9},{9,8},{10,11... | collective-permute-start | bytes 1179656 | tf_op jit(solution)/shard_map/ppermute | solution.py:222
  135.8 3.8 %collective-permute-start.6 = (bf16[8,64,384]{2,1,0:T(8,128)(2,1)S(1)}, bf16[8,64,384]{2,1,0:T(8,128)(2,1)S(1)}, u32[]{:S(2)}, u32[]{:S(2)}) collective-permute-start(bf16[8,64,384]{2,1,0:T(8,128)(2,1)S(1)} %get-tuple-element.26), channel_id=1, source_target_pairs={{0,1},{1,0},{2,3},{3,2},{4,5},{5,4},{6,7},{7,6},{8,9},{9,8},{10,11... | collective-permute-start | bytes 1179656 | tf_op jit(solution)/shard_map/ppermute | solution.py:224
  139.9 44.7 %copy-start.4 = (bf16[768]{0:T(1024)(128)(2,1)S(1)}, bf16[768]{0:T(1024)(128)(2,1)}, u32[]{:S(2)}) copy-start(bf16[768]{0:T(1024)(128)(2,1)} %param.15) | copy-start | bytes 4612
  169.6 15.0 %collective-permute-start.9 = (bf16[64,384]{1,0:T(8,128)(2,1)S(1)}, bf16[64,384]{1,0:T(8,128)(2,1)S(1)}, u32[]{:S(2)}, u32[]{:S(2)}) collective-permute-start(bf16[64,384]{1,0:T(8,128)(2,1)S(1)} %get-tuple-element.29), channel_id=1, source_target_pairs={{0,48},{1,16},{2,112},{3,80},{4,176},{5,144},{6,240},{7,208},{8,30... | collective-permute-start | bytes 147464 | tf_op jit(solution)/shard_map/ppermute | solution.py:241
  178.9 12.9 %collective-permute-start.10 = (bf16[64,384]{1,0:T(8,128)(2,1)S(1)}, bf16[64,384]{1,0:T(8,128)(2,1)S(1)}, u32[]{:S(2)}, u32[]{:S(2)}) collective-permute-start(bf16[64,384]{1,0:T(8,128)(2,1)S(1)} %get-tuple-element.30), channel_id=1, source_target_pairs={{0,0},{1,32},{2,64},{3,96},{4,128},{5,160},{6,192},{7,224},{8,256}... | collective-permute-start | bytes 147464 | tf_op jit(solution)/shard_map/ppermute | solution.py:240

commit v9 on v8

--- a/solution.py
+++ b/solution.py
@@ -177,6 +177,11 @@
 
 def pairs(steps):
     return [(x * NC + c, (x + steps[c]) % NX * NC + c) for x in range(NX) for c in range(NC)]
+
+
+def owners_sum(pair):
+    parts = lax.all_to_all(pair, "z", split_axis=0, concat_axis=0, tiled=True)
+    return jnp.sum(parts.astype(F32), axis=0).astype(BF16)
 
 
 def body(
@@ -220,25 +225,20 @@
     (odd_keep,) = down(1, 1, where, ids, near, down_weight)
     (odd_send,) = down(2, 1, where, ids, other_side, down_weight)
     odd_got = lax.ppermute(odd_send, "c", around(NC, 1))
+    odd_pair = (odd_keep.astype(F32) + odd_got.astype(F32)).astype(BF16)
+    even, odd_pair = lax.optimization_barrier((even, odd_pair))
+    odd_branch = owners_sum(odd_pair)
     even_keep, even_send = down(3, 2, where, ids, far, down_weight, even)
     even_got = lax.ppermute(even_send, "c", around(NC, 1))
-    pair = jnp.stack(
-        [
-            (kept.astype(F32) + got.astype(F32)).astype(BF16)
-            for kept, got in ((even_keep, even_got), (odd_keep, odd_got))
-        ],
-        axis=1,
-    ).reshape(NZ, 2 * ROW, PIECE)
-    pair = lax.all_to_all(pair, "z", split_axis=0, concat_axis=0, tiled=True)
-    branch = jnp.sum(pair.astype(F32), axis=0).astype(BF16)
+    even_branch = owners_sum((even_keep.astype(F32) + even_got.astype(F32)).astype(BF16))
 
     back = [[], []]
     for j, ys, xs, zs, cs in itertools.product(range(2), *map(range, (NY, NX, NZ, NC))):
         row = (zs + ys) % NY * NX + (xs - 2 * cs - j) % NX
         source = ((ys * NX + xs) * NZ + zs) * NC + cs
         back[j].append((source, row * NZ * NC + (ys * NX + xs) // 2))
-    first = lax.ppermute(branch[:ROW], ALL, back[0])
-    second = lax.ppermute(branch[ROW:], ALL, back[1])
+    first = lax.ppermute(even_branch, ALL, back[0])
+    second = lax.ppermute(odd_branch, ALL, back[1])
     summed = jnp.concatenate(
         [jnp.where(odd, second, first), jnp.where(odd, first, second)], axis=1
     ).astype(F32)

time: 194 us -> 196 us (1.010)
  the two profiles are of different devices: /device:TPU:176 before, /device:TPU:118 now
where the time goes in v9:
time: 196 us; the launch traced here: 195 us
  waiting for transfers between devices  72.2 us (37%)
  blocking collectives  49.1 us (25%)
  starting transfers between devices  49 us (25%)
  Pallas kernels  15.7 us (8%)
  other arithmetic  5.99 us (3%)
  local copies, waits for them, and re-layouts  2.84 us (1%)
    all_to_all x1, blocking collectives, body(): lax.all_to_all(normed, ('y', 'x'), split_axis=0, concat_axis=0, tiled=True)  28.7 us
    all_to_all x2, waiting for transfers between devices, owners_sum(): parts = lax.all_to_all(pair, 'z', split_axis=0, concat_axis=0, tiled=True)  20.4 us
    all_to_all x1, blocking collectives, body(): act = lax.all_to_all(act, 'y', split_axis=0, concat_axis=0, tiled=True)  20.3 us
    all_to_all x2, starting transfers between devices, owners_sum(): parts = lax.all_to_all(pair, 'z', split_axis=0, concat_axis=0, tiled=True)  14.7 us
    all_to_all x1, waiting for transfers between devices, body(): part = lax.all_to_all(part, 'y', split_axis=0, concat_axis=0, tiled=True)  13.7 us
    ppermute x1, waiting for transfers between devices, body(): first = lax.ppermute(even_branch, ALL, back[0])  13.7 us
    ppermute x1, waiting for transfers between devices, body(): other_side = lax.ppermute(act, ('x', 'c'), pairs(TURNS[2]))  10.2 us
    pallas_call x5, Pallas kernels, up(): pl.pallas_call(functools.partial(up_kernel, turns), out_shape=[shape] * l...  7.36 us
  transfers between devices with their start and end apart: 14, of which 9 were waited for; matrix products, arithmetic and copies ran while one was open for 2% of the time, Pallas kernels for 7%

profile of v9, /device:TPU:118, one launch (start us, length us, event | category | flops | bytes accessed | tf_op | source)
XLA Modules:
  0.0 195.1 jit_solution(8549219584106047941)
XLA Ops:
  3.6 28.7 %all_to_all.25 = bf16[32,32,384]{2,1,0:T(8,128)(2,1)S(1)} all-to-all(bf16[32,32,384]{2,1,0:T(8,128)(2,1)S(1)} %norm.1), channel_id=1, replica_groups=mesh['y'=8,'x'=4,'z'=8,'c'=2] {'y','x'}, dimensions={0} | all-to-all | bytes 1572864 | tf_op jit(solution)/shard_map/all_to_all | solution.py:202
  32.3 1.9 collective-permute-start
  34.5 2.6 %up_first.1 = (bf16[8,2,32,512]{3,2,1,0:T(8,128)(2,1)S(1)}, bf16[8,2,32,512]{3,2,1,0:T(8,128)(2,1)S(1)}, bf16[8,2,32,512]{3,2,1,0:T(8,128)(2,1)S(1)}, bf16[8,2,32,512]{3,2,1,0:T(8,128)(2,1)S(1)}) custom-call(s32[3]{0:T(128)S(1)} %add_add_fusion.1.at, s32[256]{0:T(256)S(1)} %reshape.30.ids, bf16[8,4,32,384]{3,2,1,0:T(8,128)(2,1)S(1)} %bitcast.26, ...), custom_call_target="tpu_custom_call" | custom-call | flops 1207959552 | tf_op jit(solution)/shard_map/up_first/pallas_call | solution.py:89
  38.3 2.8 %collective-permute-start.2 = (bf16[8,64,512]{2,1,0:T(8,128)(2,1)S(1)}, bf16[8,64,512]{2,1,0:T(8,128)(2,1)S(1)}, u32[]{:S(2)}, u32[]{:S(2)}) collective-permute-start(bf16[8,64,512]{2,1,0:T(8,128)(2,1)S(1)} %bitcast.28), channel_id=1, source_target_pairs={{0,16},{1,49},{16,32},{17,1},{32,48},{33,17},{48,0},{49,33},{2,18}... | collective-permute-start | bytes 1572872 | tf_op jit(solution)/shard_map/ppermute | solution.py:210
  42.3 3.1 %collective-permute-start.1 = (bf16[8,64,512]{2,1,0:T(8,128)(2,1)S(1)}, bf16[8,64,512]{2,1,0:T(8,128)(2,1)S(1)}, u32[]{:S(2)}, u32[]{:S(2)}) collective-permute-start(bf16[8,64,512]{2,1,0:T(8,128)(2,1)S(1)} %bitcast.27), channel_id=1, source_target_pairs={{0,48},{1,17},{16,0},{17,33},{32,16},{33,49},{48,32},{49,1},{2,50}... | collective-permute-start | bytes 1572872 | tf_op jit(solution)/shard_map/ppermute | solution.py:211
  46.6 5.1 %collective-permute-done.2 = bf16[8,64,512]{2,1,0:T(8,128)(2,1)S(1)} collective-permute-done((bf16[8,64,512]{2,1,0:T(8,128)(2,1)S(1)}, bf16[8,64,512]{2,1,0:T(8,128)(2,1)S(1)}, u32[]{:S(2)}, u32[]{:S(2)}) %collective-permute-start.2) | collective-permute-done | bytes 524320 | tf_op jit(solution)/shard_map/ppermute | solution.py:210
  51.9 2.5 %collective-permute-start.3 = (bf16[8,64,512]{2,1,0:T(8,128)(2,1)S(1)}, bf16[8,64,512]{2,1,0:T(8,128)(2,1)S(1)}, u32[]{:S(2)}, u32[]{:S(2)}) collective-permute-start(bf16[8,64,512]{2,1,0:T(8,128)(2,1)S(1)} %fusion), channel_id=1, source_target_pairs={{0,16},{1,49},{16,32},{17,1},{32,48},{33,17},{48,0},{49,33},{2,18}... | collective-permute-start | bytes 1572872 | tf_op jit(solution)/shard_map/ppermute | solution.py:213
  55.8 7.2 %collective-permute-done.3 = bf16[8,64,512]{2,1,0:T(8,128)(2,1)S(1)} collective-permute-done((bf16[8,64,512]{2,1,0:T(8,128)(2,1)S(1)}, bf16[8,64,512]{2,1,0:T(8,128)(2,1)S(1)}, u32[]{:S(2)}, u32[]{:S(2)}) %collective-permute-start.3) | collective-permute-done | bytes 524320 | tf_op jit(solution)/shard_map/ppermute | solution.py:213
  64.0 7.4 %all-to-all-start.1 = ((bf16[8,64,512]{2,1,0:T(8,128)(2,1)}), bf16[8,64,512]{2,1,0:T(8,128)(2,1)S(1)}, u32[]{:S(2)}, u32[]{:S(2)}) async-start(bf16[8,64,512]{2,1,0:T(8,128)(2,1)} %fusion.2), calls=%async_computation.1 | async-start | bytes 1048576 | tf_op jit(solution)/shard_map/all_to_all | solution.py:215
  71.4 13.7 %all-to-all-done.1.parts = bf16[8,64,512]{2,1,0:T(8,128)(2,1)S(1)} async-done(((bf16[8,64,512]{2,1,0:T(8,128)(2,1)}), bf16[8,64,512]{2,1,0:T(8,128)(2,1)S(1)}, u32[]{:S(2)}, u32[]{:S(2)}) %all-to-all-start.1) | async-done | bytes 524320 | tf_op jit(solution)/shard_map/all_to_all | solution.py:215
  85.9 20.3 %all_to_all.26.act = bf16[8,64,512]{2,1,0:T(8,128)(2,1)S(1)} all-to-all(bf16[8,64,512]{2,1,0:T(8,128)(2,1)S(1)} %act.1), channel_id=1, replica_groups=mesh['y'=8,'x'=4,'z'=8,'c'=2] {'y'}, dimensions={0} | all-to-all | bytes 1048576 | tf_op jit(solution)/shard_map/all_to_all | solution.py:219
  106.2 1.9 collective-permute-start.5
  108.1 5.1 %collective-permute-start.4 = (bf16[8,64,512]{2,1,0:T(8,128)(2,1)S(1)}, bf16[8,64,512]{2,1,0:T(8,128)(2,1)S(1)}, u32[]{:S(2)}, u32[]{:S(2)}) collective-permute-start(bf16[8,64,512]{2,1,0:T(8,128)(2,1)S(1)} %all_to_all.26.act), channel_id=1, source_target_pairs={{0,16},{1,49},{16,32},{17,1},{32,48},{33,17},{48,0},{49,33},{2,18}... | collective-permute-start | bytes 1572872 | tf_op jit(solution)/shard_map/ppermute | solution.py:220
  113.2 10.2 %collective-permute-done.5.act = bf16[8,64,512]{2,1,0:T(8,128)(2,1)S(1)} collective-permute-done((bf16[8,64,512]{2,1,0:T(8,128)(2,1)S(1)}, bf16[8,64,512]{2,1,0:T(8,128)(2,1)S(1)}, u32[]{:S(2)}, u32[]{:S(2)}) %collective-permute-start.5) | collective-permute-done | bytes 524320 | tf_op jit(solution)/shard_map/ppermute | solution.py:221
  125.2 1.9 collective-permute-start.6
  128.9 1.9 collective-permute-start.8
  133.4 9.9 %all-to-all-start.3 = ((bf16[8,64,384]{2,1,0:T(8,128)(2,1)}), bf16[8,64,384]{2,1,0:T(8,128)(2,1)}, u32[]{:S(2)}, u32[]{:S(2)}) async-start(bf16[8,64,384]{2,1,0:T(8,128)(2,1)} %add_convert_fusion.1), calls=%async_computation.3 | async-start | bytes 786432 | tf_op jit(solution)/shard_map/all_to_all | solution.py:183
  145.1 1.9 collective-permute-start.9
  149.6 7.7 %all-to-all-done.3 = bf16[8,64,384]{2,1,0:T(8,128)(2,1)} async-done(((bf16[8,64,384]{2,1,0:T(8,128)(2,1)}), bf16[8,64,384]{2,1,0:T(8,128)(2,1)}, u32[]{:S(2)}, u32[]{:S(2)}) %all-to-all-start.3) | async-done | bytes 393248 | tf_op jit(solution)/shard_map/all_to_all | solution.py:183
  157.3 4.8 %all-to-all-start.4 = ((bf16[8,64,384]{2,1,0:T(8,128)(2,1)}), bf16[8,64,384]{2,1,0:T(8,128)(2,1)S(1)}, u32[]{:S(2)}, u32[]{:S(2)}) async-start(bf16[8,64,384]{2,1,0:T(8,128)(2,1)} %add_convert_fusion), calls=%async_computation.4 | async-start | bytes 786432 | tf_op jit(solution)/shard_map/all_to_all | solution.py:183
  163.2 1.9 collective-permute-start.7
  165.1 12.7 %all-to-all-done.4 = bf16[8,64,384]{2,1,0:T(8,128)(2,1)S(1)} async-done(((bf16[8,64,384]{2,1,0:T(8,128)(2,1)}), bf16[8,64,384]{2,1,0:T(8,128)(2,1)S(1)}, u32[]{:S(2)}, u32[]{:S(2)}) %all-to-all-start.4) | async-done | bytes 393248 | tf_op jit(solution)/shard_map/all_to_all | solution.py:183
  177.9 1.9 collective-permute-start.10
  179.8 13.7 %collective-permute-done.10 = bf16[64,384]{1,0:T(8,128)(2,1)S(1)} collective-permute-done((bf16[64,384]{1,0:T(8,128)(2,1)S(1)}, bf16[64,384]{1,0:T(8,128)(2,1)S(1)}, u32[]{:S(2)}, u32[]{:S(2)}) %collective-permute-start.10) | collective-permute-done | bytes 49184 | tf_op jit(solution)/shard_map/ppermute | solution.py:240
  (47 shorter events, 23.8 us)
Async XLA Ops:
  2.9 31.4 %copy-start.5 = (s32[64,1,4]{0,2,1:T(4,128)S(1)}, s32[64,1,4]{0,2,1:T(4,128)}, u32[]{:S(2)}) copy-start(s32[64,1,4]{0,2,1:T(4,128)} %param.16) | copy-start | bytes 3076
  2.9 31.6 %copy-start = (bf16[384,1536]{1,0:T(8,128)(2,1)S(1)}, bf16[384,1536]{1,0:T(8,128)(2,1)}, u32[]{:S(2)}) copy-start(bf16[384,1536]{1,0:T(8,128)(2,1)} %weight.13) | copy-start | bytes 3538948
  32.3 4.8 %collective-permute-start = (bf16[32,32,384]{2,1,0:T(8,128)(2,1)S(1)}, bf16[32,32,384]{2,1,0:T(8,128)(2,1)S(1)}, u32[]{:S(2)}, u32[]{:S(2)}) collective-permute-start(bf16[32,32,384]{2,1,0:T(8,128)(2,1)S(1)} %all_to_all.25), channel_id=1, source_target_pairs={{0,1},{1,0},{2,3},{3,2},{4,5},{5,4},{6,7},{7,6},{8,9},{9,8},{10,11... | collective-permute-start | bytes 2359304 | tf_op jit(solution)/shard_map/ppermute | solution.py:203
  38.3 13.4 %collective-permute-start.2 = (bf16[8,64,512]{2,1,0:T(8,128)(2,1)S(1)}, bf16[8,64,512]{2,1,0:T(8,128)(2,1)S(1)}, u32[]{:S(2)}, u32[]{:S(2)}) collective-permute-start(bf16[8,64,512]{2,1,0:T(8,128)(2,1)S(1)} %bitcast.28), channel_id=1, source_target_pairs={{0,16},{1,49},{16,32},{17,1},{32,48},{33,17},{48,0},{49,33},{2,18}... | collective-permute-start | bytes 1572872 | tf_op jit(solution)/shard_map/ppermute | solution.py:210
  42.3 13.5 %collective-permute-start.1 = (bf16[8,64,512]{2,1,0:T(8,128)(2,1)S(1)}, bf16[8,64,512]{2,1,0:T(8,128)(2,1)S(1)}, u32[]{:S(2)}, u32[]{:S(2)}) collective-permute-start(bf16[8,64,512]{2,1,0:T(8,128)(2,1)S(1)} %bitcast.27), channel_id=1, source_target_pairs={{0,48},{1,17},{16,0},{17,33},{32,16},{33,49},{48,32},{49,1},{2,50}... | collective-permute-start | bytes 1572872 | tf_op jit(solution)/shard_map/ppermute | solution.py:211
  51.9 11.1 %collective-permute-start.3 = (bf16[8,64,512]{2,1,0:T(8,128)(2,1)S(1)}, bf16[8,64,512]{2,1,0:T(8,128)(2,1)S(1)}, u32[]{:S(2)}, u32[]{:S(2)}) collective-permute-start(bf16[8,64,512]{2,1,0:T(8,128)(2,1)S(1)} %fusion), channel_id=1, source_target_pairs={{0,16},{1,49},{16,32},{17,1},{32,48},{33,17},{48,0},{49,33},{2,18}... | collective-permute-start | bytes 1572872 | tf_op jit(solution)/shard_map/ppermute | solution.py:213
  55.5 15.9 %copy-start.3 = (bf16[1536]{0:T(1024)(128)(2,1)S(1)}, bf16[1536]{0:T(1024)(128)(2,1)}, u32[]{:S(2)}) copy-start(bf16[1536]{0:T(1024)(128)(2,1)} %param.13) | copy-start | bytes 9220
  55.5 29.6 %copy-start.2 = (s32[64,1]{0,1:T(1,128)S(1)}, s32[64,1]{0,1:T(1,128)}, u32[]{:S(2)}) copy-start(s32[64,1]{0,1:T(1,128)} %param.17) | copy-start | bytes 772
  64.0 59.4 %copy-start.1 = (bf16[1536,384]{1,0:T(8,128)(2,1)S(1)}, bf16[1536,384]{1,0:T(8,128)(2,1)}, u32[]{:S(2)}) copy-start(bf16[1536,384]{1,0:T(8,128)(2,1)} %weight.17) | copy-start | bytes 3538948
  64.0 21.2 %all-to-all-start.1 = ((bf16[8,64,512]{2,1,0:T(8,128)(2,1)}), bf16[8,64,512]{2,1,0:T(8,128)(2,1)S(1)}, u32[]{:S(2)}, u32[]{:S(2)}) async-start(bf16[8,64,512]{2,1,0:T(8,128)(2,1)} %fusion.2), calls=%async_computation.1 | async-start | bytes 1048576 | tf_op jit(solution)/shard_map/all_to_all | solution.py:215
  106.2 17.2 %collective-permute-start.5 = (bf16[8,64,512]{2,1,0:T(8,128)(2,1)S(1)}, bf16[8,64,512]{2,1,0:T(8,128)(2,1)S(1)}, u32[]{:S(2)}, u32[]{:S(2)}) collective-permute-start(bf16[8,64,512]{2,1,0:T(8,128)(2,1)S(1)} %all_to_all.26.act), channel_id=1, source_target_pairs={{0,48},{1,17},{16,0},{17,33},{32,16},{33,49},{48,32},{49,1},{2,50}... | collective-permute-start | bytes 1572872 | tf_op jit(solution)/shard_map/ppermute | solution.py:221
  108.1 20.8 %collective-permute-start.4 = (bf16[8,64,512]{2,1,0:T(8,128)(2,1)S(1)}, bf16[8,64,512]{2,1,0:T(8,128)(2,1)S(1)}, u32[]{:S(2)}, u32[]{:S(2)}) collective-permute-start(bf16[8,64,512]{2,1,0:T(8,128)(2,1)S(1)} %all_to_all.26.act), channel_id=1, source_target_pairs={{0,16},{1,49},{16,32},{17,1},{32,48},{33,17},{48,0},{49,33},{2,18}... | collective-permute-start | bytes 1572872 | tf_op jit(solution)/shard_map/ppermute | solution.py:220
  125.2 7.4 %collective-permute-start.6 = (bf16[8,64,384]{2,1,0:T(8,128)(2,1)S(1)}, bf16[8,64,384]{2,1,0:T(8,128)(2,1)S(1)}, u32[]{:S(2)}, u32[]{:S(2)}) collective-permute-start(bf16[8,64,384]{2,1,0:T(8,128)(2,1)S(1)} %down.6), channel_id=1, source_target_pairs={{0,1},{1,0},{2,3},{3,2},{4,5},{5,4},{6,7},{7,6},{8,9},{9,8},{10,11... | collective-permute-start | bytes 1179656 | tf_op jit(solution)/shard_map/ppermute | solution.py:227
  128.9 14.4 %collective-permute-start.8 = (bf16[8,64,512]{2,1,0:T(8,128)(2,1)S(1)}, bf16[8,64,512]{2,1,0:T(8,128)(2,1)S(1)}, u32[]{:S(2)}, u32[]{:S(2)}) collective-permute-start(bf16[8,64,512]{2,1,0:T(8,128)(2,1)S(1)} %collective-permute-done.4.act), channel_id=1, source_target_pairs={{0,16},{1,49},{16,32},{17,1},{32,48},{33,17},{48,0},{49,33},{2,18}... | collective-permute-start | bytes 1572872 | tf_op jit(solution)/shard_map/ppermute | solution.py:224
  133.4 23.9 %all-to-all-start.3 = ((bf16[8,64,384]{2,1,0:T(8,128)(2,1)}), bf16[8,64,384]{2,1,0:T(8,128)(2,1)}, u32[]{:S(2)}, u32[]{:S(2)}) async-start(bf16[8,64,384]{2,1,0:T(8,128)(2,1)} %add_convert_fusion.1), calls=%async_computation.3 | async-start | bytes 786432 | tf_op jit(solution)/shard_map/all_to_all | solution.py:183
  145.1 34.7 %copy-start.4 = (bf16[768]{0:T(1024)(128)(2,1)S(1)}, bf16[768]{0:T(1024)(128)(2,1)}, u32[]{:S(2)}) copy-start(bf16[768]{0:T(1024)(128)(2,1)} %param.15) | copy-start | bytes 4612
  145.1 3.6 %collective-permute-start.9 = (bf16[8,64,384]{2,1,0:T(8,128)(2,1)S(1)}, bf16[8,64,384]{2,1,0:T(8,128)(2,1)S(1)}, u32[]{:S(2)}, u32[]{:S(2)}) collective-permute-start(bf16[8,64,384]{2,1,0:T(8,128)(2,1)S(1)} %get-tuple-element.32), channel_id=1, source_target_pairs={{0,1},{1,0},{2,3},{3,2},{4,5},{5,4},{6,7},{7,6},{8,9},{9,8},{10,11... | collective-permute-start | bytes 1179656 | tf_op jit(solution)/shard_map/ppermute | solution.py:232
  157.3 20.5 %all-to-all-start.4 = ((bf16[8,64,384]{2,1,0:T(8,128)(2,1)}), bf16[8,64,384]{2,1,0:T(8,128)(2,1)S(1)}, u32[]{:S(2)}, u32[]{:S(2)}) async-start(bf16[8,64,384]{2,1,0:T(8,128)(2,1)} %add_convert_fusion), calls=%async_computation.4 | async-start | bytes 786432 | tf_op jit(solution)/shard_map/all_to_all | solution.py:183
  163.2 16.6 %collective-permute-start.7 = (bf16[64,384]{1,0:T(8,128)(2,1)S(1)}, bf16[64,384]{1,0:T(8,128)(2,1)S(1)}, u32[]{:S(2)}, u32[]{:S(2)}) collective-permute-start(bf16[64,384]{1,0:T(8,128)(2,1)S(1)} %reduce_sum.24), channel_id=1, source_target_pairs={{0,48},{1,16},{2,112},{3,80},{4,176},{5,144},{6,240},{7,208},{8,30... | collective-permute-start | bytes 147464 | tf_op jit(solution)/shard_map/ppermute | solution.py:241
  177.9 15.6 %collective-permute-start.10 = (bf16[64,384]{1,0:T(8,128)(2,1)S(1)}, bf16[64,384]{1,0:T(8,128)(2,1)S(1)}, u32[]{:S(2)}, u32[]{:S(2)}) collective-permute-start(bf16[64,384]{1,0:T(8,128)(2,1)S(1)} %reduce_sum.25), channel_id=1, source_target_pairs={{0,0},{1,32},{2,64},{3,96},{4,128},{5,160},{6,192},{7,224},{8,256}... | collective-permute-start | bytes 147464 | tf_op jit(solution)/shard_map/ppermute | solution.py:240

commit v10 on v8

--- a/solution.py
+++ b/solution.py
@@ -31,6 +31,8 @@
 def norm_kernel(hidden, scales, out):
     rows, features = hidden.shape
     pieces = features // PIECE
+    gains = scales[:features].astype(F32).reshape(1, features)
+    shifts = scales[features:].astype(F32).reshape(1, features)
 
     def piece(p):
         return hidden[:, p * PIECE : (p + 1) * PIECE].astype(F32)
@@ -47,7 +49,7 @@
     scale = lax.rsqrt(spread + 1e-05)
     for p in range(pieces):
         at = slice(p * PIECE, (p + 1) * PIECE)
-        value = (piece(p) - mean) * scale * scales[0:1, at] + scales[1:2, at]
+        value = (piece(p) - mean) * scale * gains[:, at] + shifts[:, at]
         out[p] = value.astype(BF16)
 
 
@@ -192,7 +194,7 @@
 
     mine = jnp.stack([c, x, c]).astype(jnp.int32)
     others = jnp.stack([1 - c, x, c]).astype(jnp.int32)
-    scales = jnp.stack([norm_gain, norm_shift]).astype(F32)
+    scales = jnp.concatenate([norm_gain, norm_shift])
     normed = norm(lax.dynamic_slice_in_dim(hidden_in, c * GROUP, GROUP, 0), scales)
     own = lax.all_to_all(normed, ("y", "x"), split_axis=0, concat_axis=0, tiled=True)
     other = lax.ppermute(own, "c", around(NC, 1))
@@ -232,6 +234,8 @@
     pair = lax.all_to_all(pair, "z", split_axis=0, concat_axis=0, tiled=True)
     branch = jnp.sum(pair.astype(F32), axis=0).astype(BF16)
 
+    resid = lax.dynamic_slice_in_dim(hidden_in, t * width, width, 1).astype(F32)
+    base, branch = lax.optimization_barrier((resid + down_bias.astype(F32), branch))
     back = [[], []]
     for j, ys, xs, zs, cs in itertools.product(range(2), *map(range, (NY, NX, NZ, NC))):
         row = (zs + ys) % NY * NX + (xs - 2 * cs - j) % NX
@@ -242,8 +246,7 @@
     summed = jnp.concatenate(
         [jnp.where(odd, second, first), jnp.where(odd, first, second)], axis=1
     ).astype(F32)
-    resid = lax.dynamic_slice_in_dim(hidden_in, t * width, width, 1).astype(F32)
-    return (resid + summed + down_bias.astype(F32)).astype(BF16)
+    return (base + summed).astype(BF16)
 
 
 def solution(mesh):

time: 194 us -> 194 us (level)
  blocking collectives: 74.4 us -> 44.8 us
  waiting for transfers between devices: 40.8 us -> 61.1 us
  starting transfers between devices: 55.8 us -> 63.9 us
    all_to_all x1 -> x0, blocking collectives: 29.6 us -> none  [body(): pair = lax.all_to_all(pair, 'z', split_axis=0, concat_axis=0, tiled=True)]
    all_to_all x0 -> x1, waiting for transfers between devices: none -> 20.4 us  [body(): pair = lax.all_to_all(pair, 'z', split_axis=0, concat_axis=0, tiled=True)]
    all_to_all x0 -> x1, starting transfers between devices: none -> 9.08 us  [body(): pair = lax.all_to_all(pair, 'z', split_axis=0, concat_axis=0, tiled=True)]
    ppermute x1, waiting for transfers between devices: 7.27 us -> 0.01 us  [body(): first = lax.ppermute(branch[:ROW], ALL, back[0])]
    ppermute x1, waiting for transfers between devices: 0.01 us -> 7.16 us  [body(): second = lax.ppermute(branch[ROW:], ALL, back[1])]
    ppermute x1, starting transfers between devices: 9.33 us -> 6.62 us  [body(): second = lax.ppermute(branch[ROW:], ALL, back[1])]
  transfers between devices with their start and end apart: 12 -> 13, of which waited for: 7 -> 8; matrix products, arithmetic and copies ran while one was open for 0% -> 1% of each run, Pallas kernels for 7% -> 7%
where the time goes in v10:
time: 194 us; the launch traced here: 192 us
  starting transfers between devices  63.9 us (33%)
  waiting for transfers between devices  61.1 us (31%)
  blocking collectives  44.8 us (23%)
  Pallas kernels  15.7 us (8%)
  other arithmetic  3.46 us (2%)
  local copies, waits for them, and re-layouts  2.3 us (1%)
    all_to_all x1, blocking collectives, body(): lax.all_to_all(normed, ('y', 'x'), split_axis=0, concat_axis=0, tiled=True)  29.1 us
    all_to_all x1, waiting for transfers between devices, body(): pair = lax.all_to_all(pair, 'z', split_axis=0, concat_axis=0, tiled=True)  20.4 us
    all_to_all x1, blocking collectives, body(): act = lax.all_to_all(act, 'y', split_axis=0, concat_axis=0, tiled=True)  15.7 us
    ppermute x1, starting transfers between devices, body(): other_side = lax.ppermute(act, ('x', 'c'), pairs(TURNS[2]))  9.97 us
    all_to_all x1, waiting for transfers between devices, body(): part = lax.all_to_all(part, 'y', split_axis=0, concat_axis=0, tiled=True)  9.89 us
    all_to_all x1, starting transfers between devices, body(): part = lax.all_to_all(part, 'y', split_axis=0, concat_axis=0, tiled=True)  9.26 us
    all_to_all x1, starting transfers between devices, body(): pair = lax.all_to_all(pair, 'z', split_axis=0, concat_axis=0, tiled=True)  9.08 us
    ppermute x1, waiting for transfers between devices, body(): joined = lax.ppermute(joined, ('x', 'c'), pairs(LEAVES[2]))  8.28 us
  transfers between devices with their start and end apart: 13, of which 8 were waited for; matrix products, arithmetic and copies ran while one was open for 1% of the time, Pallas kernels for 7%

profile of v10, /device:TPU:176, one launch (start us, length us, event | category | flops | bytes accessed | tf_op | source)
XLA Modules:
  0.0 191.6 jit_solution(10639448913248972392)
XLA Ops:
  2.0 29.1 %all_to_all.20 = bf16[32,32,384]{2,1,0:T(8,128)(2,1)S(1)} all-to-all(bf16[32,32,384]{2,1,0:T(8,128)(2,1)S(1)} %norm.1), channel_id=1, replica_groups=mesh['y'=8,'x'=4,'z'=8,'c'=2] {'y','x'}, dimensions={0} | all-to-all | bytes 1572864 | tf_op jit(solution)/shard_map/all_to_all | solution.py:199
  31.1 1.9 collective-permute-start
  33.3 2.6 %up_first.1 = (bf16[8,2,32,512]{3,2,1,0:T(8,128)(2,1)S(1)}, bf16[8,2,32,512]{3,2,1,0:T(8,128)(2,1)S(1)}, bf16[8,2,32,512]{3,2,1,0:T(8,128)(2,1)S(1)}, bf16[8,2,32,512]{3,2,1,0:T(8,128)(2,1)S(1)}) custom-call(s32[3]{0:T(128)S(1)} %add_add_fusion.1.at, s32[256]{0:T(256)S(1)} %reshape.33.ids, bf16[8,4,32,384]{3,2,1,0:T(8,128)(2,1)S(1)} %bitcast.31, ...), custom_call_target="tpu_custom_call" | custom-call | flops 1207959552 | tf_op jit(solution)/shard_map/up_first/pallas_call | solution.py:91
  37.1 3.1 %collective-permute-start.2 = (bf16[8,64,512]{2,1,0:T(8,128)(2,1)S(1)}, bf16[8,64,512]{2,1,0:T(8,128)(2,1)S(1)}, u32[]{:S(2)}, u32[]{:S(2)}) collective-permute-start(bf16[8,64,512]{2,1,0:T(8,128)(2,1)S(1)} %bitcast.33), channel_id=1, source_target_pairs={{0,16},{1,49},{16,32},{17,1},{32,48},{33,17},{48,0},{49,33},{2,18}... | collective-permute-start | bytes 1572872 | tf_op jit(solution)/shard_map/ppermute | solution.py:207
  41.4 4.0 %collective-permute-start.1 = (bf16[8,64,512]{2,1,0:T(8,128)(2,1)S(1)}, bf16[8,64,512]{2,1,0:T(8,128)(2,1)S(1)}, u32[]{:S(2)}, u32[]{:S(2)}) collective-permute-start(bf16[8,64,512]{2,1,0:T(8,128)(2,1)S(1)} %bitcast.32), channel_id=1, source_target_pairs={{0,48},{1,17},{16,0},{17,33},{32,16},{33,49},{48,32},{49,1},{2,50}... | collective-permute-start | bytes 1572872 | tf_op jit(solution)/shard_map/ppermute | solution.py:208
  46.6 3.6 %collective-permute-done.2 = bf16[8,64,512]{2,1,0:T(8,128)(2,1)S(1)} collective-permute-done((bf16[8,64,512]{2,1,0:T(8,128)(2,1)S(1)}, bf16[8,64,512]{2,1,0:T(8,128)(2,1)S(1)}, u32[]{:S(2)}, u32[]{:S(2)}) %collective-permute-start.2) | collective-permute-done | bytes 524320 | tf_op jit(solution)/shard_map/ppermute | solution.py:207
  50.4 2.8 %collective-permute-start.3 = (bf16[8,64,512]{2,1,0:T(8,128)(2,1)S(1)}, bf16[8,64,512]{2,1,0:T(8,128)(2,1)S(1)}, u32[]{:S(2)}, u32[]{:S(2)}) collective-permute-start(bf16[8,64,512]{2,1,0:T(8,128)(2,1)S(1)} %fusion), channel_id=1, source_target_pairs={{0,16},{1,49},{16,32},{17,1},{32,48},{33,17},{48,0},{49,33},{2,18}... | collective-permute-start | bytes 1572872 | tf_op jit(solution)/shard_map/ppermute | solution.py:210
  54.4 8.3 %collective-permute-done.3 = bf16[8,64,512]{2,1,0:T(8,128)(2,1)S(1)} collective-permute-done((bf16[8,64,512]{2,1,0:T(8,128)(2,1)S(1)}, bf16[8,64,512]{2,1,0:T(8,128)(2,1)S(1)}, u32[]{:S(2)}, u32[]{:S(2)}) %collective-permute-start.3) | collective-permute-done | bytes 524320 | tf_op jit(solution)/shard_map/ppermute | solution.py:210
  63.8 9.3 %all-to-all-start.1 = ((bf16[8,64,512]{2,1,0:T(8,128)(2,1)}), bf16[8,64,512]{2,1,0:T(8,128)(2,1)S(1)}, u32[]{:S(2)}, u32[]{:S(2)}) async-start(bf16[8,64,512]{2,1,0:T(8,128)(2,1)} %fusion.2), calls=%async_computation.1 | async-start | bytes 1048576 | tf_op jit(solution)/shard_map/all_to_all | solution.py:212
  73.1 9.9 %all-to-all-done.1.parts = bf16[8,64,512]{2,1,0:T(8,128)(2,1)S(1)} async-done(((bf16[8,64,512]{2,1,0:T(8,128)(2,1)}), bf16[8,64,512]{2,1,0:T(8,128)(2,1)S(1)}, u32[]{:S(2)}, u32[]{:S(2)}) %all-to-all-start.1) | async-done | bytes 524320 | tf_op jit(solution)/shard_map/all_to_all | solution.py:212
  83.7 15.7 %all_to_all.21.act = bf16[8,64,512]{2,1,0:T(8,128)(2,1)S(1)} all-to-all(bf16[8,64,512]{2,1,0:T(8,128)(2,1)S(1)} %act.1), channel_id=1, replica_groups=mesh['y'=8,'x'=4,'z'=8,'c'=2] {'y'}, dimensions={0} | all-to-all | bytes 1048576 | tf_op jit(solution)/shard_map/all_to_all | solution.py:216
  99.3 1.9 collective-permute-start.4
  101.2 10.0 %collective-permute-start.7 = (bf16[8,64,512]{2,1,0:T(8,128)(2,1)S(1)}, bf16[8,64,512]{2,1,0:T(8,128)(2,1)S(1)}, u32[]{:S(2)}, u32[]{:S(2)}) collective-permute-start(bf16[8,64,512]{2,1,0:T(8,128)(2,1)S(1)} %all_to_all.21.act), channel_id=1, source_target_pairs={{0,48},{1,17},{16,0},{17,33},{32,16},{33,49},{48,32},{49,1},{2,50}... | collective-permute-start | bytes 1572872 | tf_op jit(solution)/shard_map/ppermute | solution.py:218
  111.2 1.8 down.4
  113.0 5.4 %collective-permute-done.4.act = bf16[8,64,512]{2,1,0:T(8,128)(2,1)S(1)} collective-permute-done((bf16[8,64,512]{2,1,0:T(8,128)(2,1)S(1)}, bf16[8,64,512]{2,1,0:T(8,128)(2,1)S(1)}, u32[]{:S(2)}, u32[]{:S(2)}) %collective-permute-start.4) | collective-permute-done | bytes 524320 | tf_op jit(solution)/shard_map/ppermute | solution.py:217
  118.4 1.9 collective-permute-start.5
  122.1 4.1 %collective-permute-start.8 = (bf16[8,64,384]{2,1,0:T(8,128)(2,1)S(1)}, bf16[8,64,384]{2,1,0:T(8,128)(2,1)S(1)}, u32[]{:S(2)}, u32[]{:S(2)}) collective-permute-start(bf16[8,64,384]{2,1,0:T(8,128)(2,1)S(1)} %down.7), channel_id=1, source_target_pairs={{0,1},{1,0},{2,3},{3,2},{4,5},{5,4},{6,7},{7,6},{8,9},{9,8},{10,11... | collective-permute-start | bytes 1179656 | tf_op jit(solution)/shard_map/ppermute | solution.py:224
  126.2 6.3 %collective-permute-done.5.act = bf16[8,64,512]{2,1,0:T(8,128)(2,1)S(1)} collective-permute-done((bf16[8,64,512]{2,1,0:T(8,128)(2,1)S(1)}, bf16[8,64,512]{2,1,0:T(8,128)(2,1)S(1)}, u32[]{:S(2)}, u32[]{:S(2)}) %collective-permute-start.5) | collective-permute-done | bytes 524320 | tf_op jit(solution)/shard_map/ppermute | solution.py:221
  134.2 1.9 %collective-permute-start.6 = (bf16[8,64,384]{2,1,0:T(8,128)(2,1)S(1)}, bf16[8,64,384]{2,1,0:T(8,128)(2,1)S(1)}, u32[]{:S(2)}, u32[]{:S(2)}) collective-permute-start(bf16[8,64,384]{2,1,0:T(8,128)(2,1)S(1)} %get-tuple-element.28), channel_id=1, source_target_pairs={{0,1},{1,0},{2,3},{3,2},{4,5},{5,4},{6,7},{7,6},{8,9},{9,8},{10,11... | collective-permute-start | bytes 1179656 | tf_op jit(solution)/shard_map/ppermute | solution.py:226
  139.2 9.1 %all-to-all-start.3 = ((bf16[8,128,384]{2,1,0:T(8,128)(2,1)}), bf16[8,128,384]{2,1,0:T(8,128)(2,1)S(1)}, u32[]{:S(2)}, u32[]{:S(2)}) async-start(bf16[8,128,384]{2,1,0:T(8,128)(2,1)} %bitcast.17), calls=%async_computation.3 | async-start | bytes 1572864 | tf_op jit(solution)/shard_map/all_to_all | solution.py:234
  149.2 20.4 %all-to-all-done.3 = bf16[8,128,384]{2,1,0:T(8,128)(2,1)S(1)} async-done(((bf16[8,128,384]{2,1,0:T(8,128)(2,1)}), bf16[8,128,384]{2,1,0:T(8,128)(2,1)S(1)}, u32[]{:S(2)}, u32[]{:S(2)}) %all-to-all-start.3) | async-done | bytes 786464 | tf_op jit(solution)/shard_map/all_to_all | solution.py:234
  169.7 7.4 %collective-permute-start.10 = (bf16[64,384]{1,0:T(8,128)(2,1)S(1)}, bf16[64,384]{1,0:T(8,128)(2,1)S(1)}, u32[]{:S(2)}, u32[]{:S(2)}) collective-permute-start(bf16[64,384]{1,0:T(8,128)(2,1)S(1)} %get-tuple-element.34), channel_id=1, source_target_pairs={{0,0},{1,32},{2,64},{3,96},{4,128},{5,160},{6,192},{7,224},{8,256}... | collective-permute-start | bytes 147464 | tf_op jit(solution)/shard_map/ppermute | solution.py:244
  177.1 6.6 %collective-permute-start.9 = (bf16[64,384]{1,0:T(8,128)(2,1)S(1)}, bf16[64,384]{1,0:T(8,128)(2,1)S(1)}, u32[]{:S(2)}, u32[]{:S(2)}) collective-permute-start(bf16[64,384]{1,0:T(8,128)(2,1)S(1)} %get-tuple-element.33), channel_id=1, source_target_pairs={{0,48},{1,16},{2,112},{3,80},{4,176},{5,144},{6,240},{7,208},{8,30... | collective-permute-start | bytes 147464 | tf_op jit(solution)/shard_map/ppermute | solution.py:245
  183.8 7.2 %collective-permute-done.9 = bf16[64,384]{1,0:T(8,128)(2,1)S(1)} collective-permute-done((bf16[64,384]{1,0:T(8,128)(2,1)S(1)}, bf16[64,384]{1,0:T(8,128)(2,1)S(1)}, u32[]{:S(2)}, u32[]{:S(2)}) %collective-permute-start.9) | collective-permute-done | bytes 49184 | tf_op jit(solution)/shard_map/ppermute | solution.py:245
  (50 shorter events, 17.2 us)
Async XLA Ops:
  0.0 1.2 copy-start.4
  0.0 1.2 copy-start.3
  1.2 31.8 %copy-start.7 = (s32[64,1,4]{0,2,1:T(4,128)S(1)}, s32[64,1,4]{0,2,1:T(4,128)}, u32[]{:S(2)}) copy-start(s32[64,1,4]{0,2,1:T(4,128)} %param.16) | copy-start | bytes 3076
  1.2 32.0 %copy-start = (bf16[384,1536]{1,0:T(8,128)(2,1)S(1)}, bf16[384,1536]{1,0:T(8,128)(2,1)}, u32[]{:S(2)}) copy-start(bf16[384,1536]{1,0:T(8,128)(2,1)} %weight.13) | copy-start | bytes 3538948
  31.1 4.8 %collective-permute-start = (bf16[32,32,384]{2,1,0:T(8,128)(2,1)S(1)}, bf16[32,32,384]{2,1,0:T(8,128)(2,1)S(1)}, u32[]{:S(2)}, u32[]{:S(2)}) collective-permute-start(bf16[32,32,384]{2,1,0:T(8,128)(2,1)S(1)} %all_to_all.20), channel_id=1, source_target_pairs={{0,1},{1,0},{2,3},{3,2},{4,5},{5,4},{6,7},{7,6},{8,9},{9,8},{10,11... | collective-permute-start | bytes 2359304 | tf_op jit(solution)/shard_map/ppermute | solution.py:200
  37.1 13.1 %collective-permute-start.2 = (bf16[8,64,512]{2,1,0:T(8,128)(2,1)S(1)}, bf16[8,64,512]{2,1,0:T(8,128)(2,1)S(1)}, u32[]{:S(2)}, u32[]{:S(2)}) collective-permute-start(bf16[8,64,512]{2,1,0:T(8,128)(2,1)S(1)} %bitcast.33), channel_id=1, source_target_pairs={{0,16},{1,49},{16,32},{17,1},{32,48},{33,17},{48,0},{49,33},{2,18}... | collective-permute-start | bytes 1572872 | tf_op jit(solution)/shard_map/ppermute | solution.py:207
  41.4 13.0 %collective-permute-start.1 = (bf16[8,64,512]{2,1,0:T(8,128)(2,1)S(1)}, bf16[8,64,512]{2,1,0:T(8,128)(2,1)S(1)}, u32[]{:S(2)}, u32[]{:S(2)}) collective-permute-start(bf16[8,64,512]{2,1,0:T(8,128)(2,1)S(1)} %bitcast.32), channel_id=1, source_target_pairs={{0,48},{1,17},{16,0},{17,33},{32,16},{33,49},{48,32},{49,1},{2,50}... | collective-permute-start | bytes 1572872 | tf_op jit(solution)/shard_map/ppermute | solution.py:208
  50.4 12.3 %collective-permute-start.3 = (bf16[8,64,512]{2,1,0:T(8,128)(2,1)S(1)}, bf16[8,64,512]{2,1,0:T(8,128)(2,1)S(1)}, u32[]{:S(2)}, u32[]{:S(2)}) collective-permute-start(bf16[8,64,512]{2,1,0:T(8,128)(2,1)S(1)} %fusion), channel_id=1, source_target_pairs={{0,16},{1,49},{16,32},{17,1},{32,48},{33,17},{48,0},{49,33},{2,18}... | collective-permute-start | bytes 1572872 | tf_op jit(solution)/shard_map/ppermute | solution.py:210
  54.4 18.7 %copy-start.5 = (bf16[1536]{0:T(1024)(128)(2,1)S(1)}, bf16[1536]{0:T(1024)(128)(2,1)}, u32[]{:S(2)}) copy-start(bf16[1536]{0:T(1024)(128)(2,1)} %param.13) | copy-start | bytes 9220
  54.4 28.6 %copy-start.2 = (s32[64,1]{0,1:T(1,128)S(1)}, s32[64,1]{0,1:T(1,128)}, u32[]{:S(2)}) copy-start(s32[64,1]{0,1:T(1,128)} %param.17) | copy-start | bytes 772
  63.8 47.5 %copy-start.1 = (bf16[1536,384]{1,0:T(8,128)(2,1)S(1)}, bf16[1536,384]{1,0:T(8,128)(2,1)}, u32[]{:S(2)}) copy-start(bf16[1536,384]{1,0:T(8,128)(2,1)} %weight.17) | copy-start | bytes 3538948
  63.8 19.2 %all-to-all-start.1 = ((bf16[8,64,512]{2,1,0:T(8,128)(2,1)}), bf16[8,64,512]{2,1,0:T(8,128)(2,1)S(1)}, u32[]{:S(2)}, u32[]{:S(2)}) async-start(bf16[8,64,512]{2,1,0:T(8,128)(2,1)} %fusion.2), calls=%async_computation.1 | async-start | bytes 1048576 | tf_op jit(solution)/shard_map/all_to_all | solution.py:212
  99.3 19.0 %collective-permute-start.4 = (bf16[8,64,512]{2,1,0:T(8,128)(2,1)S(1)}, bf16[8,64,512]{2,1,0:T(8,128)(2,1)S(1)}, u32[]{:S(2)}, u32[]{:S(2)}) collective-permute-start(bf16[8,64,512]{2,1,0:T(8,128)(2,1)S(1)} %all_to_all.21.act), channel_id=1, source_target_pairs={{0,16},{1,49},{16,32},{17,1},{32,48},{33,17},{48,0},{49,33},{2,18}... | collective-permute-start | bytes 1572872 | tf_op jit(solution)/shard_map/ppermute | solution.py:217
  101.2 19.1 %collective-permute-start.7 = (bf16[8,64,512]{2,1,0:T(8,128)(2,1)S(1)}, bf16[8,64,512]{2,1,0:T(8,128)(2,1)S(1)}, u32[]{:S(2)}, u32[]{:S(2)}) collective-permute-start(bf16[8,64,512]{2,1,0:T(8,128)(2,1)S(1)} %all_to_all.21.act), channel_id=1, source_target_pairs={{0,48},{1,17},{16,0},{17,33},{32,16},{33,49},{48,32},{49,1},{2,50}... | collective-permute-start | bytes 1572872 | tf_op jit(solution)/shard_map/ppermute | solution.py:218
  118.4 14.1 %collective-permute-start.5 = (bf16[8,64,512]{2,1,0:T(8,128)(2,1)S(1)}, bf16[8,64,512]{2,1,0:T(8,128)(2,1)S(1)}, u32[]{:S(2)}, u32[]{:S(2)}) collective-permute-start(bf16[8,64,512]{2,1,0:T(8,128)(2,1)S(1)} %collective-permute-done.4.act), channel_id=1, source_target_pairs={{0,16},{1,49},{16,32},{17,1},{32,48},{33,17},{48,0},{49,33},{2,18}... | collective-permute-start | bytes 1572872 | tf_op jit(solution)/shard_map/ppermute | solution.py:221
  122.1 15.8 %collective-permute-start.8 = (bf16[8,64,384]{2,1,0:T(8,128)(2,1)S(1)}, bf16[8,64,384]{2,1,0:T(8,128)(2,1)S(1)}, u32[]{:S(2)}, u32[]{:S(2)}) collective-permute-start(bf16[8,64,384]{2,1,0:T(8,128)(2,1)S(1)} %down.7), channel_id=1, source_target_pairs={{0,1},{1,0},{2,3},{3,2},{4,5},{5,4},{6,7},{7,6},{8,9},{9,8},{10,11... | collective-permute-start | bytes 1179656 | tf_op jit(solution)/shard_map/ppermute | solution.py:224
  134.2 3.8 %collective-permute-start.6 = (bf16[8,64,384]{2,1,0:T(8,128)(2,1)S(1)}, bf16[8,64,384]{2,1,0:T(8,128)(2,1)S(1)}, u32[]{:S(2)}, u32[]{:S(2)}) collective-permute-start(bf16[8,64,384]{2,1,0:T(8,128)(2,1)S(1)} %get-tuple-element.28), channel_id=1, source_target_pairs={{0,1},{1,0},{2,3},{3,2},{4,5},{5,4},{6,7},{7,6},{8,9},{9,8},{10,11... | collective-permute-start | bytes 1179656 | tf_op jit(solution)/shard_map/ppermute | solution.py:226
  138.2 10.1 %copy-start.6 = (bf16[768]{0:T(1024)(128)(2,1)S(1)}, bf16[768]{0:T(1024)(128)(2,1)}, u32[]{:S(2)}) copy-start(bf16[768]{0:T(1024)(128)(2,1)} %param.15) | copy-start | bytes 4612
  139.2 30.4 %all-to-all-start.3 = ((bf16[8,128,384]{2,1,0:T(8,128)(2,1)}), bf16[8,128,384]{2,1,0:T(8,128)(2,1)S(1)}, u32[]{:S(2)}, u32[]{:S(2)}) async-start(bf16[8,128,384]{2,1,0:T(8,128)(2,1)} %bitcast.17), calls=%async_computation.3 | async-start | bytes 1572864 | tf_op jit(solution)/shard_map/all_to_all | solution.py:234
  169.7 14.1 %collective-permute-start.10 = (bf16[64,384]{1,0:T(8,128)(2,1)S(1)}, bf16[64,384]{1,0:T(8,128)(2,1)S(1)}, u32[]{:S(2)}, u32[]{:S(2)}) collective-permute-start(bf16[64,384]{1,0:T(8,128)(2,1)S(1)} %get-tuple-element.34), channel_id=1, source_target_pairs={{0,0},{1,32},{2,64},{3,96},{4,128},{5,160},{6,192},{7,224},{8,256}... | collective-permute-start | bytes 147464 | tf_op jit(solution)/shard_map/ppermute | solution.py:244
  177.1 13.8 %collective-permute-start.9 = (bf16[64,384]{1,0:T(8,128)(2,1)S(1)}, bf16[64,384]{1,0:T(8,128)(2,1)S(1)}, u32[]{:S(2)}, u32[]{:S(2)}) collective-permute-start(bf16[64,384]{1,0:T(8,128)(2,1)S(1)} %get-tuple-element.33), channel_id=1, source_target_pairs={{0,48},{1,16},{2,112},{3,80},{4,176},{5,144},{6,240},{7,208},{8,30... | collective-permute-start | bytes 147464 | tf_op jit(solution)/shard_map/ppermute | solution.py:245

commit v11 on v10

--- a/solution.py
+++ b/solution.py
@@ -211,6 +211,8 @@
     part = (parts[3].astype(F32) + direct.astype(F32) + joined.astype(F32)).astype(BF16)
     part = lax.all_to_all(part, "y", split_axis=0, concat_axis=0, tiled=True)
     bias = up_bias.astype(F32).reshape(-1, BLOCK)
+    resid = lax.dynamic_slice_in_dim(hidden_in, t * width, width, 1).astype(F32)
+    base, bias = lax.optimization_barrier((resid + down_bias.astype(F32), bias))
     act = activate(where, ids, valid, part, bias)
 
     act = lax.all_to_all(act, "y", split_axis=0, concat_axis=0, tiled=True)
@@ -234,8 +236,6 @@
     pair = lax.all_to_all(pair, "z", split_axis=0, concat_axis=0, tiled=True)
     branch = jnp.sum(pair.astype(F32), axis=0).astype(BF16)
 
-    resid = lax.dynamic_slice_in_dim(hidden_in, t * width, width, 1).astype(F32)
-    base, branch = lax.optimization_barrier((resid + down_bias.astype(F32), branch))
     back = [[], []]
     for j, ys, xs, zs, cs in itertools.product(range(2), *map(range, (NY, NX, NZ, NC))):
         row = (zs + ys) % NY * NX + (xs - 2 * cs - j) % NX

time: 194 us -> 192 us (0.990)
  blocking collectives: 44.8 us -> 74.3 us
  waiting for transfers between devices: 61.1 us -> 39.7 us
  starting transfers between devices: 63.9 us -> 55.4 us
    all_to_all x0 -> x1, blocking collectives: none -> 29.6 us  [body(): pair = lax.all_to_all(pair, 'z', split_axis=0, concat_axis=0, tiled=True)]
    all_to_all x1 -> x0, waiting for transfers between devices: 20.4 us -> none  [body(): pair = lax.all_to_all(pair, 'z', split_axis=0, concat_axis=0, tiled=True)]
    all_to_all x1 -> x0, starting transfers between devices: 9.08 us -> none  [body(): pair = lax.all_to_all(pair, 'z', split_axis=0, concat_axis=0, tiled=True)]
  transfers between devices with their start and end apart: 13 -> 12, of which waited for: 8 -> 7; matrix products, arithmetic and copies ran while one was open for 1% -> 1% of each run, Pallas kernels for 7% -> 7%
where the time goes in v11:
time: 192 us; the launch traced here: 190 us
  blocking collectives  74.3 us (39%)
  starting transfers between devices  55.4 us (29%)
  waiting for transfers between devices  39.7 us (21%)
  Pallas kernels  15.7 us (8%)
  other arithmetic  3.43 us (2%)
    all_to_all x1, blocking collectives, body(): pair = lax.all_to_all(pair, 'z', split_axis=0, concat_axis=0, tiled=True)  29.6 us
    all_to_all x1, blocking collectives, body(): lax.all_to_all(normed, ('y', 'x'), split_axis=0, concat_axis=0, tiled=True)  29.1 us
    all_to_all x1, blocking collectives, body(): act = lax.all_to_all(act, 'y', split_axis=0, concat_axis=0, tiled=True)  15.7 us
    ppermute x1, starting transfers between devices, body(): other_side = lax.ppermute(act, ('x', 'c'), pairs(TURNS[2]))  9.86 us
    all_to_all x1, starting transfers between devices, body(): part = lax.all_to_all(part, 'y', split_axis=0, concat_axis=0, tiled=True)  9.26 us
    all_to_all x1, waiting for transfers between devices, body(): part = lax.all_to_all(part, 'y', split_axis=0, concat_axis=0, tiled=True)  8.93 us
    ppermute x1, waiting for transfers between devices, body(): joined = lax.ppermute(joined, ('x', 'c'), pairs(LEAVES[2]))  8.27 us
    ppermute x1, starting transfers between devices, body(): first = lax.ppermute(branch[:ROW], ALL, back[0])  7.88 us
  transfers between devices with their start and end apart: 12, of which 7 were waited for; matrix products, arithmetic and copies ran while one was open for 1% of the time, Pallas kernels for 7%

profile of v11, /device:TPU:176, one launch (start us, length us, event | category | flops | bytes accessed | tf_op | source)
XLA Modules:
  0.0 190.3 jit_solution(17885476436226693548)
XLA Ops:
  2.0 29.1 %all_to_all.20 = bf16[32,32,384]{2,1,0:T(8,128)(2,1)S(1)} all-to-all(bf16[32,32,384]{2,1,0:T(8,128)(2,1)S(1)} %norm.1), channel_id=1, replica_groups=mesh['y'=8,'x'=4,'z'=8,'c'=2] {'y','x'}, dimensions={0} | all-to-all | bytes 1572864 | tf_op jit(solution)/shard_map/all_to_all | solution.py:199
  31.1 1.9 %collective-permute-start = (bf16[32,32,384]{2,1,0:T(8,128)(2,1)S(1)}, bf16[32,32,384]{2,1,0:T(8,128)(2,1)S(1)}, u32[]{:S(2)}, u32[]{:S(2)}) collective-permute-start(bf16[32,32,384]{2,1,0:T(8,128)(2,1)S(1)} %all_to_all.20), channel_id=1, source_target_pairs={{0,1},{1,0},{2,3},{3,2},{4,5},{5,4},{6,7},{7,6},{8,9},{9,8},{10,11... | collective-permute-start | bytes 2359304 | tf_op jit(solution)/shard_map/ppermute | solution.py:200
  33.3 2.6 %up_first.1 = (bf16[8,2,32,512]{3,2,1,0:T(8,128)(2,1)S(1)}, bf16[8,2,32,512]{3,2,1,0:T(8,128)(2,1)S(1)}, bf16[8,2,32,512]{3,2,1,0:T(8,128)(2,1)S(1)}, bf16[8,2,32,512]{3,2,1,0:T(8,128)(2,1)S(1)}) custom-call(s32[3]{0:T(128)S(1)} %add_add_fusion.1.at, s32[256]{0:T(256)S(1)} %reshape.36.ids, bf16[8,4,32,384]{3,2,1,0:T(8,128)(2,1)S(1)} %bitcast.31, ...), custom_call_target="tpu_custom_call" | custom-call | flops 1207959552 | tf_op jit(solution)/shard_map/up_first/pallas_call | solution.py:91
  37.1 3.1 %collective-permute-start.2 = (bf16[8,64,512]{2,1,0:T(8,128)(2,1)S(1)}, bf16[8,64,512]{2,1,0:T(8,128)(2,1)S(1)}, u32[]{:S(2)}, u32[]{:S(2)}) collective-permute-start(bf16[8,64,512]{2,1,0:T(8,128)(2,1)S(1)} %bitcast.33), channel_id=1, source_target_pairs={{0,16},{1,49},{16,32},{17,1},{32,48},{33,17},{48,0},{49,33},{2,18}... | collective-permute-start | bytes 1572872 | tf_op jit(solution)/shard_map/ppermute | solution.py:207
  41.4 4.0 %collective-permute-start.1 = (bf16[8,64,512]{2,1,0:T(8,128)(2,1)S(1)}, bf16[8,64,512]{2,1,0:T(8,128)(2,1)S(1)}, u32[]{:S(2)}, u32[]{:S(2)}) collective-permute-start(bf16[8,64,512]{2,1,0:T(8,128)(2,1)S(1)} %bitcast.32), channel_id=1, source_target_pairs={{0,48},{1,17},{16,0},{17,33},{32,16},{33,49},{48,32},{49,1},{2,50}... | collective-permute-start | bytes 1572872 | tf_op jit(solution)/shard_map/ppermute | solution.py:208
  46.6 3.6 %collective-permute-done.2 = bf16[8,64,512]{2,1,0:T(8,128)(2,1)S(1)} collective-permute-done((bf16[8,64,512]{2,1,0:T(8,128)(2,1)S(1)}, bf16[8,64,512]{2,1,0:T(8,128)(2,1)S(1)}, u32[]{:S(2)}, u32[]{:S(2)}) %collective-permute-start.2) | collective-permute-done | bytes 524320 | tf_op jit(solution)/shard_map/ppermute | solution.py:207
  50.4 2.8 %collective-permute-start.3 = (bf16[8,64,512]{2,1,0:T(8,128)(2,1)S(1)}, bf16[8,64,512]{2,1,0:T(8,128)(2,1)S(1)}, u32[]{:S(2)}, u32[]{:S(2)}) collective-permute-start(bf16[8,64,512]{2,1,0:T(8,128)(2,1)S(1)} %fusion), channel_id=1, source_target_pairs={{0,16},{1,49},{16,32},{17,1},{32,48},{33,17},{48,0},{49,33},{2,18}... | collective-permute-start | bytes 1572872 | tf_op jit(solution)/shard_map/ppermute | solution.py:210
  54.4 8.3 %collective-permute-done.3 = bf16[8,64,512]{2,1,0:T(8,128)(2,1)S(1)} collective-permute-done((bf16[8,64,512]{2,1,0:T(8,128)(2,1)S(1)}, bf16[8,64,512]{2,1,0:T(8,128)(2,1)S(1)}, u32[]{:S(2)}, u32[]{:S(2)}) %collective-permute-start.3) | collective-permute-done | bytes 524320 | tf_op jit(solution)/shard_map/ppermute | solution.py:210
  63.7 9.3 %all-to-all-start.1 = ((bf16[8,64,512]{2,1,0:T(8,128)(2,1)}), bf16[8,64,512]{2,1,0:T(8,128)(2,1)S(1)}, u32[]{:S(2)}, u32[]{:S(2)}) async-start(bf16[8,64,512]{2,1,0:T(8,128)(2,1)} %fusion.2), calls=%async_computation.1 | async-start | bytes 1048576 | tf_op jit(solution)/shard_map/all_to_all | solution.py:212
  74.0 8.9 %all-to-all-done.1.parts = bf16[8,64,512]{2,1,0:T(8,128)(2,1)S(1)} async-done(((bf16[8,64,512]{2,1,0:T(8,128)(2,1)}), bf16[8,64,512]{2,1,0:T(8,128)(2,1)S(1)}, u32[]{:S(2)}, u32[]{:S(2)}) %all-to-all-start.1) | async-done | bytes 524320 | tf_op jit(solution)/shard_map/all_to_all | solution.py:212
  83.6 15.7 %all_to_all.21.act = bf16[8,64,512]{2,1,0:T(8,128)(2,1)S(1)} all-to-all(bf16[8,64,512]{2,1,0:T(8,128)(2,1)S(1)} %act.1), channel_id=1, replica_groups=mesh['y'=8,'x'=4,'z'=8,'c'=2] {'y'}, dimensions={0} | all-to-all | bytes 1048576 | tf_op jit(solution)/shard_map/all_to_all | solution.py:218
  99.3 2.0 %collective-permute-start.4 = (bf16[8,64,512]{2,1,0:T(8,128)(2,1)S(1)}, bf16[8,64,512]{2,1,0:T(8,128)(2,1)S(1)}, u32[]{:S(2)}, u32[]{:S(2)}) collective-permute-start(bf16[8,64,512]{2,1,0:T(8,128)(2,1)S(1)} %all_to_all.21.act), channel_id=1, source_target_pairs={{0,16},{1,49},{16,32},{17,1},{32,48},{33,17},{48,0},{49,33},{2,18}... | collective-permute-start | bytes 1572872 | tf_op jit(solution)/shard_map/ppermute | solution.py:219
  101.3 9.9 %collective-permute-start.7 = (bf16[8,64,512]{2,1,0:T(8,128)(2,1)S(1)}, bf16[8,64,512]{2,1,0:T(8,128)(2,1)S(1)}, u32[]{:S(2)}, u32[]{:S(2)}) collective-permute-start(bf16[8,64,512]{2,1,0:T(8,128)(2,1)S(1)} %all_to_all.21.act), channel_id=1, source_target_pairs={{0,48},{1,17},{16,0},{17,33},{32,16},{33,49},{48,32},{49,1},{2,50}... | collective-permute-start | bytes 1572872 | tf_op jit(solution)/shard_map/ppermute | solution.py:220
  111.2 1.8 down.4
  113.0 5.4 %collective-permute-done.4.act = bf16[8,64,512]{2,1,0:T(8,128)(2,1)S(1)} collective-permute-done((bf16[8,64,512]{2,1,0:T(8,128)(2,1)S(1)}, bf16[8,64,512]{2,1,0:T(8,128)(2,1)S(1)}, u32[]{:S(2)}, u32[]{:S(2)}) %collective-permute-start.4) | collective-permute-done | bytes 524320 | tf_op jit(solution)/shard_map/ppermute | solution.py:219
  118.3 1.9 %collective-permute-start.5 = (bf16[8,64,512]{2,1,0:T(8,128)(2,1)S(1)}, bf16[8,64,512]{2,1,0:T(8,128)(2,1)S(1)}, u32[]{:S(2)}, u32[]{:S(2)}) collective-permute-start(bf16[8,64,512]{2,1,0:T(8,128)(2,1)S(1)} %collective-permute-done.4.act), channel_id=1, source_target_pairs={{0,16},{1,49},{16,32},{17,1},{32,48},{33,17},{48,0},{49,33},{2,18}... | collective-permute-start | bytes 1572872 | tf_op jit(solution)/shard_map/ppermute | solution.py:223
  122.0 4.1 %collective-permute-start.8 = (bf16[8,64,384]{2,1,0:T(8,128)(2,1)S(1)}, bf16[8,64,384]{2,1,0:T(8,128)(2,1)S(1)}, u32[]{:S(2)}, u32[]{:S(2)}) collective-permute-start(bf16[8,64,384]{2,1,0:T(8,128)(2,1)S(1)} %down.7), channel_id=1, source_target_pairs={{0,1},{1,0},{2,3},{3,2},{4,5},{5,4},{6,7},{7,6},{8,9},{9,8},{10,11... | collective-permute-start | bytes 1179656 | tf_op jit(solution)/shard_map/ppermute | solution.py:226
  126.2 6.3 %collective-permute-done.5.act = bf16[8,64,512]{2,1,0:T(8,128)(2,1)S(1)} collective-permute-done((bf16[8,64,512]{2,1,0:T(8,128)(2,1)S(1)}, bf16[8,64,512]{2,1,0:T(8,128)(2,1)S(1)}, u32[]{:S(2)}, u32[]{:S(2)}) %collective-permute-start.5) | collective-permute-done | bytes 524320 | tf_op jit(solution)/shard_map/ppermute | solution.py:223
  132.4 1.8 down.5
  134.2 1.9 %collective-permute-start.6 = (bf16[8,64,384]{2,1,0:T(8,128)(2,1)S(1)}, bf16[8,64,384]{2,1,0:T(8,128)(2,1)S(1)}, u32[]{:S(2)}, u32[]{:S(2)}) collective-permute-start(bf16[8,64,384]{2,1,0:T(8,128)(2,1)S(1)} %get-tuple-element.30), channel_id=1, source_target_pairs={{0,1},{1,0},{2,3},{3,2},{4,5},{5,4},{6,7},{7,6},{8,9},{9,8},{10,11... | collective-permute-start | bytes 1179656 | tf_op jit(solution)/shard_map/ppermute | solution.py:228
  138.3 29.6 %all_to_all.22 = bf16[8,128,384]{2,1,0:T(8,128)(2,1)S(1)} all-to-all(bf16[8,128,384]{2,1,0:T(8,128)(2,1)S(1)} %bitcast.35), channel_id=1, replica_groups=mesh['y'=8,'x'=4,'z'=8,'c'=2] {'z'}, dimensions={0} | all-to-all | bytes 1572864 | tf_op jit(solution)/shard_map/all_to_all | solution.py:236
  168.0 7.9 %collective-permute-start.10 = (bf16[64,384]{1,0:T(8,128)(2,1)S(1)}, bf16[64,384]{1,0:T(8,128)(2,1)S(1)}, u32[]{:S(2)}, u32[]{:S(2)}) collective-permute-start(bf16[64,384]{1,0:T(8,128)(2,1)S(1)} %get-tuple-element.34), channel_id=1, source_target_pairs={{0,0},{1,32},{2,64},{3,96},{4,128},{5,160},{6,192},{7,224},{8,256}... | collective-permute-start | bytes 147464 | tf_op jit(solution)/shard_map/ppermute | solution.py:244
  175.9 6.7 %collective-permute-start.9 = (bf16[64,384]{1,0:T(8,128)(2,1)S(1)}, bf16[64,384]{1,0:T(8,128)(2,1)S(1)}, u32[]{:S(2)}, u32[]{:S(2)}) collective-permute-start(bf16[64,384]{1,0:T(8,128)(2,1)S(1)} %get-tuple-element.33), channel_id=1, source_target_pairs={{0,48},{1,16},{2,112},{3,80},{4,176},{5,144},{6,240},{7,208},{8,30... | collective-permute-start | bytes 147464 | tf_op jit(solution)/shard_map/ppermute | solution.py:245
  182.6 7.1 %collective-permute-done.9 = bf16[64,384]{1,0:T(8,128)(2,1)S(1)} collective-permute-done((bf16[64,384]{1,0:T(8,128)(2,1)S(1)}, bf16[64,384]{1,0:T(8,128)(2,1)S(1)}, u32[]{:S(2)}, u32[]{:S(2)}) %collective-permute-start.9) | collective-permute-done | bytes 49184 | tf_op jit(solution)/shard_map/ppermute | solution.py:245
  (49 shorter events, 14.5 us)
Async XLA Ops:
  0.0 1.2 copy-start.4
  0.0 1.2 copy-start.3
  1.2 31.8 %copy-start.7 = (s32[64,1,4]{0,2,1:T(4,128)S(1)}, s32[64,1,4]{0,2,1:T(4,128)}, u32[]{:S(2)}) copy-start(s32[64,1,4]{0,2,1:T(4,128)} %param.16) | copy-start | bytes 3076
  1.2 32.0 %copy-start = (bf16[384,1536]{1,0:T(8,128)(2,1)S(1)}, bf16[384,1536]{1,0:T(8,128)(2,1)}, u32[]{:S(2)}) copy-start(bf16[384,1536]{1,0:T(8,128)(2,1)} %weight.13) | copy-start | bytes 3538948
  31.1 4.8 %collective-permute-start = (bf16[32,32,384]{2,1,0:T(8,128)(2,1)S(1)}, bf16[32,32,384]{2,1,0:T(8,128)(2,1)S(1)}, u32[]{:S(2)}, u32[]{:S(2)}) collective-permute-start(bf16[32,32,384]{2,1,0:T(8,128)(2,1)S(1)} %all_to_all.20), channel_id=1, source_target_pairs={{0,1},{1,0},{2,3},{3,2},{4,5},{5,4},{6,7},{7,6},{8,9},{9,8},{10,11... | collective-permute-start | bytes 2359304 | tf_op jit(solution)/shard_map/ppermute | solution.py:200
  37.1 13.1 %collective-permute-start.2 = (bf16[8,64,512]{2,1,0:T(8,128)(2,1)S(1)}, bf16[8,64,512]{2,1,0:T(8,128)(2,1)S(1)}, u32[]{:S(2)}, u32[]{:S(2)}) collective-permute-start(bf16[8,64,512]{2,1,0:T(8,128)(2,1)S(1)} %bitcast.33), channel_id=1, source_target_pairs={{0,16},{1,49},{16,32},{17,1},{32,48},{33,17},{48,0},{49,33},{2,18}... | collective-permute-start | bytes 1572872 | tf_op jit(solution)/shard_map/ppermute | solution.py:207
  41.4 13.0 %collective-permute-start.1 = (bf16[8,64,512]{2,1,0:T(8,128)(2,1)S(1)}, bf16[8,64,512]{2,1,0:T(8,128)(2,1)S(1)}, u32[]{:S(2)}, u32[]{:S(2)}) collective-permute-start(bf16[8,64,512]{2,1,0:T(8,128)(2,1)S(1)} %bitcast.32), channel_id=1, source_target_pairs={{0,48},{1,17},{16,0},{17,33},{32,16},{33,49},{48,32},{49,1},{2,50}... | collective-permute-start | bytes 1572872 | tf_op jit(solution)/shard_map/ppermute | solution.py:208
  50.4 12.3 %collective-permute-start.3 = (bf16[8,64,512]{2,1,0:T(8,128)(2,1)S(1)}, bf16[8,64,512]{2,1,0:T(8,128)(2,1)S(1)}, u32[]{:S(2)}, u32[]{:S(2)}) collective-permute-start(bf16[8,64,512]{2,1,0:T(8,128)(2,1)S(1)} %fusion), channel_id=1, source_target_pairs={{0,16},{1,49},{16,32},{17,1},{32,48},{33,17},{48,0},{49,33},{2,18}... | collective-permute-start | bytes 1572872 | tf_op jit(solution)/shard_map/ppermute | solution.py:210
  54.4 18.6 %copy-start.6 = (bf16[768]{0:T(1024)(128)(2,1)S(1)}, bf16[768]{0:T(1024)(128)(2,1)}, u32[]{:S(2)}) copy-start(bf16[768]{0:T(1024)(128)(2,1)} %param.15) | copy-start | bytes 4612
  54.4 18.6 %copy-start.5 = (bf16[1536]{0:T(1024)(128)(2,1)S(1)}, bf16[1536]{0:T(1024)(128)(2,1)}, u32[]{:S(2)}) copy-start(bf16[1536]{0:T(1024)(128)(2,1)} %param.13) | copy-start | bytes 9220
  54.4 28.5 %copy-start.2 = (s32[64,1]{0,1:T(1,128)S(1)}, s32[64,1]{0,1:T(1,128)}, u32[]{:S(2)}) copy-start(s32[64,1]{0,1:T(1,128)} %param.17) | copy-start | bytes 772
  63.7 47.5 %copy-start.1 = (bf16[1536,384]{1,0:T(8,128)(2,1)S(1)}, bf16[1536,384]{1,0:T(8,128)(2,1)}, u32[]{:S(2)}) copy-start(bf16[1536,384]{1,0:T(8,128)(2,1)} %weight.17) | copy-start | bytes 3538948
  63.7 19.2 %all-to-all-start.1 = ((bf16[8,64,512]{2,1,0:T(8,128)(2,1)}), bf16[8,64,512]{2,1,0:T(8,128)(2,1)S(1)}, u32[]{:S(2)}, u32[]{:S(2)}) async-start(bf16[8,64,512]{2,1,0:T(8,128)(2,1)} %fusion.2), calls=%async_computation.1 | async-start | bytes 1048576 | tf_op jit(solution)/shard_map/all_to_all | solution.py:212
  99.3 19.0 %collective-permute-start.4 = (bf16[8,64,512]{2,1,0:T(8,128)(2,1)S(1)}, bf16[8,64,512]{2,1,0:T(8,128)(2,1)S(1)}, u32[]{:S(2)}, u32[]{:S(2)}) collective-permute-start(bf16[8,64,512]{2,1,0:T(8,128)(2,1)S(1)} %all_to_all.21.act), channel_id=1, source_target_pairs={{0,16},{1,49},{16,32},{17,1},{32,48},{33,17},{48,0},{49,33},{2,18}... | collective-permute-start | bytes 1572872 | tf_op jit(solution)/shard_map/ppermute | solution.py:219
  101.3 19.0 %collective-permute-start.7 = (bf16[8,64,512]{2,1,0:T(8,128)(2,1)S(1)}, bf16[8,64,512]{2,1,0:T(8,128)(2,1)S(1)}, u32[]{:S(2)}, u32[]{:S(2)}) collective-permute-start(bf16[8,64,512]{2,1,0:T(8,128)(2,1)S(1)} %all_to_all.21.act), channel_id=1, source_target_pairs={{0,48},{1,17},{16,0},{17,33},{32,16},{33,49},{48,32},{49,1},{2,50}... | collective-permute-start | bytes 1572872 | tf_op jit(solution)/shard_map/ppermute | solution.py:220
  118.3 14.1 %collective-permute-start.5 = (bf16[8,64,512]{2,1,0:T(8,128)(2,1)S(1)}, bf16[8,64,512]{2,1,0:T(8,128)(2,1)S(1)}, u32[]{:S(2)}, u32[]{:S(2)}) collective-permute-start(bf16[8,64,512]{2,1,0:T(8,128)(2,1)S(1)} %collective-permute-done.4.act), channel_id=1, source_target_pairs={{0,16},{1,49},{16,32},{17,1},{32,48},{33,17},{48,0},{49,33},{2,18}... | collective-permute-start | bytes 1572872 | tf_op jit(solution)/shard_map/ppermute | solution.py:223
  122.0 15.8 %collective-permute-start.8 = (bf16[8,64,384]{2,1,0:T(8,128)(2,1)S(1)}, bf16[8,64,384]{2,1,0:T(8,128)(2,1)S(1)}, u32[]{:S(2)}, u32[]{:S(2)}) collective-permute-start(bf16[8,64,384]{2,1,0:T(8,128)(2,1)S(1)} %down.7), channel_id=1, source_target_pairs={{0,1},{1,0},{2,3},{3,2},{4,5},{5,4},{6,7},{7,6},{8,9},{9,8},{10,11... | collective-permute-start | bytes 1179656 | tf_op jit(solution)/shard_map/ppermute | solution.py:226
  134.2 3.8 %collective-permute-start.6 = (bf16[8,64,384]{2,1,0:T(8,128)(2,1)S(1)}, bf16[8,64,384]{2,1,0:T(8,128)(2,1)S(1)}, u32[]{:S(2)}, u32[]{:S(2)}) collective-permute-start(bf16[8,64,384]{2,1,0:T(8,128)(2,1)S(1)} %get-tuple-element.30), channel_id=1, source_target_pairs={{0,1},{1,0},{2,3},{3,2},{4,5},{5,4},{6,7},{7,6},{8,9},{9,8},{10,11... | collective-permute-start | bytes 1179656 | tf_op jit(solution)/shard_map/ppermute | solution.py:228
  168.0 14.6 %collective-permute-start.10 = (bf16[64,384]{1,0:T(8,128)(2,1)S(1)}, bf16[64,384]{1,0:T(8,128)(2,1)S(1)}, u32[]{:S(2)}, u32[]{:S(2)}) collective-permute-start(bf16[64,384]{1,0:T(8,128)(2,1)S(1)} %get-tuple-element.34), channel_id=1, source_target_pairs={{0,0},{1,32},{2,64},{3,96},{4,128},{5,160},{6,192},{7,224},{8,256}... | collective-permute-start | bytes 147464 | tf_op jit(solution)/shard_map/ppermute | solution.py:244
  175.9 13.8 %collective-permute-start.9 = (bf16[64,384]{1,0:T(8,128)(2,1)S(1)}, bf16[64,384]{1,0:T(8,128)(2,1)S(1)}, u32[]{:S(2)}, u32[]{:S(2)}) collective-permute-start(bf16[64,384]{1,0:T(8,128)(2,1)S(1)} %get-tuple-element.33), channel_id=1, source_target_pairs={{0,48},{1,16},{2,112},{3,80},{4,176},{5,144},{6,240},{7,208},{8,30... | collective-permute-start | bytes 147464 | tf_op jit(solution)/shard_map/ppermute | solution.py:245
